TPU v7x, 256 devices: a whole 4x4x8 slice. The times are simulated.
256 devices in a mesh: dp: 32 (over x_lo, z, core), tensor: 8 (over y, x_hi).
Axes of the slice: x: 4 (x_hi: 2, x_lo: 2; x = x_hi * 2 + x_lo), y: 4, z: 8, core: 2. Of those that a mesh axis runs over, the one named last changes fastest.
Arguments:
- images: bfloat16 [4096, 1152], P('dp'), may hold values from -6 to 6
- gain: float32 [1152], replicated, may hold values from 0.1 to 1.9
- w_in: bfloat16 [1152, 4304], P(None, 'tensor'), may hold values from -0.1875 to 0.1875
- b_in: float32 [4304], P('tensor'), may hold values from -4 to 4
- w_out: bfloat16 [4304, 1152], P('tensor'), may hold values from -0.09375 to 0.09375
- texts: bfloat16 [4096, 1152], P(('dp', 'tensor')), may hold values from -6 to 6
- log_scale: float32 [1], replicated, may hold values from 1.6 to 3
- bias: float32 [1], replicated, may hold values from -3 to -0.5
Outputs:
- image_loss_gradient: float32 [4096, 1152], P('dp')
- text_grad: float32 [4096, 1152], P(('dp', 'tensor'))
- in_grad: float32 [1152, 4304], P('dp', 'tensor')
- out_grad_t: float32 [1152, 4304], P('dp', 'tensor')
All inputs are finite; a program needn't handle non-finite values.
Results may differ from a plain program's by a relative error of at most 0.019.
Values may be sent and summed in bfloat16 or wider, within the bound.
No kernel may reach another device: no remote copies, remote signals or barrier semaphores. Data moves between devices by JAX's collectives and lax.ppermute only.
A program may use at most 64 MiB of HBM per device.

v0:
```python
import jax
import jax.numpy as jnp
from jax import lax
from jax.sharding import PartitionSpec as P


def gelu_tanh(value):
    return jax.nn.gelu(value, approximate=True)


def local(images, gain, w_in, b_in, w_out, texts, log_scale, bias):
    rank_d = lax.axis_index("dp")
    rank_t = lax.axis_index("tensor")
    img_rows = images.shape[0]
    txt_rows = texts.shape[0]
    xf = images.astype(jnp.float32)
    feature_average = jnp.mean(xf, axis=-1, keepdims=True)
    centered_input = xf - feature_average
    standard_deviation = jnp.sqrt(
        jnp.mean(centered_input * centered_input, axis=-1, keepdims=True) + 1e-06
    )
    standardized_input = centered_input / standard_deviation
    normalized_rows = (standardized_input * gain).astype(jnp.bfloat16)
    pre = jnp.dot(normalized_rows, w_in, preferred_element_type=jnp.float32) + b_in
    hidden = gelu_tanh(pre).astype(jnp.bfloat16)
    partial_out = jnp.dot(hidden, w_out, preferred_element_type=jnp.float32)
    embed = xf + lax.psum(partial_out, "tensor")
    enorm = jnp.sqrt(jnp.sum(embed * embed, axis=-1, keepdims=True) + 1e-06)
    unit = embed / enorm
    unit_b = unit.astype(jnp.bfloat16)
    tf = texts.astype(jnp.float32)
    tnorm = jnp.sqrt(jnp.sum(tf * tf, axis=-1, keepdims=True) + 1e-06)
    tunit = tf / tnorm
    tunit_b = tunit.astype(jnp.bfloat16)
    scale = jnp.exp(log_scale[0])
    shift = bias[0]
    local_rows = jnp.arange(img_rows, dtype=jnp.int32)
    target = rank_d * txt_rows + local_rows - rank_t * txt_rows
    owned = (local_rows >= rank_t * txt_rows) & (local_rows < (rank_t + 1) * txt_rows)
    piece = lax.all_gather(tunit_b, "dp", axis=0, tiled=True)
    logits = (
        scale
        * lax.dot_general(
            unit_b, piece, (((1,), (1,)), ((), ())), preferred_element_type=jnp.float32
        )
        + shift
    )
    places = jnp.arange(piece.shape[0], dtype=jnp.int32)
    labels = (owned[:, None] & (places[None, :] == target[:, None])).astype(jnp.float32)
    coef = (jax.nn.sigmoid(logits) - labels).astype(jnp.bfloat16)
    du_acc = scale * jnp.dot(coef, piece, preferred_element_type=jnp.float32)
    dw = lax.psum_scatter(
        (
            scale
            * lax.dot_general(
                coef, unit_b, (((0,), (0,)), ((), ())), preferred_element_type=jnp.float32
            )
        ).astype(jnp.bfloat16),
        "dp",
        scatter_dimension=0,
        tiled=True,
    ).astype(jnp.float32)
    du = lax.psum(du_acc.astype(jnp.bfloat16), "tensor").astype(jnp.float32)
    text_grad = (dw - tunit * jnp.sum(tunit * dw, axis=-1, keepdims=True)) / tnorm
    embedding_gradient = ((du - unit * jnp.sum(unit * du, axis=-1, keepdims=True)) / enorm).astype(
        jnp.bfloat16
    )
    dhid = lax.dot_general(
        embedding_gradient, w_out, (((1,), (1,)), ((), ())), preferred_element_type=jnp.float32
    )
    unused_value, pull = jax.vjp(gelu_tanh, pre)
    dpre = pull(dhid)[0].astype(jnp.bfloat16)
    dn_part = lax.dot_general(
        dpre, w_in, (((1,), (1,)), ((), ())), preferred_element_type=jnp.float32
    )
    dn = lax.psum(dn_part.astype(jnp.bfloat16), "tensor").astype(jnp.float32)
    unit_input_gradient = dn * gain
    image_loss_gradient = (
        embedding_gradient.astype(jnp.float32)
        + (
            unit_input_gradient
            - jnp.mean(unit_input_gradient, axis=-1, keepdims=True)
            - standardized_input
            * jnp.mean(unit_input_gradient * standardized_input, axis=-1, keepdims=True)
        )
        / standard_deviation
    )
    in_grad = lax.psum_scatter(
        lax.dot_general(
            normalized_rows, dpre, (((0,), (0,)), ((), ())), preferred_element_type=jnp.float32
        ).astype(jnp.bfloat16),
        "dp",
        scatter_dimension=0,
        tiled=True,
    ).astype(jnp.float32)
    out_grad_t = lax.psum_scatter(
        lax.dot_general(
            embedding_gradient, hidden, (((0,), (0,)), ((), ())), preferred_element_type=jnp.float32
        ).astype(jnp.bfloat16),
        "dp",
        scatter_dimension=0,
        tiled=True,
    ).astype(jnp.float32)
    return (image_loss_gradient, text_grad, in_grad, out_grad_t)


def solution(mesh):
    return jax.shard_map(
        local,
        mesh=mesh,
        in_specs=(
            P("dp", None),
            P(),
            P(None, "tensor"),
            P("tensor"),
            P("tensor", None),
            P(("dp", "tensor"), None),
            P(),
            P(),
        ),
        out_specs=(P("dp", None), P(("dp", "tensor"), None), P("dp", "tensor"), P("dp", "tensor")),
        check_vma=False,
    )
```

profile of v0, /device:TPU:1, one launch (start us, length us, event | category | flops | bytes accessed | tf_op | source)
XLA Modules:
  0.0 356.4 jit_solution(14264018659109873483)
XLA Ops:
  10.4 2.0 convolution_add_fusion
  12.5 1.3 fusion.33
  16.2 88.5 %all-reduce.9.cloned.1.call-done = f32[128,1152]{1,0:T(8,128)} async-done(((f32[128,1152]{1,0:T(8,128)}), f32[128,1152]{1,0:T(8,128)}) %all-reduce.9.cloned.1.call-update) | async-done | bytes 589840 | tf_op jit(solution)/shard_map/psum | solution.py:27
  105.9 2.1 fusion.10
  109.2 87.5 %all-reduce.11.cloned.1.call-done = bf16[128,1152]{1,0:T(8,128)(2,1)} async-done(((bf16[128,1152]{1,0:T(8,128)(2,1)}), bf16[128,1152]{1,0:T(8,128)(2,1)}) %all-reduce.11.cloned.1.call-update) | async-done | bytes 294928 | tf_op jit(solution)/shard_map/psum | solution.py:63
  200.8 1.6 fusion.2
  202.4 1.6 convolution_convert_fusion
  203.9 1.8 convolution_convert_fusion.1
  205.8 71.5 %fusion.38 = (bf16[48,538]{1,0:T(8,128)(2,1)S(1)}, bf16[48,538]{1,0:T(8,128)(2,1)S(1)}) fusion(bf16[1152,538]{1,0:T(8,128)(2,1)} %convolution_convert_fusion.1, bf16[1152,538]{1,0:T(8,128)(2,1)S(1)} %convolution_convert_fusion), kind=kCustom, calls=%all-reduce-scatter.2 | all-reduce-scatter fusion | flops 1652737 | bytes 2583424
  278.6 11.5 %collective-permute-start.6 = (bf16[48,538]{1,0:T(8,128)(2,1)S(1)}, bf16[48,538]{1,0:T(8,128)(2,1)S(1)}, u32[]{:S(2)}, u32[]{:S(2)}) collective-permute-start(bf16[48,538]{1,0:T(8,128)(2,1)S(1)} %get-tuple-element.8), channel_id=1, source_target_pairs={{0,56},{8,64},{16,72},{24,80},{32,88},{40,96},{48,104},{56,112},{6... | collective-permute-start | bytes 154952
  292.7 4.5 %collective-permute-start.3 = (bf16[48,538]{1,0:T(8,128)(2,1)S(1)}, bf16[48,538]{1,0:T(8,128)(2,1)S(1)}, u32[]{:S(2)}, u32[]{:S(2)}) collective-permute-start(bf16[48,538]{1,0:T(8,128)(2,1)S(1)} %get-tuple-element.8), channel_id=1, source_target_pairs={{0,32},{8,40},{16,48},{24,56},{32,64},{40,72},{48,80},{56,88},{64,... | collective-permute-start | bytes 154952
  299.7 7.6 %collective-permute-start.2 = (bf16[48,538]{1,0:T(8,128)(2,1)S(1)}, bf16[48,538]{1,0:T(8,128)(2,1)S(1)}, u32[]{:S(2)}, u32[]{:S(2)}) collective-permute-start(bf16[48,538]{1,0:T(8,128)(2,1)S(1)} %get-tuple-element.8), channel_id=1, source_target_pairs={{0,24},{8,32},{16,40},{24,48},{32,56},{40,64},{48,72},{56,80},{64,... | collective-permute-start | bytes 154952
  308.6 3.1 collective-permute-start
  311.7 8.0 %collective-permute-start.14 = (bf16[48,538]{1,0:T(8,128)(2,1)S(1)}, bf16[48,538]{1,0:T(8,128)(2,1)S(1)}, u32[]{:S(2)}, u32[]{:S(2)}) collective-permute-start(bf16[48,538]{1,0:T(8,128)(2,1)S(1)} %get-tuple-element.9), channel_id=1, source_target_pairs={{0,56},{8,64},{16,72},{24,80},{32,88},{40,96},{48,104},{56,112},{6... | collective-permute-start | bytes 154952
  319.7 4.7 %collective-permute-start.13 = (bf16[48,538]{1,0:T(8,128)(2,1)S(1)}, bf16[48,538]{1,0:T(8,128)(2,1)S(1)}, u32[]{:S(2)}, u32[]{:S(2)}) collective-permute-start(bf16[48,538]{1,0:T(8,128)(2,1)S(1)} %get-tuple-element.9), channel_id=1, source_target_pairs={{0,48},{8,56},{16,64},{24,72},{32,80},{40,88},{48,96},{56,104},{64... | collective-permute-start | bytes 154952
  324.4 2.1 collective-permute-start.12
  326.5 2.2 collective-permute-start.11
  328.8 2.3 collective-permute-start.10
  331.1 2.1 collective-permute-start.9
  333.2 2.2 collective-permute-start.8
  337.4 2.0 concatenate
  339.5 2.8 concatenate.1
  344.8 2.1 divide_add_fusion
  347.8 1.5 fusion.31
  (82 shorter events, 22.3 us)
Async XLA Ops:
  8.0 96.6 %all-reduce.9.cloned.1.call-start = ((), (), s32[]{:S(2)}) async-start(), calls=%async_computation.1 | async-start | bytes 1179648 | tf_op jit(solution)/shard_map/psum | solution.py:27
  10.4 193.5 %copy-start.10 = (f32[128]{0:T(128)}, f32[128]{0:T(128)S(1)}, u32[]{:S(2)}) copy-start(f32[128]{0:T(128)S(1)} %add_sqrt_fusion.2) | copy-start | bytes 1540
  12.5 185.8 %copy-start.6 = (f32[128,538]{0,1:T(8,128)}, f32[128,538]{0,1:T(8,128)S(1)}, u32[]{:S(2)}) copy-start(f32[128,538]{0,1:T(8,128)S(1)} %convolution_add_fusion) | copy-start | bytes 826372
  12.5 92.2 %copy-start.1 = (bf16[128,1152]{1,0:T(8,128)(2,1)S(1)}, bf16[128,1152]{1,0:T(8,128)(2,1)}, u32[]{:S(2)}) copy-start(bf16[128,1152]{1,0:T(8,128)(2,1)} %param.8) | copy-start | bytes 884740
  13.8 92.1 %all-gather.2.cloned.1.call-start = ((), (), s32[]{:S(2)}) async-start(), calls=%async_computation.2 | async-start | bytes 1216512 | tf_op jit(solution)/shard_map/all_gather | solution.py:40
  14.7 182.0 %all-reduce.11.cloned.1.call-start = ((), (), s32[]{:S(2)}) async-start(), calls=%async_computation.3 | async-start | bytes 589824 | tf_op jit(solution)/shard_map/psum | solution.py:63
  109.2 234.4 %all-reduce.13.cloned.1.call-start = ((), (), s32[]{:S(2)}) async-start(), calls=%async_computation.4 | async-start | bytes 589824 | tf_op jit(solution)/shard_map/psum | solution.py:76
  200.7 146.2 %reduce-scatter.6.cloned.1.call-start = ((), (), s32[]{:S(2)}) async-start(), calls=%async_computation.5 | async-start | bytes 1216512 | tf_op jit(solution)/shard_map/reduce_scatter | solution.py:52
  277.3 19.9 %collective-permute-start.15 = (bf16[36,538]{1,0:T(8,128)(2,1)S(1)}, bf16[36,538]{1,0:T(8,128)(2,1)S(1)}, u32[]{:S(2)}, u32[]{:S(2)}) collective-permute-start(bf16[36,538]{1,0:T(8,128)(2,1)S(1)} %slice.1), channel_id=1, source_target_pairs={{0,64},{8,72},{16,80},{24,88},{32,96},{40,104},{48,112},{56,120},{... | collective-permute-start | bytes 116216
  278.6 28.7 %collective-permute-start.6 = (bf16[48,538]{1,0:T(8,128)(2,1)S(1)}, bf16[48,538]{1,0:T(8,128)(2,1)S(1)}, u32[]{:S(2)}, u32[]{:S(2)}) collective-permute-start(bf16[48,538]{1,0:T(8,128)(2,1)S(1)} %get-tuple-element.8), channel_id=1, source_target_pairs={{0,56},{8,64},{16,72},{24,80},{32,88},{40,96},{48,104},{56,112},{6... | collective-permute-start | bytes 154952
  290.1 18.5 %collective-permute-start.5 = (bf16[48,538]{1,0:T(8,128)(2,1)S(1)}, bf16[48,538]{1,0:T(8,128)(2,1)S(1)}, u32[]{:S(2)}, u32[]{:S(2)}) collective-permute-start(bf16[48,538]{1,0:T(8,128)(2,1)S(1)} %get-tuple-element.8), channel_id=1, source_target_pairs={{0,48},{8,56},{16,64},{24,72},{32,80},{40,88},{48,96},{56,104},{64... | collective-permute-start | bytes 154952
  291.4 20.3 %collective-permute-start.4 = (bf16[48,538]{1,0:T(8,128)(2,1)S(1)}, bf16[48,538]{1,0:T(8,128)(2,1)S(1)}, u32[]{:S(2)}, u32[]{:S(2)}) collective-permute-start(bf16[48,538]{1,0:T(8,128)(2,1)S(1)} %get-tuple-element.8), channel_id=1, source_target_pairs={{0,40},{8,48},{16,56},{24,64},{32,72},{40,80},{48,88},{56,96},{64,... | collective-permute-start | bytes 154952
  292.7 27.1 %collective-permute-start.3 = (bf16[48,538]{1,0:T(8,128)(2,1)S(1)}, bf16[48,538]{1,0:T(8,128)(2,1)S(1)}, u32[]{:S(2)}, u32[]{:S(2)}) collective-permute-start(bf16[48,538]{1,0:T(8,128)(2,1)S(1)} %get-tuple-element.8), channel_id=1, source_target_pairs={{0,32},{8,40},{16,48},{24,56},{32,64},{40,72},{48,80},{56,88},{64,... | collective-permute-start | bytes 154952
  297.2 2.5 collective-permute-start.7
  299.7 24.7 %collective-permute-start.2 = (bf16[48,538]{1,0:T(8,128)(2,1)S(1)}, bf16[48,538]{1,0:T(8,128)(2,1)S(1)}, u32[]{:S(2)}, u32[]{:S(2)}) collective-permute-start(bf16[48,538]{1,0:T(8,128)(2,1)S(1)} %get-tuple-element.8), channel_id=1, source_target_pairs={{0,24},{8,32},{16,40},{24,48},{32,56},{40,64},{48,72},{56,80},{64,... | collective-permute-start | bytes 154952
  307.3 19.3 %collective-permute-start.1 = (bf16[48,538]{1,0:T(8,128)(2,1)S(1)}, bf16[48,538]{1,0:T(8,128)(2,1)S(1)}, u32[]{:S(2)}, u32[]{:S(2)}) collective-permute-start(bf16[48,538]{1,0:T(8,128)(2,1)S(1)} %get-tuple-element.8), channel_id=1, source_target_pairs={{0,16},{8,24},{16,32},{24,40},{32,48},{40,56},{48,64},{56,72},{64,... | collective-permute-start | bytes 154952
  308.6 20.2 %collective-permute-start = (bf16[48,538]{1,0:T(8,128)(2,1)S(1)}, bf16[48,538]{1,0:T(8,128)(2,1)S(1)}, u32[]{:S(2)}, u32[]{:S(2)}) collective-permute-start(bf16[48,538]{1,0:T(8,128)(2,1)S(1)} %get-tuple-element.8), channel_id=1, source_target_pairs={{0,8},{8,16},{16,24},{24,32},{32,40},{40,48},{48,56},{56,64},{64,7... | collective-permute-start | bytes 154952
  311.7 19.4 %collective-permute-start.14 = (bf16[48,538]{1,0:T(8,128)(2,1)S(1)}, bf16[48,538]{1,0:T(8,128)(2,1)S(1)}, u32[]{:S(2)}, u32[]{:S(2)}) collective-permute-start(bf16[48,538]{1,0:T(8,128)(2,1)S(1)} %get-tuple-element.9), channel_id=1, source_target_pairs={{0,56},{8,64},{16,72},{24,80},{32,88},{40,96},{48,104},{56,112},{6... | collective-permute-start | bytes 154952
  319.7 13.5 %collective-permute-start.13 = (bf16[48,538]{1,0:T(8,128)(2,1)S(1)}, bf16[48,538]{1,0:T(8,128)(2,1)S(1)}, u32[]{:S(2)}, u32[]{:S(2)}) collective-permute-start(bf16[48,538]{1,0:T(8,128)(2,1)S(1)} %get-tuple-element.9), channel_id=1, source_target_pairs={{0,48},{8,56},{16,64},{24,72},{32,80},{40,88},{48,96},{56,104},{64... | collective-permute-start | bytes 154952
  324.4 15.0 %collective-permute-start.12 = (bf16[48,538]{1,0:T(8,128)(2,1)S(1)}, bf16[48,538]{1,0:T(8,128)(2,1)S(1)}, u32[]{:S(2)}, u32[]{:S(2)}) collective-permute-start(bf16[48,538]{1,0:T(8,128)(2,1)S(1)} %get-tuple-element.9), channel_id=1, source_target_pairs={{0,40},{8,48},{16,56},{24,64},{32,72},{40,80},{48,88},{56,96},{64,... | collective-permute-start | bytes 154952
  326.5 12.9 %collective-permute-start.11 = (bf16[48,538]{1,0:T(8,128)(2,1)S(1)}, bf16[48,538]{1,0:T(8,128)(2,1)S(1)}, u32[]{:S(2)}, u32[]{:S(2)}) collective-permute-start(bf16[48,538]{1,0:T(8,128)(2,1)S(1)} %get-tuple-element.9), channel_id=1, source_target_pairs={{0,32},{8,40},{16,48},{24,56},{32,64},{40,72},{48,80},{56,88},{64,... | collective-permute-start | bytes 154952
  328.8 10.7 %collective-permute-start.10 = (bf16[48,538]{1,0:T(8,128)(2,1)S(1)}, bf16[48,538]{1,0:T(8,128)(2,1)S(1)}, u32[]{:S(2)}, u32[]{:S(2)}) collective-permute-start(bf16[48,538]{1,0:T(8,128)(2,1)S(1)} %get-tuple-element.9), channel_id=1, source_target_pairs={{0,24},{8,32},{16,40},{24,48},{32,56},{40,64},{48,72},{56,80},{64,... | collective-permute-start | bytes 154952
  331.1 8.4 %collective-permute-start.9 = (bf16[48,538]{1,0:T(8,128)(2,1)S(1)}, bf16[48,538]{1,0:T(8,128)(2,1)S(1)}, u32[]{:S(2)}, u32[]{:S(2)}) collective-permute-start(bf16[48,538]{1,0:T(8,128)(2,1)S(1)} %get-tuple-element.9), channel_id=1, source_target_pairs={{0,16},{8,24},{16,32},{24,40},{32,48},{40,56},{48,64},{56,72},{64,... | collective-permute-start | bytes 154952
  333.2 6.2 %collective-permute-start.8 = (bf16[48,538]{1,0:T(8,128)(2,1)S(1)}, bf16[48,538]{1,0:T(8,128)(2,1)S(1)}, u32[]{:S(2)}, u32[]{:S(2)}) collective-permute-start(bf16[48,538]{1,0:T(8,128)(2,1)S(1)} %get-tuple-element.9), channel_id=1, source_target_pairs={{0,8},{8,16},{16,24},{24,32},{32,40},{40,48},{48,56},{56,64},{64,7... | collective-permute-start | bytes 154952
  (9 other events, 147.9 us)
Sparse Core Ops, SparseCore 0:
  13.9 90.6 all-reduce.8
  109.3 87.3 all-reduce.10
  200.8 90.8 all-reduce.12
Sparse Core Ops, SparseCore 1:
  16.7 68.5 all-gather.1
  203.7 119.5 reduce-scatter.5
where the time goes:
time: 358 us; the launch traced here: 356 us
  waiting for transfers between devices  177 us (49%)
  blocking collectives  71.5 us (20%)
  starting transfers between devices  57 us (16%)
  between operations  17.7 us (5%)
  matrix products  13.2 us (4%)
  other arithmetic  13 us (4%)
  local copies, waits for them, and re-layouts  6.82 us (2%)
    psum x1, waiting for transfers between devices, local(): embed = xf + lax.psum(partial_out, 'tensor')  88.5 us
    psum x1, waiting for transfers between devices, local(): du = lax.psum(du_acc.astype(jnp.bfloat16), 'tensor').astype(jnp.float32)  87.5 us
    unnamed x1, blocking collectives  71.5 us
    unnamed x16, starting transfers between devices  56.8 us
  transfers between devices with their start and end apart: 21, of which 3 were waited for; matrix products, arithmetic and copies ran while one was open for 25% of the time, Pallas kernels for 0%

commit v1 on v0

v1 whole, which is shorter than its diff:
```python
import jax
import jax.numpy as jnp
from jax import lax
from jax.experimental import pallas as pl
from jax.experimental.pallas import tpu as pltpu
from jax.sharding import PartitionSpec as P

F32 = jnp.float32
BF = jnp.bfloat16
I32 = jnp.int32
D = 1152
FF_T = 538
NT = 8
ROWS = 16
COLS = 36
IMG = 128
SEL = 320
LANES = 640
OUT_AT = 576
ROOT = 0.7978845608028654


def dot(a, b, ca=1, cb=0):
    return lax.dot_general(a, b, (((ca,), (cb,)), ((), ())), preferred_element_type=F32)


def swap(x, axis, n, mask):
    return lax.ppermute(x, axis, [(i, i ^ mask) for i in range(n)])


def sds(shape, dtype):
    return jax.ShapeDtypeStruct(shape, dtype)


def hold(x):
    return pltpu.with_memory_space_constraint(x, pltpu.HBM)


def call(body, outs, args, scratch=(), smem=(), after=(), hbm=(), flops=0, size=1 << 20):
    single = not isinstance(outs, (tuple, list))
    outs = (outs,) if single else tuple(outs)
    vm = pl.BlockSpec(memory_space=pltpu.VMEM)
    sm = pl.BlockSpec(memory_space=pltpu.SMEM)
    some = pl.BlockSpec(memory_space=pl.ANY)
    far = pl.BlockSpec(memory_space=pltpu.HBM)
    n_in, n_after, n_out, n_far = len(args), len(after), len(outs), len(hbm)

    def kernel(*refs):
        ins = refs[:n_in]
        results = list(refs[n_in + n_after : n_in + n_after + n_out])
        rest = refs[n_in + n_after + n_out :]
        near, sems, own = rest[:n_far], rest[n_far : 2 * n_far], rest[2 * n_far :]
        copies = []
        for ref, at, sem in zip(near, hbm, sems):
            copies.append(pltpu.make_async_copy(ref, results[at], sem))
            results[at] = ref
        body(*ins, *results, *own)
        for copy in copies:
            copy.start()
        for copy in copies:
            copy.wait()

    got = pl.pallas_call(
        kernel,
        out_shape=tuple(
            pltpu.HBM(o.shape, o.dtype) if i in hbm else o for i, o in enumerate(outs)
        ),
        in_specs=[sm if i in smem else vm for i in range(n_in)] + [some] * n_after,
        out_specs=tuple(far if i in hbm else vm for i in range(n_out)),
        scratch_shapes=[pltpu.VMEM(outs[i].shape, outs[i].dtype) for i in hbm]
        + [pltpu.SemaphoreType.DMA(()) for _ in hbm]
        + list(scratch),
        compiler_params=pltpu.CompilerParams(vmem_limit_bytes=24 << 20),
        cost_estimate=pl.CostEstimate(flops=flops, bytes_accessed=size, transcendentals=0),
    )(*args, *[hold(x) for x in after])
    return got[0] if single else got


def text_unit(tf):
    tnorm = jnp.sqrt(jnp.sum(tf * tf, axis=-1, keepdims=True) + 1e-06)
    return tf / tnorm, tnorm


def text_body(mine, *refs):
    out = refs[3]
    for k, ref in enumerate((mine,) + refs[:3]):
        out[k] = text_unit(ref[...].astype(F32))[0].astype(BF)


def layer_stats(xf):
    centered = xf - jnp.mean(xf, axis=-1, keepdims=True)
    sd = jnp.sqrt(jnp.mean(centered * centered, axis=-1, keepdims=True) + 1e-06)
    return centered / sd, sd


def forward_body(images, gain, w_in, b_in, w_out, normed, hidden, slope, part, *scratch):
    v_images, v_in, v_out, v_normed, v_hidden, v_slope, v_part, sem = scratch

    def move(src, dst, k):
        copy = pltpu.make_async_copy(src, dst, sem.at[k])
        copy.start()
        return copy

    get_images = move(images, v_images, 0)
    get_in = move(w_in, v_in, 1)
    get_out = move(w_out, v_out, 2)
    get_images.wait()
    xhat, _ = layer_stats(v_images[...].astype(F32))
    normed_b = (xhat * gain[...].reshape(1, D)).astype(BF)
    v_normed[...] = normed_b
    put_normed = move(v_normed, normed, 3)
    get_in.wait()
    pre = dot(normed_b, v_in[...], 1, 1) + b_in[...].reshape(1, FF_T)
    square = pre * pre
    th = jnp.tanh(ROOT * (pre + 0.044715 * (square * pre)))
    cdf = 0.5 * (1.0 + th)
    hidden_b = (pre * cdf).astype(BF)
    v_hidden[...] = hidden_b
    put_hidden = move(v_hidden, hidden, 4)
    get_out.wait()
    v_part[...] = dot(hidden_b, v_out[...]).astype(BF).reshape(NT, ROWS, D)
    put_part = move(v_part, part, 5)
    v_slope[...] = cdf + 0.5 * pre * (1.0 - th * th) * (ROOT * (1.0 + 0.134145 * square))
    put_slope = move(v_slope, slope, 6)
    for copy in (put_normed, put_hidden, put_part, put_slope):
        copy.wait()


def forward(images, gain, w_in, b_in, w_out):
    far = pl.BlockSpec(memory_space=pltpu.HBM)
    near = pl.BlockSpec(memory_space=pltpu.VMEM)

    shapes = (
        ((IMG, D), BF),
        ((IMG, FF_T), BF),
        ((IMG, FF_T), F32),
        ((NT, ROWS, D), BF),
    )
    return pl.pallas_call(
        forward_body,
        out_shape=tuple(pltpu.HBM(*shape) for shape in shapes),
        in_specs=[far, near, far, near, far],
        out_specs=(far,) * 4,
        scratch_shapes=[
            pltpu.VMEM((IMG, D), BF),
            pltpu.VMEM((FF_T, D), BF),
            pltpu.VMEM((FF_T, D), BF),
        ]
        + [pltpu.VMEM(*shape) for shape in shapes]
        + [pltpu.SemaphoreType.DMA((7,))],
        compiler_params=pltpu.CompilerParams(vmem_limit_bytes=24 << 20),
        cost_estimate=pl.CostEstimate(
            flops=2 * 160_000_000, bytes_accessed=4 << 20, transcendentals=0
        ),
    )(hold(images), hold(gain), hold(w_in), hold(b_in), hold(w_out))


def embed_body(rank, images, got, t_a, t_b, t_c, t_d, unit, enorm, spread, four):
    text_body(t_a, t_b, t_c, t_d, four)
    at = pl.multiple_of(rank[0] * ROWS, ROWS)
    embed = images[pl.ds(at, ROWS), :].astype(F32)
    embed = embed + jnp.sum(got[...].astype(F32), axis=0)
    norm = jnp.sqrt(jnp.sum(embed * embed, axis=-1, keepdims=True) + 1e-06)
    value = embed / norm
    unit[...] = value
    enorm[...] = jnp.broadcast_to(norm, (ROWS, 128))
    value = value.astype(BF)
    for k in range(NT):
        spread[k] = value


def pairs_body(rank, log_scale, bias, unit, *refs):
    du, c_own, c_oth = refs[8:]
    scale = jnp.exp(jnp.full((1, 1), log_scale[0], F32))
    u = unit[...].reshape(IMG, D)
    total = None
    for half, out in ((0, c_own), (4, c_oth)):
        texts = jnp.concatenate([ref[...].reshape(64, D) for ref in refs[half : half + 4]], axis=0)
        coef = jax.nn.sigmoid(scale * dot(u, texts, 1, 1) + bias[0])
        if half == 0:
            row = lax.broadcasted_iota(I32, (IMG, 256), 0) - rank[0] * ROWS
            col = lax.broadcasted_iota(I32, (IMG, 256), 1)
            coef = coef - jnp.where((row == col) & (col < ROWS), 1.0, 0.0)
        coef = coef.astype(BF)
        out[...] = coef
        part = dot(coef, texts)
        total = part if half == 0 else total + part
    du[...] = (scale * total).astype(BF).reshape(NT, ROWS, D)


def text_grad_body(log_scale, c_mine, u_mine, c_got, u_got, keep, *sent):
    scale = jnp.exp(jnp.full((1, 1), log_scale[0], F32))
    dw = dot(c_mine[...], u_mine[...].reshape(IMG, D), 0, 0)
    dw = scale * (dw + dot(c_got[...], u_got[...].reshape(IMG, D), 0, 0))
    keep[...] = dw[:64]
    for k in range(3):
        sent[k][...] = dw[64 * (k + 1) : 64 * (k + 2)].astype(BF)


def text_fold_body(keep, a, b, c, rest, *sent):
    dw = keep[...] + a[...].astype(F32) + b[...].astype(F32) + c[...].astype(F32)
    rest[...] = dw[:ROWS]
    for k in range(3):
        sent[k][...] = dw[ROWS * (k + 1) : ROWS * (k + 2)].astype(BF)


def embed_grad_body(got, unit, enorm, rows, spread):
    du = jnp.sum(got[...].astype(F32), axis=0)
    u = unit[...]
    de = (du - u * jnp.sum(u * du, axis=-1, keepdims=True)) / enorm[:, :1]
    de = de.astype(BF)
    rows[...] = de
    for k in range(NT):
        spread[k] = de


def slope_body(rank, de, w_out, slope, dpre, *sent):
    value = dot(de[...].reshape(IMG, D), w_out[...], 1, 1) * slope[...]
    dpre[...] = value.astype(BF)
    pack_body(rank, de, dpre, *sent)


def dn_body(dpre, w_in, keep, t_a, t_b, t_c, dn, rest, *sent):
    dn[...] = dot(dpre[...], w_in[...]).astype(BF).reshape(NT, ROWS, D)
    text_fold_body(keep, t_a, t_b, t_c, rest, *sent)


def pack(rank, left, right, lefts, rights):
    r = lax.broadcasted_iota(I32, (SEL, 1), 0)
    block = (r * 52429) >> 21
    place = r - block * 40
    base = jnp.where(place < COLS, block * 72 + place, -4096)
    diff = lax.broadcasted_iota(I32, (SEL, LANES), 1) - base
    for ref, at, x_flip, c_flip in lefts:
        x, c = rank[2] ^ x_flip, rank[1] ^ c_flip
        window = pl.ds(pl.multiple_of(x * 512, 512), LANES)
        one = jnp.where(diff == x * 64 + c * COLS, 1.0, 0.0).astype(BF)
        ref[at : at + SEL] = dot(one, left[:, :, window].reshape(IMG, LANES), 1, 1).astype(BF)
    wide = jnp.concatenate([right[...].astype(F32), jnp.zeros((IMG, LANES - FF_T), F32)], axis=1)
    wide = wide.astype(BF)
    for k in range(5):
        for ref, at in rights:
            ref[at + k * 128 : at + (k + 1) * 128] = wide[:, k * 128 : (k + 1) * 128]


def pack_relay_body(rank, left, right, mine, to_core, to_x):
    lefts = ((mine, 0, 0, 0), (to_core, 0, 0, 1), (to_x, 0, 1, 0), (to_x, SEL, 1, 1))
    pack(rank, left, right, lefts, ((to_core, SEL), (to_x, 2 * SEL)))


def pack_body(rank, left, right, mine, to_core, to_x, to_both):
    lefts = ((to_x, 0, 1, 0), (to_both, 0, 1, 1), (mine, 0, 0, 0), (to_core, 0, 0, 1))
    pack(rank, left, right, lefts, ((to_core, SEL), (to_x, SEL), (to_both, SEL)))


def weights_body(*refs):
    n_mine, n_own, n_core, n_x, n_xc = refs[:5]
    e_mine, e_own, e_core, e_x, e_xc = refs[5:10]
    out = refs[10]

    def left(*parts):
        return jnp.concatenate([ref[at : at + SEL] for ref, at in parts], axis=1)

    def right(*parts):
        rows = []
        for ref, at in parts:
            chunks = [ref[at + k * 128 : at + (k + 1) * 128] for k in range(5)]
            rows.append(jnp.concatenate(chunks, axis=1))
        return jnp.concatenate(rows, axis=0)

    in_part = dot(
        left((n_mine, 0), (n_core, 0), (n_x, 0), (n_xc, SEL)),
        right((e_own, SEL), (e_core, SEL), (e_x, SEL), (e_xc, SEL)),
    )
    out_part = dot(
        left((e_mine, 0), (e_core, 0), (e_x, 0), (e_xc, 0)),
        right((n_own, SEL), (n_core, SEL), (n_x, 2 * SEL), (n_xc, 2 * SEL)),
    )
    both = jnp.concatenate([in_part[:, :OUT_AT], out_part[:, :OUT_AT]], axis=1)
    for k in range(8):
        out[k] = both[k * 40 : (k + 1) * 40].astype(BF)


def image_body(rank, got, images, gain, de_rows, rows):
    dn = jnp.sum(got[...].astype(F32), axis=0)
    at = pl.multiple_of(rank[0] * ROWS, ROWS)
    xhat, sd = layer_stats(images[pl.ds(at, ROWS), :].astype(F32))
    dxh = dn * gain[...].reshape(1, D)
    grad = (
        dxh
        - jnp.mean(dxh, axis=-1, keepdims=True)
        - xhat * jnp.mean(dxh * xhat, axis=-1, keepdims=True)
    ) / sd
    rows[...] = (de_rows[...].astype(F32) + grad).astype(BF)


def place_body(rank, *refs):
    out = refs[NT]
    for ref, k in zip(refs[:NT], (0, 1, 2, 4, 6, 3, 5, 7)):
        at = pl.multiple_of((rank[0] ^ k) * ROWS, ROWS)
        out[pl.ds(at, ROWS), :] = ref[...].astype(F32)


def final_body(got, texts, rest, a, b, c, text_grad, in_grad, out_grad):
    total = got[0].astype(F32)
    for k in range(1, 8):
        total = total + got[k].astype(F32)
    in_grad[...] = total[:COLS, 0:FF_T]
    out_grad[...] = total[:COLS, OUT_AT : OUT_AT + FF_T]
    dw = rest[...] + a[...].astype(F32) + b[...].astype(F32) + c[...].astype(F32)
    tunit, tnorm = text_unit(texts[...].astype(F32))
    text_grad[...] = (dw - tunit * jnp.sum(tunit * dw, axis=-1, keepdims=True)) / tnorm


def local(images, gain, w_in, b_in, w_out, texts, log_scale, bias):
    rank_d = lax.axis_index("dp")
    rank_t = lax.axis_index("tensor")
    rank = jnp.stack([rank_t, rank_d % 2, rank_d // 16]).astype(I32)
    w_in = w_in.T
    block = sds((ROWS, D), BF)
    blocks = sds((NT, ROWS, D), BF)
    groups = [[x * 16 + k * 2 + c for k in range(8)] for x in range(2) for c in range(2)]

    def tensor_all(x):
        return lax.all_to_all(x, "tensor", 0, 0, tiled=True)

    def dp(x, mask):
        return swap(x, "dp", 32, mask)

    normed, hidden, slope, part = forward(images, gain, w_in, b_in, w_out)
    unit, enorm, spread, four = call(
        embed_body,
        (sds((ROWS, D), F32), sds((ROWS, 128), F32), blocks, sds((4, ROWS, D), BF)),
        (rank, hold(images), tensor_all(part), hold(texts), dp(texts, 4), dp(texts, 8), dp(texts, 12)),
        smem=(0,),
        hbm=(0, 1, 2, 3),
    )
    t_own = [four, dp(four, 2), dp(four, 16), dp(four, 18)]
    t_oth = [dp(x, 1) for x in t_own]
    unit_b = tensor_all(spread)
    du, c_own, c_oth = call(
        pairs_body,
        (blocks, sds((IMG, 256), BF), sds((IMG, 256), BF)),
        (rank, log_scale, bias, unit_b, hold(four), *t_own[1:], *t_oth),
        smem=(0, 1, 2),
        hbm=(0, 1, 2),
        flops=2 * 150_000_000,
        size=2 << 20,
    )
    u_got = dp(unit_b, 1)
    c_got = dp(c_oth, 1)
    sixty = sds((4 * ROWS, D), BF)
    keep, *sent = call(
        text_grad_body,
        (sds((4 * ROWS, D), F32), sixty, sixty, sixty),
        (log_scale, hold(c_own), unit_b, c_got, u_got),
        smem=(0,),
        hbm=(0, 1, 2, 3),
        flops=2 * 75_000_000,
        size=2 << 20,
    )
    got = [dp(x, mask) for x, mask in zip(sent, (2, 16, 18))]
    n_mine, n_own, n_tox = call(
        pack_relay_body,
        (sds((SEL, 128), BF), sds((3 * SEL, 128), BF), sds((4 * SEL, 128), BF)),
        (rank, hold(normed.reshape(NT, ROWS, D)), hold(hidden)),
        smem=(0,),
        hbm=(0, 1, 2),
        after=(du,),
        flops=2 * 100_000_000,
        size=2 << 20,
    )
    n_core = dp(n_own, 1)
    n_x = dp(n_tox, 16)
    n_xc = dp(n_x, 1)
    de_rows, spread = call(
        embed_grad_body,
        (block, blocks),
        (tensor_all(du), hold(unit), hold(enorm)),
        hbm=(0, 1),
        after=(keep, n_own),
    )
    de = tensor_all(spread)

    operand = sds((3 * SEL, 128), BF)
    dpre, e_mine, e_own, e_tox, e_toxc = call(
        slope_body,
        (sds((IMG, FF_T), BF), sds((SEL, 128), BF), operand, operand, operand),
        (rank, de, hold(w_out), hold(slope)),
        smem=(0,),
        hbm=(1, 2, 3, 4),
        after=(n_x,),
        flops=2 * 180_000_000,
        size=4 << 20,
    )
    e_x = dp(e_tox, 16)
    e_xc = dp(e_toxc, 17)
    e_core = dp(e_own, 1)
    dn, rest, *sent = call(
        dn_body,
        (blocks, sds((ROWS, D), F32), block, block, block),
        (dpre, w_in, hold(keep), *got),
        hbm=(0, 1, 2, 3, 4),
        after=(n_core, n_xc),
        flops=2 * 80_000_000,
        size=2 << 20,
    )
    dn = tensor_all(dn)
    got = [dp(x, mask) for x, mask in zip(sent, (4, 8, 12))]
    rows = call(
        image_body, block, (rank, dn, hold(images), hold(gain), hold(de_rows)), smem=(0,), hbm=(0,)
    )
    payload = call(
        weights_body,
        sds((8, 40, D), BF),
        (hold(n_mine), hold(n_own), n_core, n_x, n_xc)
        + (hold(e_mine), hold(e_own), e_core, e_x, e_xc),
        hbm=(0,),
        after=(rows, *got),
        flops=2 * 160_000_000,
        size=3 << 20,
    )
    total = lax.all_to_all(payload, "dp", 0, 0, tiled=True, axis_index_groups=groups)

    spread = [rows] + [swap(rows, "tensor", NT, k) for k in (1, 2, 4, 6)]
    spread += [swap(spread[1], "tensor", NT, k) for k in (2, 4, 6)]
    image_grad = call(place_body, sds((IMG, D), F32), (rank, *spread), smem=(0,))
    text_grad, in_grad, out_grad = call(
        final_body,
        (sds((ROWS, D), F32), sds((COLS, FF_T), F32), sds((COLS, FF_T), F32)),
        (total, hold(texts), hold(rest), *got),
    )
    return (image_grad, text_grad, in_grad, out_grad)


def solution(mesh):
    return jax.shard_map(
        local,
        mesh=mesh,
        in_specs=(
            P("dp", None),
            P(),
            P(None, "tensor"),
            P("tensor"),
            P("tensor", None),
            P(("dp", "tensor"), None),
            P(),
            P(),
        ),
        out_specs=(P("dp", None), P(("dp", "tensor"), None), P("dp", "tensor"), P("dp", "tensor")),
        check_vma=False,
    )
```

time: 358 us -> 142 us (0.40)
  waiting for transfers between devices: 177 us -> 30.3 us
  blocking collectives: 71.5 us -> 0 us
  Pallas kernels: 0 us -> 28.3 us
  starting transfers between devices: 57 us -> 78.8 us
  between operations: 17.7 us -> 2.33 us
  matrix products: 13.2 us -> 0 us
  other arithmetic: 13 us -> 0.08 us
  local copies, waits for them, and re-layouts: 6.82 us -> 0.83 us
    psum x3 -> x0, waiting for transfers between devices: 176 us -> none  [the longest x1 88.5 us: local(): embed = xf + lax.psum(partial_out, 'tensor')]
    unnamed x1 -> x0, blocking collectives: 71.5 us -> none
    unnamed x16 -> x0, starting transfers between devices: 56.8 us -> none
    ppermute x0 -> x31, starting transfers between devices: none -> 47.7 us  [swap(): return lax.ppermute(x, axis, [(i, i ^ mask) for i in range(n)])]
    all_to_all x0 -> x6, starting transfers between devices: none -> 31.1 us  [the longest x5 27.5 us: tensor_all(): return lax.all_to_all(x, 'tensor', 0, 0, tiled=True)]
    pallas_call x0 -> x12, Pallas kernels: none -> 28.3 us  [the longest x11 24.2 us: call(): pl.pallas_call(kernel, out_shape=tuple((pltpu.HBM(o.shape, o.dtype) if i...]
    all_to_all x0 -> x6, waiting for transfers between devices: none -> 15.3 us  [the longest x5 9.78 us: tensor_all(): return lax.all_to_all(x, 'tensor', 0, 0, tiled=True)]
    ppermute x0 -> x31, waiting for transfers between devices: none -> 15 us  [swap(): return lax.ppermute(x, axis, [(i, i ^ mask) for i in range(n)])]
  transfers between devices with their start and end apart: 21 -> 37, of which waited for: 3 -> 13; matrix products, arithmetic and copies ran while one was open for 25% -> 0% of each run, Pallas kernels for 0% -> 7%
where the time goes in v1:
time: 142 us; the launch traced here: 141 us
  starting transfers between devices  78.8 us (55%)
  waiting for transfers between devices  30.3 us (21%)
  Pallas kernels  28.3 us (20%)
  between operations  2.33 us (2%)
    ppermute x31, starting transfers between devices, swap(): return lax.ppermute(x, axis, [(i, i ^ mask) for i in range(n)])  47.7 us
    all_to_all x5, starting transfers between devices, tensor_all(): return lax.all_to_all(x, 'tensor', 0, 0, tiled=True)  27.5 us
    pallas_call x11, Pallas kernels, call(): pl.pallas_call(kernel, out_shape=tuple((pltpu.HBM(o.shape, o.dtype) if i...  24.2 us
    ppermute x31, waiting for transfers between devices, swap(): return lax.ppermute(x, axis, [(i, i ^ mask) for i in range(n)])  15 us
    all_to_all x5, waiting for transfers between devices, tensor_all(): return lax.all_to_all(x, 'tensor', 0, 0, tiled=True)  9.78 us
    all_to_all x1, waiting for transfers between devices, local(): lax.all_to_all(payload, 'dp', 0, 0, tiled=True, axis_index_groups=groups)  5.53 us
    pallas_call x1, Pallas kernels, forward(): pl.pallas_call(forward_body, out_shape=tuple((pltpu.HBM(*shape) for shape...  4.15 us
    all_to_all x1, starting transfers between devices, local(): lax.all_to_all(payload, 'dp', 0, 0, tiled=True, axis_index_groups=groups)  3.69 us
  transfers between devices with their start and end apart: 37, of which 13 were waited for; matrix products, arithmetic and copies ran while one was open for 0% of the time, Pallas kernels for 7%

profile of v1, /device:TPU:1, one launch (start us, length us, event | category | flops | bytes accessed | tf_op | source)
XLA Modules:
  0.0 140.7 jit_solution(15393497013295624266)
XLA Ops:
  0.6 4.1 %shard_map.111 = (bf16[128,1152]{1,0:T(8,128)(2,1)}, bf16[128,538]{1,0:T(8,128)(2,1)}, f32[128,538]{1,0:T(8,128)}, bf16[8,16,1152]{2,1,0:T(8,128)(2,1)}) custom-call(bf16[128,1152]{1,0:T(8,128)(2,1)} %refs_2_.4, f32[1152]{0:T(1024)} %refs_3_.3, bf16[538,1152]{1,0:T(8,128)(2,1)} %bitcast.5, f32[538]{0:T(1024)} %b_in.1, bf16[538,1152]{1,0:T(8,128)(2,1)} %refs_2_.3), custom_call_target="tpu_custom_call" | custom-call | flops 320000000 | bytes 4194304 | tf_op jit(solution)/shard_map/pallas_call | solution.py:139
  4.8 7.5 %all-to-all-start = ((bf16[8,16,1152]{2,1,0:T(8,128)(2,1)}), bf16[8,16,1152]{2,1,0:T(8,128)(2,1)S(1)}, u32[]{:S(2)}, u32[]{:S(2)}) async-start(bf16[8,16,1152]{2,1,0:T(8,128)(2,1)} %get-tuple-element.37), calls=%async_computation | async-start | bytes 589824 | tf_op jit(solution)/shard_map/all_to_all | solution.py:325
  12.3 3.1 %collective-permute-start = (bf16[16,1152]{1,0:T(8,128)(2,1)S(1)}, bf16[16,1152]{1,0:T(8,128)(2,1)S(1)}, u32[]{:S(2)}, u32[]{:S(2)}) collective-permute-start(bf16[16,1152]{1,0:T(8,128)(2,1)S(1)} %copy-done.16), channel_id=1, source_target_pairs={{0,32},{8,40},{16,48},{24,56},{32,0},{40,8},{48,16},{56,24},{64,96... | collective-permute-start | bytes 110600 | tf_op jit(solution)/shard_map/ppermute | solution.py:28
  15.4 5.1 %collective-permute-start.1 = (bf16[16,1152]{1,0:T(8,128)(2,1)S(1)}, bf16[16,1152]{1,0:T(8,128)(2,1)S(1)}, u32[]{:S(2)}, u32[]{:S(2)}) collective-permute-start(bf16[16,1152]{1,0:T(8,128)(2,1)S(1)} %copy-done.16), channel_id=1, source_target_pairs={{0,64},{8,72},{16,80},{24,88},{32,96},{40,104},{48,112},{56,120},{... | collective-permute-start | bytes 110600 | tf_op jit(solution)/shard_map/ppermute | solution.py:28
  22.2 3.2 %collective-permute-done.2.refs_6_ = bf16[16,1152]{1,0:T(8,128)(2,1)S(1)} collective-permute-done((bf16[16,1152]{1,0:T(8,128)(2,1)S(1)}, bf16[16,1152]{1,0:T(8,128)(2,1)S(1)}, u32[]{:S(2)}, u32[]{:S(2)}) %collective-permute-start.2) | collective-permute-done | bytes 36896 | tf_op jit(solution)/shard_map/ppermute | solution.py:28
  30.1 6.6 %all-to-all-start.1 = ((bf16[8,16,1152]{2,1,0:T(8,128)(2,1)}), bf16[8,16,1152]{2,1,0:T(8,128)(2,1)S(1)}, u32[]{:S(2)}, u32[]{:S(2)}) async-start(bf16[8,16,1152]{2,1,0:T(8,128)(2,1)} %get-tuple-element.38), calls=%async_computation.1 | async-start | bytes 589824 | tf_op jit(solution)/shard_map/all_to_all | solution.py:325
  36.7 4.1 %collective-permute-start.6 = (bf16[4,16,1152]{2,1,0:T(8,128)(2,1)}, bf16[4,16,1152]{2,1,0:T(8,128)(2,1)S(1)}, u32[]{:S(2)}, u32[]{:S(2)}) collective-permute-start(bf16[4,16,1152]{2,1,0:T(8,128)(2,1)} %get-tuple-element.39.refs_4_), channel_id=1, source_target_pairs={{0,8},{8,0},{16,24},{24,16},{32,40},{40,32},{48,56},{56,48},{64,72... | collective-permute-start | bytes 442376 | tf_op jit(solution)/shard_map/ppermute | solution.py:28
  44.5 2.5 %shard_map.113 = (bf16[8,16,1152]{2,1,0:T(8,128)(2,1)}, bf16[128,256]{1,0:T(8,128)(2,1)}, bf16[128,256]{1,0:T(8,128)(2,1)}) custom-call(s32[3]{0:T(128)S(1)} %pad_add_fusion.refs_0_, f32[1]{0:T(128)S(6)} %copy.12.refs_1_.refs_0_, f32[1]{0:T(128)S(6)} %copy.13.refs_2_, bf16[8,16,1152]{2,1,0:T(8,128)(2,1)S(1)} %all-to-all-done.1.refs_3_.refs_2_, ...), custom_call_target="tpu_custom_call" | custom-call | flops 300000000 | bytes 2097152 | tf_op jit(solution)/shard_map/pallas_call | solution.py:63
  47.0 2.5 %shard_map.115 = (bf16[320,128]{1,0:T(8,128)(2,1)}, bf16[960,128]{1,0:T(8,128)(2,1)}, bf16[1280,128]{1,0:T(8,128)(2,1)}) custom-call(s32[3]{0:T(128)S(1)} %pad_add_fusion.refs_0_, bf16[8,16,1152]{2,1,0:T(8,128)(2,1)} %bitcast.7, bf16[128,538]{1,0:T(8,128)(2,1)} %get-tuple-element.47.refs_2_, bf16[8,16,1152]{2,1,0:T(8,128)(2,1)} %get-tuple-element.40.refs_3_), custom_call_target="tpu_custom_call" | custom-call | flops 200000000 | bytes 2097152 | tf_op jit(solution)/shard_map/pallas_call | solution.py:63
  49.9 5.5 %collective-permute-start.11 = (bf16[8,16,1152]{2,1,0:T(8,128)(2,1)S(1)}, bf16[8,16,1152]{2,1,0:T(8,128)(2,1)S(1)}, u32[]{:S(2)}, u32[]{:S(2)}) collective-permute-start(bf16[8,16,1152]{2,1,0:T(8,128)(2,1)S(1)} %all-to-all-done.1.refs_3_.refs_2_), channel_id=1, source_target_pairs={{0,8},{8,0},{16,24},{24,16},{32,40},{40,32},{48,56},{56,48},{64,72... | collective-permute-start | bytes 884744 | tf_op jit(solution)/shard_map/ppermute | solution.py:28
  55.4 3.4 %all-to-all-start.2 = ((bf16[8,16,1152]{2,1,0:T(8,128)(2,1)}), bf16[8,16,1152]{2,1,0:T(8,128)(2,1)S(1)}, u32[]{:S(2)}, u32[]{:S(2)}) async-start(bf16[8,16,1152]{2,1,0:T(8,128)(2,1)} %get-tuple-element.40.refs_3_), calls=%async_computation.2 | async-start | bytes 589824 | tf_op jit(solution)/shard_map/all_to_all | solution.py:325
  59.0 3.4 %collective-permute-start.17 = (bf16[1280,128]{1,0:T(8,128)(2,1)S(1)}, bf16[1280,128]{1,0:T(8,128)(2,1)S(1)}, u32[]{:S(2)}, u32[]{:S(2)}) collective-permute-start(bf16[1280,128]{1,0:T(8,128)(2,1)S(1)} %collective-permute-done.12.refs_4_.refs_3_), channel_id=1, source_target_pairs={{0,8},{8,0},{16,24},{24,16},{32,40},{40,32},{48,56},{56,48},{64,72... | collective-permute-start | bytes 983048 | tf_op jit(solution)/shard_map/ppermute | solution.py:28
  64.6 3.5 %all-to-all-done.2.refs_0_ = bf16[8,16,1152]{2,1,0:T(8,128)(2,1)S(1)} async-done(((bf16[8,16,1152]{2,1,0:T(8,128)(2,1)}), bf16[8,16,1152]{2,1,0:T(8,128)(2,1)S(1)}, u32[]{:S(2)}, u32[]{:S(2)}) %all-to-all-start.2) | async-done | bytes 294944 | tf_op jit(solution)/shard_map/all_to_all | solution.py:325
  69.8 3.4 %all-to-all-start.3 = ((bf16[8,16,1152]{2,1,0:T(8,128)(2,1)}), bf16[8,16,1152]{2,1,0:T(8,128)(2,1)S(1)}, u32[]{:S(2)}, u32[]{:S(2)}) async-start(bf16[8,16,1152]{2,1,0:T(8,128)(2,1)} %get-tuple-element.49), calls=%async_computation.3 | async-start | bytes 589824 | tf_op jit(solution)/shard_map/all_to_all | solution.py:325
  76.8 4.5 %all-to-all-done.3.refs_1_ = bf16[8,16,1152]{2,1,0:T(8,128)(2,1)S(1)} async-done(((bf16[8,16,1152]{2,1,0:T(8,128)(2,1)}), bf16[8,16,1152]{2,1,0:T(8,128)(2,1)S(1)}, u32[]{:S(2)}, u32[]{:S(2)}) %all-to-all-start.3) | async-done | bytes 294944 | tf_op jit(solution)/shard_map/all_to_all | solution.py:325
  81.3 3.2 %shard_map.117 = (bf16[128,538]{1,0:T(8,128)(2,1)S(1)}, bf16[320,128]{1,0:T(8,128)(2,1)}, bf16[960,128]{1,0:T(8,128)(2,1)}, bf16[960,128]{1,0:T(8,128)(2,1)}, bf16[960,128]{1,0:T(8,128)(2,1)}) custom-call(s32[3]{0:T(128)S(1)} %pad_add_fusion.refs_0_, bf16[8,16,1152]{2,1,0:T(8,128)(2,1)S(1)} %all-to-all-done.3.refs_1_, bf16[538,1152]{1,0:T(8,128)(2,1)} %refs_2_.3, ...), custom_call_target="tpu_custom_call" | custom-call | flops 360000000 | bytes 4194304 | tf_op jit(solution)/shard_map/pallas_call | solution.py:63
  87.6 6.6 %all-to-all-start.4 = ((bf16[8,16,1152]{2,1,0:T(8,128)(2,1)}), bf16[8,16,1152]{2,1,0:T(8,128)(2,1)S(1)}, u32[]{:S(2)}, u32[]{:S(2)}) async-start(bf16[8,16,1152]{2,1,0:T(8,128)(2,1)} %get-tuple-element.56), calls=%async_computation.4 | async-start | bytes 589824 | tf_op jit(solution)/shard_map/all_to_all | solution.py:325
  109.9 2.8 %shard_map.121 = bf16[8,40,1152]{2,1,0:T(8,128)(2,1)} custom-call(bf16[320,128]{1,0:T(8,128)(2,1)} %get-tuple-element.58.refs_0_, bf16[960,128]{1,0:T(8,128)(2,1)} %get-tuple-element.48.refs_4_.refs_1_, bf16[960,128]{1,0:T(8,128)(2,1)S(1)} %copy-done.6, bf16[1280,128]{1,0:T(8,128)(2,1)S(1)} %copy-done.2, bf16[1280,128]{1,0:T(8,128)(2,1)S(1)} %copy-done.4, ...), custom_call_target="tpu_custom_call" | custom-call | flops 320000000 | bytes 3145728 | tf_op jit(solution)/shard_map/pallas_call | solution.py:63
  112.8 3.7 %all-to-all-start.5 = ((bf16[8,40,1152]{2,1,0:T(8,128)(2,1)}), bf16[8,40,1152]{2,1,0:T(8,128)(2,1)S(1)}, u32[]{:S(2)}, u32[]{:S(2)}) async-start(bf16[8,40,1152]{2,1,0:T(8,128)(2,1)} %shard_map.121), calls=%async_computation.5 | async-start | bytes 1474560 | tf_op jit(solution)/shard_map/all_to_all | solution.py:423
  116.5 3.3 %collective-permute-start.18 = (bf16[16,1152]{1,0:T(8,128)(2,1)S(1)}, bf16[16,1152]{1,0:T(8,128)(2,1)S(1)}, u32[]{:S(2)}, u32[]{:S(2)}) collective-permute-start(bf16[16,1152]{1,0:T(8,128)(2,1)S(1)} %copy-done.7), channel_id=1, source_target_pairs={{0,1},{1,0},{2,3},{3,2},{4,5},{5,4},{6,7},{7,6},{8,9},{9,8},{10,11... | collective-permute-start | bytes 110600 | tf_op jit(solution)/shard_map/ppermute | solution.py:28
  121.0 2.4 %collective-permute-start.20 = (bf16[16,1152]{1,0:T(8,128)(2,1)S(1)}, bf16[16,1152]{1,0:T(8,128)(2,1)S(1)}, u32[]{:S(2)}, u32[]{:S(2)}) collective-permute-start(bf16[16,1152]{1,0:T(8,128)(2,1)S(1)} %copy-done.7), channel_id=1, source_target_pairs={{0,4},{1,5},{2,6},{3,7},{4,0},{5,1},{6,2},{7,3},{8,12},{9,13},{10,... | collective-permute-start | bytes 110600 | tf_op jit(solution)/shard_map/ppermute | solution.py:28
  123.7 3.6 %collective-permute-start.23 = (bf16[16,1152]{1,0:T(8,128)(2,1)S(1)}, bf16[16,1152]{1,0:T(8,128)(2,1)S(1)}, u32[]{:S(2)}, u32[]{:S(2)}) collective-permute-start(bf16[16,1152]{1,0:T(8,128)(2,1)S(1)} %collective-permute-done.18.refs_2_), channel_id=1, source_target_pairs={{0,4},{1,5},{2,6},{3,7},{4,0},{5,1},{6,2},{7,3},{8,12},{9,13},{10,... | collective-permute-start | bytes 110600 | tf_op jit(solution)/shard_map/ppermute | solution.py:28
  129.1 2.8 %collective-permute-done.24.refs_8_ = bf16[16,1152]{1,0:T(8,128)(2,1)S(1)} collective-permute-done((bf16[16,1152]{1,0:T(8,128)(2,1)S(1)}, bf16[16,1152]{1,0:T(8,128)(2,1)S(1)}, u32[]{:S(2)}, u32[]{:S(2)}) %collective-permute-start.24) | collective-permute-done | bytes 36896 | tf_op jit(solution)/shard_map/ppermute | solution.py:28
  133.3 5.5 %all-to-all-done.5.refs_0_ = bf16[8,40,1152]{2,1,0:T(8,128)(2,1)S(1)} async-done(((bf16[8,40,1152]{2,1,0:T(8,128)(2,1)}), bf16[8,40,1152]{2,1,0:T(8,128)(2,1)S(1)}, u32[]{:S(2)}, u32[]{:S(2)}) %all-to-all-start.5) | async-done | bytes 737312 | tf_op jit(solution)/shard_map/all_to_all | solution.py:423
  (105 shorter events, 42.1 us)
Async XLA Ops:
  4.8 20.6 %all-to-all-start = ((bf16[8,16,1152]{2,1,0:T(8,128)(2,1)}), bf16[8,16,1152]{2,1,0:T(8,128)(2,1)S(1)}, u32[]{:S(2)}, u32[]{:S(2)}) async-start(bf16[8,16,1152]{2,1,0:T(8,128)(2,1)} %get-tuple-element.37), calls=%async_computation | async-start | bytes 589824 | tf_op jit(solution)/shard_map/all_to_all | solution.py:325
  12.3 8.3 %collective-permute-start = (bf16[16,1152]{1,0:T(8,128)(2,1)S(1)}, bf16[16,1152]{1,0:T(8,128)(2,1)S(1)}, u32[]{:S(2)}, u32[]{:S(2)}) collective-permute-start(bf16[16,1152]{1,0:T(8,128)(2,1)S(1)} %copy-done.16), channel_id=1, source_target_pairs={{0,32},{8,40},{16,48},{24,56},{32,0},{40,8},{48,16},{56,24},{64,96... | collective-permute-start | bytes 110600 | tf_op jit(solution)/shard_map/ppermute | solution.py:28
  15.4 6.9 %collective-permute-start.1 = (bf16[16,1152]{1,0:T(8,128)(2,1)S(1)}, bf16[16,1152]{1,0:T(8,128)(2,1)S(1)}, u32[]{:S(2)}, u32[]{:S(2)}) collective-permute-start(bf16[16,1152]{1,0:T(8,128)(2,1)S(1)} %copy-done.16), channel_id=1, source_target_pairs={{0,64},{8,72},{16,80},{24,88},{32,96},{40,104},{48,112},{56,120},{... | collective-permute-start | bytes 110600 | tf_op jit(solution)/shard_map/ppermute | solution.py:28
  27.4 13.4 %collective-permute-start.3 = (bf16[4,16,1152]{2,1,0:T(8,128)(2,1)}, bf16[4,16,1152]{2,1,0:T(8,128)(2,1)S(1)}, u32[]{:S(2)}, u32[]{:S(2)}) collective-permute-start(bf16[4,16,1152]{2,1,0:T(8,128)(2,1)} %get-tuple-element.39.refs_4_), channel_id=1, source_target_pairs={{0,16},{8,24},{16,0},{24,8},{32,48},{40,56},{48,32},{56,40},{64,80... | collective-permute-start | bytes 442376 | tf_op jit(solution)/shard_map/ppermute | solution.py:28
  28.2 12.6 %collective-permute-start.4 = (bf16[4,16,1152]{2,1,0:T(8,128)(2,1)}, bf16[4,16,1152]{2,1,0:T(8,128)(2,1)S(1)}, u32[]{:S(2)}, u32[]{:S(2)}) collective-permute-start(bf16[4,16,1152]{2,1,0:T(8,128)(2,1)} %get-tuple-element.39.refs_4_), channel_id=1, source_target_pairs={{0,128},{8,136},{16,144},{24,152},{32,160},{40,168},{48,176},{56,1... | collective-permute-start | bytes 442376 | tf_op jit(solution)/shard_map/ppermute | solution.py:28
  28.5 12.8 %collective-permute-start.5 = (bf16[4,16,1152]{2,1,0:T(8,128)(2,1)}, bf16[4,16,1152]{2,1,0:T(8,128)(2,1)S(1)}, u32[]{:S(2)}, u32[]{:S(2)}) collective-permute-start(bf16[4,16,1152]{2,1,0:T(8,128)(2,1)} %get-tuple-element.39.refs_4_), channel_id=1, source_target_pairs={{0,144},{8,152},{16,128},{24,136},{32,176},{40,184},{48,160},{56,1... | collective-permute-start | bytes 442376 | tf_op jit(solution)/shard_map/ppermute | solution.py:28
  30.1 14.4 %all-to-all-start.1 = ((bf16[8,16,1152]{2,1,0:T(8,128)(2,1)}), bf16[8,16,1152]{2,1,0:T(8,128)(2,1)S(1)}, u32[]{:S(2)}, u32[]{:S(2)}) async-start(bf16[8,16,1152]{2,1,0:T(8,128)(2,1)} %get-tuple-element.38), calls=%async_computation.1 | async-start | bytes 589824 | tf_op jit(solution)/shard_map/all_to_all | solution.py:325
  49.5 9.5 %collective-permute-start.12 = (bf16[1280,128]{1,0:T(8,128)(2,1)}, bf16[1280,128]{1,0:T(8,128)(2,1)S(1)}, u32[]{:S(2)}, u32[]{:S(2)}) collective-permute-start(bf16[1280,128]{1,0:T(8,128)(2,1)} %get-tuple-element.51), channel_id=1, source_target_pairs={{0,128},{8,136},{16,144},{24,152},{32,160},{40,168},{48,176},{56,1... | collective-permute-start | bytes 983048 | tf_op jit(solution)/shard_map/ppermute | solution.py:28
  49.9 12.5 %collective-permute-start.11 = (bf16[8,16,1152]{2,1,0:T(8,128)(2,1)S(1)}, bf16[8,16,1152]{2,1,0:T(8,128)(2,1)S(1)}, u32[]{:S(2)}, u32[]{:S(2)}) collective-permute-start(bf16[8,16,1152]{2,1,0:T(8,128)(2,1)S(1)} %all-to-all-done.1.refs_3_.refs_2_), channel_id=1, source_target_pairs={{0,8},{8,0},{16,24},{24,16},{32,40},{40,32},{48,56},{56,48},{64,72... | collective-permute-start | bytes 884744 | tf_op jit(solution)/shard_map/ppermute | solution.py:28
  55.4 12.7 %all-to-all-start.2 = ((bf16[8,16,1152]{2,1,0:T(8,128)(2,1)}), bf16[8,16,1152]{2,1,0:T(8,128)(2,1)S(1)}, u32[]{:S(2)}, u32[]{:S(2)}) async-start(bf16[8,16,1152]{2,1,0:T(8,128)(2,1)} %get-tuple-element.40.refs_3_), calls=%async_computation.2 | async-start | bytes 589824 | tf_op jit(solution)/shard_map/all_to_all | solution.py:325
  59.0 25.7 %collective-permute-start.17 = (bf16[1280,128]{1,0:T(8,128)(2,1)S(1)}, bf16[1280,128]{1,0:T(8,128)(2,1)S(1)}, u32[]{:S(2)}, u32[]{:S(2)}) collective-permute-start(bf16[1280,128]{1,0:T(8,128)(2,1)S(1)} %collective-permute-done.12.refs_4_.refs_3_), channel_id=1, source_target_pairs={{0,8},{8,0},{16,24},{24,16},{32,40},{40,32},{48,56},{56,48},{64,72... | collective-permute-start | bytes 983048 | tf_op jit(solution)/shard_map/ppermute | solution.py:28
  69.8 11.5 %all-to-all-start.3 = ((bf16[8,16,1152]{2,1,0:T(8,128)(2,1)}), bf16[8,16,1152]{2,1,0:T(8,128)(2,1)S(1)}, u32[]{:S(2)}, u32[]{:S(2)}) async-start(bf16[8,16,1152]{2,1,0:T(8,128)(2,1)} %get-tuple-element.49), calls=%async_computation.3 | async-start | bytes 589824 | tf_op jit(solution)/shard_map/all_to_all | solution.py:325
  73.3 11.3 %collective-permute-start.16 = (bf16[960,128]{1,0:T(8,128)(2,1)S(1)}, bf16[960,128]{1,0:T(8,128)(2,1)S(1)}, u32[]{:S(2)}, u32[]{:S(2)}) collective-permute-start(bf16[960,128]{1,0:T(8,128)(2,1)S(1)} %copy-done.14), channel_id=1, source_target_pairs={{0,8},{8,0},{16,24},{24,16},{32,40},{40,32},{48,56},{56,48},{64,72... | collective-permute-start | bytes 737288 | tf_op jit(solution)/shard_map/ppermute | solution.py:28
  74.2 10.4 %collective-permute-start.13 = (bf16[64,1152]{1,0:T(8,128)(2,1)}, bf16[64,1152]{1,0:T(8,128)(2,1)S(1)}, u32[]{:S(2)}, u32[]{:S(2)}) collective-permute-start(bf16[64,1152]{1,0:T(8,128)(2,1)} %get-tuple-element.53), channel_id=1, source_target_pairs={{0,16},{8,24},{16,0},{24,8},{32,48},{40,56},{48,32},{56,40},{64,80... | collective-permute-start | bytes 442376 | tf_op jit(solution)/shard_map/ppermute | solution.py:28
  74.9 9.7 %collective-permute-start.14 = (bf16[64,1152]{1,0:T(8,128)(2,1)S(1)}, bf16[64,1152]{1,0:T(8,128)(2,1)S(1)}, u32[]{:S(2)}, u32[]{:S(2)}) collective-permute-start(bf16[64,1152]{1,0:T(8,128)(2,1)S(1)} %copy-done.19), channel_id=1, source_target_pairs={{0,128},{8,136},{16,144},{24,152},{32,160},{40,168},{48,176},{56,1... | collective-permute-start | bytes 442376 | tf_op jit(solution)/shard_map/ppermute | solution.py:28
  76.1 8.5 %collective-permute-start.15 = (bf16[64,1152]{1,0:T(8,128)(2,1)S(1)}, bf16[64,1152]{1,0:T(8,128)(2,1)S(1)}, u32[]{:S(2)}, u32[]{:S(2)}) collective-permute-start(bf16[64,1152]{1,0:T(8,128)(2,1)S(1)} %copy-done.18), channel_id=1, source_target_pairs={{0,144},{8,152},{16,128},{24,136},{32,176},{40,184},{48,160},{56,1... | collective-permute-start | bytes 442376 | tf_op jit(solution)/shard_map/ppermute | solution.py:28
  87.6 16.2 %all-to-all-start.4 = ((bf16[8,16,1152]{2,1,0:T(8,128)(2,1)}), bf16[8,16,1152]{2,1,0:T(8,128)(2,1)S(1)}, u32[]{:S(2)}, u32[]{:S(2)}) async-start(bf16[8,16,1152]{2,1,0:T(8,128)(2,1)} %get-tuple-element.56), calls=%async_computation.4 | async-start | bytes 589824 | tf_op jit(solution)/shard_map/all_to_all | solution.py:325
  94.2 13.5 %collective-permute-start.25 = (bf16[960,128]{1,0:T(8,128)(2,1)S(1)}, bf16[960,128]{1,0:T(8,128)(2,1)S(1)}, u32[]{:S(2)}, u32[]{:S(2)}) collective-permute-start(bf16[960,128]{1,0:T(8,128)(2,1)S(1)} %copy-done.15), channel_id=1, source_target_pairs={{0,8},{8,0},{16,24},{24,16},{32,40},{40,32},{48,56},{56,48},{64,72... | collective-permute-start | bytes 737288 | tf_op jit(solution)/shard_map/ppermute | solution.py:28
  96.4 11.2 %collective-permute-start.26 = (bf16[960,128]{1,0:T(8,128)(2,1)}, bf16[960,128]{1,0:T(8,128)(2,1)S(1)}, u32[]{:S(2)}, u32[]{:S(2)}) collective-permute-start(bf16[960,128]{1,0:T(8,128)(2,1)} %get-tuple-element.61), channel_id=1, source_target_pairs={{0,128},{8,136},{16,144},{24,152},{32,160},{40,168},{48,176},{56,1... | collective-permute-start | bytes 737288 | tf_op jit(solution)/shard_map/ppermute | solution.py:28
  96.4 13.5 %collective-permute-start.27 = (bf16[960,128]{1,0:T(8,128)(2,1)S(1)}, bf16[960,128]{1,0:T(8,128)(2,1)S(1)}, u32[]{:S(2)}, u32[]{:S(2)}) collective-permute-start(bf16[960,128]{1,0:T(8,128)(2,1)S(1)} %copy-done.17), channel_id=1, source_target_pairs={{0,136},{8,128},{16,152},{24,144},{32,168},{40,160},{48,184},{56,1... | collective-permute-start | bytes 737288 | tf_op jit(solution)/shard_map/ppermute | solution.py:28
  99.3 7.2 %collective-permute-start.29 = (bf16[16,1152]{1,0:T(8,128)(2,1)}, bf16[16,1152]{1,0:T(8,128)(2,1)S(1)}, u32[]{:S(2)}, u32[]{:S(2)}) collective-permute-start(bf16[16,1152]{1,0:T(8,128)(2,1)} %get-tuple-element.64), channel_id=1, source_target_pairs={{0,64},{8,72},{16,80},{24,88},{32,96},{40,104},{48,112},{56,120},{... | collective-permute-start | bytes 110600 | tf_op jit(solution)/shard_map/ppermute | solution.py:28
  112.8 26.1 %all-to-all-start.5 = ((bf16[8,40,1152]{2,1,0:T(8,128)(2,1)}), bf16[8,40,1152]{2,1,0:T(8,128)(2,1)S(1)}, u32[]{:S(2)}, u32[]{:S(2)}) async-start(bf16[8,40,1152]{2,1,0:T(8,128)(2,1)} %shard_map.121), calls=%async_computation.5 | async-start | bytes 1474560 | tf_op jit(solution)/shard_map/all_to_all | solution.py:423
  116.5 7.2 %collective-permute-start.18 = (bf16[16,1152]{1,0:T(8,128)(2,1)S(1)}, bf16[16,1152]{1,0:T(8,128)(2,1)S(1)}, u32[]{:S(2)}, u32[]{:S(2)}) collective-permute-start(bf16[16,1152]{1,0:T(8,128)(2,1)S(1)} %copy-done.7), channel_id=1, source_target_pairs={{0,1},{1,0},{2,3},{3,2},{4,5},{5,4},{6,7},{7,6},{8,9},{9,8},{10,11... | collective-permute-start | bytes 110600 | tf_op jit(solution)/shard_map/ppermute | solution.py:28
  119.8 7.4 %collective-permute-start.19 = (bf16[16,1152]{1,0:T(8,128)(2,1)S(1)}, bf16[16,1152]{1,0:T(8,128)(2,1)S(1)}, u32[]{:S(2)}, u32[]{:S(2)}) collective-permute-start(bf16[16,1152]{1,0:T(8,128)(2,1)S(1)} %copy-done.7), channel_id=1, source_target_pairs={{0,2},{1,3},{2,0},{3,1},{4,6},{5,7},{6,4},{7,5},{8,10},{9,11},{10,... | collective-permute-start | bytes 110600 | tf_op jit(solution)/shard_map/ppermute | solution.py:28
  (34 other events, 338.1 us)

commit v2 on v1

--- a/solution.py
+++ b/solution.py
@@ -170,7 +170,8 @@
 
 
 def pairs_body(rank, log_scale, bias, unit, *refs):
-    du, c_own, c_oth = refs[8:]
+    du, c_own, c_oth, again = refs[8:]
+    again[...] = unit[...]
     scale = jnp.exp(jnp.full((1, 1), log_scale[0], F32))
     u = unit[...].reshape(IMG, D)
     total = None
@@ -328,26 +329,37 @@
         return swap(x, "dp", 32, mask)
 
     normed, hidden, slope, part = forward(images, gain, w_in, b_in, w_out)
+    n_mine, n_own, n_tox = call(
+        pack_relay_body,
+        (sds((SEL, 128), BF), sds((3 * SEL, 128), BF), sds((4 * SEL, 128), BF)),
+        (rank, hold(normed.reshape(NT, ROWS, D)), hold(hidden)),
+        smem=(0,),
+        hbm=(0, 1, 2),
+        after=(part,),
+        flops=2 * 100_000_000,
+        size=2 << 20,
+    )
     unit, enorm, spread, four = call(
         embed_body,
         (sds((ROWS, D), F32), sds((ROWS, 128), F32), blocks, sds((4, ROWS, D), BF)),
-        (rank, hold(images), tensor_all(part), hold(texts), dp(texts, 4), dp(texts, 8), dp(texts, 12)),
+        (rank, images, tensor_all(part), texts, dp(texts, 4), dp(texts, 8), dp(texts, 12)),
         smem=(0,),
         hbm=(0, 1, 2, 3),
+        after=(n_own,),
     )
     t_own = [four, dp(four, 2), dp(four, 16), dp(four, 18)]
     t_oth = [dp(x, 1) for x in t_own]
     unit_b = tensor_all(spread)
-    du, c_own, c_oth = call(
+    du, c_own, c_oth, again = call(
         pairs_body,
-        (blocks, sds((IMG, 256), BF), sds((IMG, 256), BF)),
+        (blocks, sds((IMG, 256), BF), sds((IMG, 256), BF), blocks),
         (rank, log_scale, bias, unit_b, hold(four), *t_own[1:], *t_oth),
         smem=(0, 1, 2),
-        hbm=(0, 1, 2),
+        hbm=(0, 1, 2, 3),
         flops=2 * 150_000_000,
         size=2 << 20,
     )
-    u_got = dp(unit_b, 1)
+    u_got = dp(again, 1)
     c_got = dp(c_oth, 1)
     sixty = sds((4 * ROWS, D), BF)
     keep, *sent = call(
@@ -360,16 +372,6 @@
         size=2 << 20,
     )
     got = [dp(x, mask) for x, mask in zip(sent, (2, 16, 18))]
-    n_mine, n_own, n_tox = call(
-        pack_relay_body,
-        (sds((SEL, 128), BF), sds((3 * SEL, 128), BF), sds((4 * SEL, 128), BF)),
-        (rank, hold(normed.reshape(NT, ROWS, D)), hold(hidden)),
-        smem=(0,),
-        hbm=(0, 1, 2),
-        after=(du,),
-        flops=2 * 100_000_000,
-        size=2 << 20,
-    )
     n_core = dp(n_own, 1)
     n_x = dp(n_tox, 16)
     n_xc = dp(n_x, 1)
@@ -378,7 +380,7 @@
         (block, blocks),
         (tensor_all(du), hold(unit), hold(enorm)),
         hbm=(0, 1),
-        after=(keep, n_own),
+        after=(keep,),
     )
     de = tensor_all(spread)
 
@@ -408,7 +410,7 @@
     dn = tensor_all(dn)
     got = [dp(x, mask) for x, mask in zip(sent, (4, 8, 12))]
     rows = call(
-        image_body, block, (rank, dn, hold(images), hold(gain), hold(de_rows)), smem=(0,), hbm=(0,)
+        image_body, block, (rank, dn, images, gain, de_rows), smem=(0,), hbm=(0,)
     )
     payload = call(
         weights_body,
@@ -428,7 +430,7 @@
     text_grad, in_grad, out_grad = call(
         final_body,
         (sds((ROWS, D), F32), sds((COLS, FF_T), F32), sds((COLS, FF_T), F32)),
-        (total, hold(texts), hold(rest), *got),
+        (total, texts, rest, *got),
     )
     return (image_grad, text_grad, in_grad, out_grad)
 

time: 142 us -> 137 us (0.965)
  starting transfers between devices: 78.8 us -> 76 us
  Pallas kernels: 28.3 us -> 26.6 us
    ppermute x31, starting transfers between devices: 47.7 us -> 45.3 us  [swap(): return lax.ppermute(x, axis, [(i, i ^ mask) for i in range(n)])]
    pallas_call x11, Pallas kernels: 24.2 us -> 22.4 us  [call(): pl.pallas_call(kernel, out_shape=tuple((pltpu.HBM(o.shape, o.dtype) if i...]
  transfers between devices with their start and end apart: 37 -> 37, of which waited for: 13 -> 13; matrix products, arithmetic and copies ran while one was open for 0% -> 0% of each run, Pallas kernels for 7% -> 11%
where the time goes in v2:
time: 137 us; the launch traced here: 135 us
  starting transfers between devices  76 us (55%)
  waiting for transfers between devices  29.6 us (22%)
  Pallas kernels  26.6 us (19%)
  between operations  2.33 us (2%)
    ppermute x31, starting transfers between devices, swap(): return lax.ppermute(x, axis, [(i, i ^ mask) for i in range(n)])  45.3 us
    all_to_all x5, starting transfers between devices, tensor_all(): return lax.all_to_all(x, 'tensor', 0, 0, tiled=True)  27 us
    pallas_call x11, Pallas kernels, call(): pl.pallas_call(kernel, out_shape=tuple((pltpu.HBM(o.shape, o.dtype) if i...  22.4 us
    ppermute x31, waiting for transfers between devices, swap(): return lax.ppermute(x, axis, [(i, i ^ mask) for i in range(n)])  13.7 us
    all_to_all x5, waiting for transfers between devices, tensor_all(): return lax.all_to_all(x, 'tensor', 0, 0, tiled=True)  10.5 us
    all_to_all x1, waiting for transfers between devices, local(): lax.all_to_all(payload, 'dp', 0, 0, tiled=True, axis_index_groups=groups)  5.36 us
    pallas_call x1, Pallas kernels, forward(): pl.pallas_call(forward_body, out_shape=tuple((pltpu.HBM(*shape) for shape...  4.14 us
    all_to_all x1, starting transfers between devices, local(): lax.all_to_all(payload, 'dp', 0, 0, tiled=True, axis_index_groups=groups)  3.69 us
  transfers between devices with their start and end apart: 37, of which 13 were waited for; matrix products, arithmetic and copies ran while one was open for 0% of the time, Pallas kernels for 11%

profile of v2, /device:TPU:1, one launch (start us, length us, event | category | flops | bytes accessed | tf_op | source)
XLA Modules:
  0.0 135.5 jit_solution(15146318165181321227)
XLA Ops:
  0.6 4.1 %shard_map.111 = (bf16[128,1152]{1,0:T(8,128)(2,1)}, bf16[128,538]{1,0:T(8,128)(2,1)}, f32[128,538]{1,0:T(8,128)}, bf16[8,16,1152]{2,1,0:T(8,128)(2,1)}) custom-call(bf16[128,1152]{1,0:T(8,128)(2,1)} %refs_2_.4, f32[1152]{0:T(1024)} %refs_3_.3, bf16[538,1152]{1,0:T(8,128)(2,1)} %bitcast.5, f32[538]{0:T(1024)} %b_in.1, bf16[538,1152]{1,0:T(8,128)(2,1)} %refs_2_.3), custom_call_target="tpu_custom_call" | custom-call | flops 320000000 | bytes 4194304 | tf_op jit(solution)/shard_map/pallas_call | solution.py:139
  4.8 7.6 %all-to-all-start = ((bf16[8,16,1152]{2,1,0:T(8,128)(2,1)}), bf16[8,16,1152]{2,1,0:T(8,128)(2,1)S(1)}, u32[]{:S(2)}, u32[]{:S(2)}) async-start(bf16[8,16,1152]{2,1,0:T(8,128)(2,1)} %get-tuple-element.38.refs_3_), calls=%async_computation | async-start | bytes 589824 | tf_op jit(solution)/shard_map/all_to_all | solution.py:326
  12.4 3.1 %collective-permute-start = (bf16[16,1152]{1,0:T(8,128)(2,1)S(1)}, bf16[16,1152]{1,0:T(8,128)(2,1)S(1)}, u32[]{:S(2)}, u32[]{:S(2)}) collective-permute-start(bf16[16,1152]{1,0:T(8,128)(2,1)S(1)} %copy-done.9), channel_id=1, source_target_pairs={{0,32},{8,40},{16,48},{24,56},{32,0},{40,8},{48,16},{56,24},{64,96... | collective-permute-start | bytes 110600 | tf_op jit(solution)/shard_map/ppermute | solution.py:28
  15.5 5.1 %collective-permute-start.1 = (bf16[16,1152]{1,0:T(8,128)(2,1)S(1)}, bf16[16,1152]{1,0:T(8,128)(2,1)S(1)}, u32[]{:S(2)}, u32[]{:S(2)}) collective-permute-start(bf16[16,1152]{1,0:T(8,128)(2,1)S(1)} %copy-done.9), channel_id=1, source_target_pairs={{0,64},{8,72},{16,80},{24,88},{32,96},{40,104},{48,112},{56,120},{... | collective-permute-start | bytes 110600 | tf_op jit(solution)/shard_map/ppermute | solution.py:28
  20.7 2.4 %shard_map.112 = (bf16[320,128]{1,0:T(8,128)(2,1)}, bf16[960,128]{1,0:T(8,128)(2,1)}, bf16[1280,128]{1,0:T(8,128)(2,1)}) custom-call(s32[3]{0:T(128)S(1)} %pad_add_fusion.refs_0_, bf16[8,16,1152]{2,1,0:T(8,128)(2,1)} %bitcast.7, bf16[128,538]{1,0:T(8,128)(2,1)} %get-tuple-element.40.refs_2_, bf16[8,16,1152]{2,1,0:T(8,128)(2,1)} %get-tuple-element.38.refs_3_), custom_call_target="tpu_custom_call" | custom-call | flops 200000000 | bytes 2097152 | tf_op jit(solution)/shard_map/pallas_call | solution.py:63
  23.2 2.4 %collective-permute-done.2.refs_6_ = bf16[16,1152]{1,0:T(8,128)(2,1)S(1)} collective-permute-done((bf16[16,1152]{1,0:T(8,128)(2,1)S(1)}, bf16[16,1152]{1,0:T(8,128)(2,1)S(1)}, u32[]{:S(2)}, u32[]{:S(2)}) %collective-permute-start.2) | collective-permute-done | bytes 36896 | tf_op jit(solution)/shard_map/ppermute | solution.py:28
  29.8 6.6 %all-to-all-start.1 = ((bf16[8,16,1152]{2,1,0:T(8,128)(2,1)}), bf16[8,16,1152]{2,1,0:T(8,128)(2,1)S(1)}, u32[]{:S(2)}, u32[]{:S(2)}) async-start(bf16[8,16,1152]{2,1,0:T(8,128)(2,1)} %get-tuple-element.42), calls=%async_computation.1 | async-start | bytes 589824 | tf_op jit(solution)/shard_map/all_to_all | solution.py:326
  36.3 4.1 %collective-permute-start.6 = (bf16[4,16,1152]{2,1,0:T(8,128)(2,1)}, bf16[4,16,1152]{2,1,0:T(8,128)(2,1)S(1)}, u32[]{:S(2)}, u32[]{:S(2)}) collective-permute-start(bf16[4,16,1152]{2,1,0:T(8,128)(2,1)} %get-tuple-element.43.refs_4_), channel_id=1, source_target_pairs={{0,8},{8,0},{16,24},{24,16},{32,40},{40,32},{48,56},{56,48},{64,72... | collective-permute-start | bytes 442376 | tf_op jit(solution)/shard_map/ppermute | solution.py:28
  44.2 2.5 %shard_map.114 = (bf16[8,16,1152]{2,1,0:T(8,128)(2,1)}, bf16[128,256]{1,0:T(8,128)(2,1)}, bf16[128,256]{1,0:T(8,128)(2,1)}, bf16[8,16,1152]{2,1,0:T(8,128)(2,1)}) custom-call(s32[3]{0:T(128)S(1)} %pad_add_fusion.refs_0_, f32[1]{0:T(128)S(6)} %copy.12.refs_1_.refs_0_, f32[1]{0:T(128)S(6)} %copy.13.refs_2_, ...), custom_call_target="tpu_custom_call" | custom-call | flops 300000000 | bytes 2097152 | tf_op jit(solution)/shard_map/pallas_call | solution.py:63
  46.7 5.7 %collective-permute-start.11 = (bf16[8,16,1152]{2,1,0:T(8,128)(2,1)}, bf16[8,16,1152]{2,1,0:T(8,128)(2,1)S(1)}, u32[]{:S(2)}, u32[]{:S(2)}) collective-permute-start(bf16[8,16,1152]{2,1,0:T(8,128)(2,1)} %get-tuple-element.49), channel_id=1, source_target_pairs={{0,8},{8,0},{16,24},{24,16},{32,40},{40,32},{48,56},{56,48},{64,72... | collective-permute-start | bytes 884744 | tf_op jit(solution)/shard_map/ppermute | solution.py:28
  52.4 3.4 %all-to-all-start.2 = ((bf16[8,16,1152]{2,1,0:T(8,128)(2,1)}), bf16[8,16,1152]{2,1,0:T(8,128)(2,1)S(1)}, u32[]{:S(2)}, u32[]{:S(2)}) async-start(bf16[8,16,1152]{2,1,0:T(8,128)(2,1)} %get-tuple-element.44), calls=%async_computation.2 | async-start | bytes 589824 | tf_op jit(solution)/shard_map/all_to_all | solution.py:326
  59.7 5.1 %all-to-all-done.2.refs_0_ = bf16[8,16,1152]{2,1,0:T(8,128)(2,1)S(1)} async-done(((bf16[8,16,1152]{2,1,0:T(8,128)(2,1)}), bf16[8,16,1152]{2,1,0:T(8,128)(2,1)S(1)}, u32[]{:S(2)}, u32[]{:S(2)}) %all-to-all-start.2) | async-done | bytes 294944 | tf_op jit(solution)/shard_map/all_to_all | solution.py:326
  66.6 3.4 %all-to-all-start.3 = ((bf16[8,16,1152]{2,1,0:T(8,128)(2,1)}), bf16[8,16,1152]{2,1,0:T(8,128)(2,1)S(1)}, u32[]{:S(2)}, u32[]{:S(2)}) async-start(bf16[8,16,1152]{2,1,0:T(8,128)(2,1)} %get-tuple-element.51), calls=%async_computation.3 | async-start | bytes 589824 | tf_op jit(solution)/shard_map/all_to_all | solution.py:326
  73.9 3.9 %all-to-all-done.3.refs_1_ = bf16[8,16,1152]{2,1,0:T(8,128)(2,1)S(1)} async-done(((bf16[8,16,1152]{2,1,0:T(8,128)(2,1)}), bf16[8,16,1152]{2,1,0:T(8,128)(2,1)S(1)}, u32[]{:S(2)}, u32[]{:S(2)}) %all-to-all-start.3) | async-done | bytes 294944 | tf_op jit(solution)/shard_map/all_to_all | solution.py:326
  77.8 3.2 %shard_map.117 = (bf16[128,538]{1,0:T(8,128)(2,1)S(1)}, bf16[320,128]{1,0:T(8,128)(2,1)}, bf16[960,128]{1,0:T(8,128)(2,1)}, bf16[960,128]{1,0:T(8,128)(2,1)}, bf16[960,128]{1,0:T(8,128)(2,1)}) custom-call(s32[3]{0:T(128)S(1)} %pad_add_fusion.refs_0_, bf16[8,16,1152]{2,1,0:T(8,128)(2,1)S(1)} %all-to-all-done.3.refs_1_, bf16[538,1152]{1,0:T(8,128)(2,1)} %refs_2_.3, ...), custom_call_target="tpu_custom_call" | custom-call | flops 360000000 | bytes 4194304 | tf_op jit(solution)/shard_map/pallas_call | solution.py:63
  84.1 6.0 %all-to-all-start.4 = ((bf16[8,16,1152]{2,1,0:T(8,128)(2,1)}), bf16[8,16,1152]{2,1,0:T(8,128)(2,1)S(1)}, u32[]{:S(2)}, u32[]{:S(2)}) async-start(bf16[8,16,1152]{2,1,0:T(8,128)(2,1)} %get-tuple-element.58), calls=%async_computation.4 | async-start | bytes 589824 | tf_op jit(solution)/shard_map/all_to_all | solution.py:326
  103.3 2.2 %collective-permute-done.27.refs_9_ = bf16[960,128]{1,0:T(8,128)(2,1)S(1)} collective-permute-done((bf16[960,128]{1,0:T(8,128)(2,1)S(1)}, bf16[960,128]{1,0:T(8,128)(2,1)S(1)}, u32[]{:S(2)}, u32[]{:S(2)}) %collective-permute-start.27) | collective-permute-done | bytes 245792 | tf_op jit(solution)/shard_map/ppermute | solution.py:28
  105.6 2.8 %shard_map.121 = bf16[8,40,1152]{2,1,0:T(8,128)(2,1)} custom-call(bf16[320,128]{1,0:T(8,128)(2,1)} %get-tuple-element.60.refs_0_, bf16[960,128]{1,0:T(8,128)(2,1)} %get-tuple-element.41.refs_7_.refs_1_, bf16[960,128]{1,0:T(8,128)(2,1)S(1)} %copy-done.7, bf16[1280,128]{1,0:T(8,128)(2,1)S(1)} %copy-done.3, bf16[1280,128]{1,0:T(8,128)(2,1)S(1)} %copy-done.5, ...), custom_call_target="tpu_custom_call" | custom-call | flops 320000000 | bytes 3145728 | tf_op jit(solution)/shard_map/pallas_call | solution.py:63
  108.5 3.7 %all-to-all-start.5 = ((bf16[8,40,1152]{2,1,0:T(8,128)(2,1)}), bf16[8,40,1152]{2,1,0:T(8,128)(2,1)S(1)}, u32[]{:S(2)}, u32[]{:S(2)}) async-start(bf16[8,40,1152]{2,1,0:T(8,128)(2,1)} %shard_map.121), calls=%async_computation.5 | async-start | bytes 1474560 | tf_op jit(solution)/shard_map/all_to_all | solution.py:425
  112.2 3.6 %collective-permute-start.18 = (bf16[16,1152]{1,0:T(8,128)(2,1)S(1)}, bf16[16,1152]{1,0:T(8,128)(2,1)S(1)}, u32[]{:S(2)}, u32[]{:S(2)}) collective-permute-start(bf16[16,1152]{1,0:T(8,128)(2,1)S(1)} %copy-done.8), channel_id=1, source_target_pairs={{0,1},{1,0},{2,3},{3,2},{4,5},{5,4},{6,7},{7,6},{8,9},{9,8},{10,11... | collective-permute-start | bytes 110600 | tf_op jit(solution)/shard_map/ppermute | solution.py:28
  117.0 2.4 %collective-permute-start.20 = (bf16[16,1152]{1,0:T(8,128)(2,1)S(1)}, bf16[16,1152]{1,0:T(8,128)(2,1)S(1)}, u32[]{:S(2)}, u32[]{:S(2)}) collective-permute-start(bf16[16,1152]{1,0:T(8,128)(2,1)S(1)} %copy-done.8), channel_id=1, source_target_pairs={{0,4},{1,5},{2,6},{3,7},{4,0},{5,1},{6,2},{7,3},{8,12},{9,13},{10,... | collective-permute-start | bytes 110600 | tf_op jit(solution)/shard_map/ppermute | solution.py:28
  119.7 3.6 %collective-permute-start.23 = (bf16[16,1152]{1,0:T(8,128)(2,1)S(1)}, bf16[16,1152]{1,0:T(8,128)(2,1)S(1)}, u32[]{:S(2)}, u32[]{:S(2)}) collective-permute-start(bf16[16,1152]{1,0:T(8,128)(2,1)S(1)} %collective-permute-done.18.refs_2_), channel_id=1, source_target_pairs={{0,4},{1,5},{2,6},{3,7},{4,0},{5,1},{6,2},{7,3},{8,12},{9,13},{10,... | collective-permute-start | bytes 110600 | tf_op jit(solution)/shard_map/ppermute | solution.py:28
  125.3 2.5 %collective-permute-done.24.refs_8_ = bf16[16,1152]{1,0:T(8,128)(2,1)S(1)} collective-permute-done((bf16[16,1152]{1,0:T(8,128)(2,1)S(1)}, bf16[16,1152]{1,0:T(8,128)(2,1)S(1)}, u32[]{:S(2)}, u32[]{:S(2)}) %collective-permute-start.24) | collective-permute-done | bytes 36896 | tf_op jit(solution)/shard_map/ppermute | solution.py:28
  129.2 5.4 %all-to-all-done.5.refs_0_ = bf16[8,40,1152]{2,1,0:T(8,128)(2,1)S(1)} async-done(((bf16[8,40,1152]{2,1,0:T(8,128)(2,1)}), bf16[8,40,1152]{2,1,0:T(8,128)(2,1)S(1)}, u32[]{:S(2)}, u32[]{:S(2)}) %all-to-all-start.5) | async-done | bytes 737312 | tf_op jit(solution)/shard_map/all_to_all | solution.py:425
  (109 shorter events, 38.2 us)
Async XLA Ops:
  4.8 20.7 %all-to-all-start = ((bf16[8,16,1152]{2,1,0:T(8,128)(2,1)}), bf16[8,16,1152]{2,1,0:T(8,128)(2,1)S(1)}, u32[]{:S(2)}, u32[]{:S(2)}) async-start(bf16[8,16,1152]{2,1,0:T(8,128)(2,1)} %get-tuple-element.38.refs_3_), calls=%async_computation | async-start | bytes 589824 | tf_op jit(solution)/shard_map/all_to_all | solution.py:326
  12.4 10.7 %collective-permute-start = (bf16[16,1152]{1,0:T(8,128)(2,1)S(1)}, bf16[16,1152]{1,0:T(8,128)(2,1)S(1)}, u32[]{:S(2)}, u32[]{:S(2)}) collective-permute-start(bf16[16,1152]{1,0:T(8,128)(2,1)S(1)} %copy-done.9), channel_id=1, source_target_pairs={{0,32},{8,40},{16,48},{24,56},{32,0},{40,8},{48,16},{56,24},{64,96... | collective-permute-start | bytes 110600 | tf_op jit(solution)/shard_map/ppermute | solution.py:28
  15.5 7.7 %collective-permute-start.1 = (bf16[16,1152]{1,0:T(8,128)(2,1)S(1)}, bf16[16,1152]{1,0:T(8,128)(2,1)S(1)}, u32[]{:S(2)}, u32[]{:S(2)}) collective-permute-start(bf16[16,1152]{1,0:T(8,128)(2,1)S(1)} %copy-done.9), channel_id=1, source_target_pairs={{0,64},{8,72},{16,80},{24,88},{32,96},{40,104},{48,112},{56,120},{... | collective-permute-start | bytes 110600 | tf_op jit(solution)/shard_map/ppermute | solution.py:28
  27.1 13.4 %collective-permute-start.3 = (bf16[4,16,1152]{2,1,0:T(8,128)(2,1)}, bf16[4,16,1152]{2,1,0:T(8,128)(2,1)S(1)}, u32[]{:S(2)}, u32[]{:S(2)}) collective-permute-start(bf16[4,16,1152]{2,1,0:T(8,128)(2,1)} %get-tuple-element.43.refs_4_), channel_id=1, source_target_pairs={{0,16},{8,24},{16,0},{24,8},{32,48},{40,56},{48,32},{56,40},{64,80... | collective-permute-start | bytes 442376 | tf_op jit(solution)/shard_map/ppermute | solution.py:28
  27.9 12.6 %collective-permute-start.4 = (bf16[4,16,1152]{2,1,0:T(8,128)(2,1)}, bf16[4,16,1152]{2,1,0:T(8,128)(2,1)S(1)}, u32[]{:S(2)}, u32[]{:S(2)}) collective-permute-start(bf16[4,16,1152]{2,1,0:T(8,128)(2,1)} %get-tuple-element.43.refs_4_), channel_id=1, source_target_pairs={{0,128},{8,136},{16,144},{24,152},{32,160},{40,168},{48,176},{56,1... | collective-permute-start | bytes 442376 | tf_op jit(solution)/shard_map/ppermute | solution.py:28
  28.2 12.7 %collective-permute-start.5 = (bf16[4,16,1152]{2,1,0:T(8,128)(2,1)}, bf16[4,16,1152]{2,1,0:T(8,128)(2,1)S(1)}, u32[]{:S(2)}, u32[]{:S(2)}) collective-permute-start(bf16[4,16,1152]{2,1,0:T(8,128)(2,1)} %get-tuple-element.43.refs_4_), channel_id=1, source_target_pairs={{0,144},{8,152},{16,128},{24,136},{32,176},{40,184},{48,160},{56,1... | collective-permute-start | bytes 442376 | tf_op jit(solution)/shard_map/ppermute | solution.py:28
  29.8 14.4 %all-to-all-start.1 = ((bf16[8,16,1152]{2,1,0:T(8,128)(2,1)}), bf16[8,16,1152]{2,1,0:T(8,128)(2,1)S(1)}, u32[]{:S(2)}, u32[]{:S(2)}) async-start(bf16[8,16,1152]{2,1,0:T(8,128)(2,1)} %get-tuple-element.42), calls=%async_computation.1 | async-start | bytes 589824 | tf_op jit(solution)/shard_map/all_to_all | solution.py:326
  41.0 15.0 %collective-permute-start.12 = (bf16[1280,128]{1,0:T(8,128)(2,1)S(1)}, bf16[1280,128]{1,0:T(8,128)(2,1)S(1)}, u32[]{:S(2)}, u32[]{:S(2)}) collective-permute-start(bf16[1280,128]{1,0:T(8,128)(2,1)S(1)} %copy-done.20), channel_id=1, source_target_pairs={{0,128},{8,136},{16,144},{24,152},{32,160},{40,168},{48,176},{56,1... | collective-permute-start | bytes 983048 | tf_op jit(solution)/shard_map/ppermute | solution.py:28
  46.7 10.7 %collective-permute-start.11 = (bf16[8,16,1152]{2,1,0:T(8,128)(2,1)}, bf16[8,16,1152]{2,1,0:T(8,128)(2,1)S(1)}, u32[]{:S(2)}, u32[]{:S(2)}) collective-permute-start(bf16[8,16,1152]{2,1,0:T(8,128)(2,1)} %get-tuple-element.49), channel_id=1, source_target_pairs={{0,8},{8,0},{16,24},{24,16},{32,40},{40,32},{48,56},{56,48},{64,72... | collective-permute-start | bytes 884744 | tf_op jit(solution)/shard_map/ppermute | solution.py:28
  52.4 12.3 %all-to-all-start.2 = ((bf16[8,16,1152]{2,1,0:T(8,128)(2,1)}), bf16[8,16,1152]{2,1,0:T(8,128)(2,1)S(1)}, u32[]{:S(2)}, u32[]{:S(2)}) async-start(bf16[8,16,1152]{2,1,0:T(8,128)(2,1)} %get-tuple-element.44), calls=%async_computation.2 | async-start | bytes 589824 | tf_op jit(solution)/shard_map/all_to_all | solution.py:326
  56.0 25.0 %collective-permute-start.17 = (bf16[1280,128]{1,0:T(8,128)(2,1)S(1)}, bf16[1280,128]{1,0:T(8,128)(2,1)S(1)}, u32[]{:S(2)}, u32[]{:S(2)}) collective-permute-start(bf16[1280,128]{1,0:T(8,128)(2,1)S(1)} %collective-permute-done.12.refs_4_.refs_3_), channel_id=1, source_target_pairs={{0,8},{8,0},{16,24},{24,16},{32,40},{40,32},{48,56},{56,48},{64,72... | collective-permute-start | bytes 983048 | tf_op jit(solution)/shard_map/ppermute | solution.py:28
  66.6 11.2 %all-to-all-start.3 = ((bf16[8,16,1152]{2,1,0:T(8,128)(2,1)}), bf16[8,16,1152]{2,1,0:T(8,128)(2,1)S(1)}, u32[]{:S(2)}, u32[]{:S(2)}) async-start(bf16[8,16,1152]{2,1,0:T(8,128)(2,1)} %get-tuple-element.51), calls=%async_computation.3 | async-start | bytes 589824 | tf_op jit(solution)/shard_map/all_to_all | solution.py:326
  70.0 11.0 %collective-permute-start.16 = (bf16[960,128]{1,0:T(8,128)(2,1)}, bf16[960,128]{1,0:T(8,128)(2,1)S(1)}, u32[]{:S(2)}, u32[]{:S(2)}) collective-permute-start(bf16[960,128]{1,0:T(8,128)(2,1)} %get-tuple-element.41.refs_7_.refs_1_), channel_id=1, source_target_pairs={{0,8},{8,0},{16,24},{24,16},{32,40},{40,32},{48,56},{56,48},{64,72... | collective-permute-start | bytes 737288 | tf_op jit(solution)/shard_map/ppermute | solution.py:28
  71.2 9.8 %collective-permute-start.13 = (bf16[64,1152]{1,0:T(8,128)(2,1)}, bf16[64,1152]{1,0:T(8,128)(2,1)S(1)}, u32[]{:S(2)}, u32[]{:S(2)}) collective-permute-start(bf16[64,1152]{1,0:T(8,128)(2,1)} %get-tuple-element.55), channel_id=1, source_target_pairs={{0,16},{8,24},{16,0},{24,8},{32,48},{40,56},{48,32},{56,40},{64,80... | collective-permute-start | bytes 442376 | tf_op jit(solution)/shard_map/ppermute | solution.py:28
  72.0 9.1 %collective-permute-start.14 = (bf16[64,1152]{1,0:T(8,128)(2,1)}, bf16[64,1152]{1,0:T(8,128)(2,1)S(1)}, u32[]{:S(2)}, u32[]{:S(2)}) collective-permute-start(bf16[64,1152]{1,0:T(8,128)(2,1)} %get-tuple-element.56), channel_id=1, source_target_pairs={{0,128},{8,136},{16,144},{24,152},{32,160},{40,168},{48,176},{56,1... | collective-permute-start | bytes 442376 | tf_op jit(solution)/shard_map/ppermute | solution.py:28
  72.7 8.4 %collective-permute-start.15 = (bf16[64,1152]{1,0:T(8,128)(2,1)S(1)}, bf16[64,1152]{1,0:T(8,128)(2,1)S(1)}, u32[]{:S(2)}, u32[]{:S(2)}) collective-permute-start(bf16[64,1152]{1,0:T(8,128)(2,1)S(1)} %copy-done.22), channel_id=1, source_target_pairs={{0,144},{8,152},{16,128},{24,136},{32,176},{40,184},{48,160},{56,1... | collective-permute-start | bytes 442376 | tf_op jit(solution)/shard_map/ppermute | solution.py:28
  84.1 15.4 %all-to-all-start.4 = ((bf16[8,16,1152]{2,1,0:T(8,128)(2,1)}), bf16[8,16,1152]{2,1,0:T(8,128)(2,1)S(1)}, u32[]{:S(2)}, u32[]{:S(2)}) async-start(bf16[8,16,1152]{2,1,0:T(8,128)(2,1)} %get-tuple-element.58), calls=%async_computation.4 | async-start | bytes 589824 | tf_op jit(solution)/shard_map/all_to_all | solution.py:326
  90.0 13.3 %collective-permute-start.25 = (bf16[960,128]{1,0:T(8,128)(2,1)S(1)}, bf16[960,128]{1,0:T(8,128)(2,1)S(1)}, u32[]{:S(2)}, u32[]{:S(2)}) collective-permute-start(bf16[960,128]{1,0:T(8,128)(2,1)S(1)} %copy-done.19), channel_id=1, source_target_pairs={{0,8},{8,0},{16,24},{24,16},{32,40},{40,32},{48,56},{56,48},{64,72... | collective-permute-start | bytes 737288 | tf_op jit(solution)/shard_map/ppermute | solution.py:28
  92.0 11.3 %collective-permute-start.26 = (bf16[960,128]{1,0:T(8,128)(2,1)}, bf16[960,128]{1,0:T(8,128)(2,1)S(1)}, u32[]{:S(2)}, u32[]{:S(2)}) collective-permute-start(bf16[960,128]{1,0:T(8,128)(2,1)} %get-tuple-element.63), channel_id=1, source_target_pairs={{0,128},{8,136},{16,144},{24,152},{32,160},{40,168},{48,176},{56,1... | collective-permute-start | bytes 737288 | tf_op jit(solution)/shard_map/ppermute | solution.py:28
  92.0 13.5 %collective-permute-start.27 = (bf16[960,128]{1,0:T(8,128)(2,1)S(1)}, bf16[960,128]{1,0:T(8,128)(2,1)S(1)}, u32[]{:S(2)}, u32[]{:S(2)}) collective-permute-start(bf16[960,128]{1,0:T(8,128)(2,1)S(1)} %copy-done.21), channel_id=1, source_target_pairs={{0,136},{8,128},{16,152},{24,144},{32,168},{40,160},{48,184},{56,1... | collective-permute-start | bytes 737288 | tf_op jit(solution)/shard_map/ppermute | solution.py:28
  95.0 7.0 %collective-permute-start.29 = (bf16[16,1152]{1,0:T(8,128)(2,1)}, bf16[16,1152]{1,0:T(8,128)(2,1)S(1)}, u32[]{:S(2)}, u32[]{:S(2)}) collective-permute-start(bf16[16,1152]{1,0:T(8,128)(2,1)} %get-tuple-element.66), channel_id=1, source_target_pairs={{0,64},{8,72},{16,80},{24,88},{32,96},{40,104},{48,112},{56,120},{... | collective-permute-start | bytes 110600 | tf_op jit(solution)/shard_map/ppermute | solution.py:28
  108.5 26.1 %all-to-all-start.5 = ((bf16[8,40,1152]{2,1,0:T(8,128)(2,1)}), bf16[8,40,1152]{2,1,0:T(8,128)(2,1)S(1)}, u32[]{:S(2)}, u32[]{:S(2)}) async-start(bf16[8,40,1152]{2,1,0:T(8,128)(2,1)} %shard_map.121), calls=%async_computation.5 | async-start | bytes 1474560 | tf_op jit(solution)/shard_map/all_to_all | solution.py:425
  112.2 7.5 %collective-permute-start.18 = (bf16[16,1152]{1,0:T(8,128)(2,1)S(1)}, bf16[16,1152]{1,0:T(8,128)(2,1)S(1)}, u32[]{:S(2)}, u32[]{:S(2)}) collective-permute-start(bf16[16,1152]{1,0:T(8,128)(2,1)S(1)} %copy-done.8), channel_id=1, source_target_pairs={{0,1},{1,0},{2,3},{3,2},{4,5},{5,4},{6,7},{7,6},{8,9},{9,8},{10,11... | collective-permute-start | bytes 110600 | tf_op jit(solution)/shard_map/ppermute | solution.py:28
  115.8 7.4 %collective-permute-start.19 = (bf16[16,1152]{1,0:T(8,128)(2,1)S(1)}, bf16[16,1152]{1,0:T(8,128)(2,1)S(1)}, u32[]{:S(2)}, u32[]{:S(2)}) collective-permute-start(bf16[16,1152]{1,0:T(8,128)(2,1)S(1)} %copy-done.8), channel_id=1, source_target_pairs={{0,2},{1,3},{2,0},{3,1},{4,6},{5,7},{6,4},{7,5},{8,10},{9,11},{10,... | collective-permute-start | bytes 110600 | tf_op jit(solution)/shard_map/ppermute | solution.py:28
  (36 other events, 396.4 us)

commit v3 on v2

--- a/solution.py
+++ b/solution.py
@@ -36,14 +36,15 @@
     return pltpu.with_memory_space_constraint(x, pltpu.HBM)
 
 
-def call(body, outs, args, scratch=(), smem=(), after=(), hbm=(), flops=0, size=1 << 20):
+def call(body, outs, args, scratch=(), smem=(), after=(), beside=(), hbm=(), flops=0, size=1 << 20):
     single = not isinstance(outs, (tuple, list))
     outs = (outs,) if single else tuple(outs)
     vm = pl.BlockSpec(memory_space=pltpu.VMEM)
     sm = pl.BlockSpec(memory_space=pltpu.SMEM)
     some = pl.BlockSpec(memory_space=pl.ANY)
     far = pl.BlockSpec(memory_space=pltpu.HBM)
-    n_in, n_after, n_out, n_far = len(args), len(after), len(outs), len(hbm)
+    order = [hold(x) for x in after] + list(beside)
+    n_in, n_after, n_out, n_far = len(args), len(order), len(outs), len(hbm)
 
     def kernel(*refs):
         ins = refs[:n_in]
@@ -72,7 +73,7 @@
         + list(scratch),
         compiler_params=pltpu.CompilerParams(vmem_limit_bytes=24 << 20),
         cost_estimate=pl.CostEstimate(flops=flops, bytes_accessed=size, transcendentals=0),
-    )(*args, *[hold(x) for x in after])
+    )(*args, *order)
     return got[0] if single else got
 
 
@@ -117,11 +118,11 @@
     hidden_b = (pre * cdf).astype(BF)
     v_hidden[...] = hidden_b
     put_hidden = move(v_hidden, hidden, 4)
+    v_slope[...] = cdf + 0.5 * pre * (1.0 - th * th) * (ROOT * (1.0 + 0.134145 * square))
+    put_slope = move(v_slope, slope, 6)
     get_out.wait()
     v_part[...] = dot(hidden_b, v_out[...]).astype(BF).reshape(NT, ROWS, D)
     put_part = move(v_part, part, 5)
-    v_slope[...] = cdf + 0.5 * pre * (1.0 - th * th) * (ROOT * (1.0 + 0.134145 * square))
-    put_slope = move(v_slope, slope, 6)
     for copy in (put_normed, put_hidden, put_part, put_slope):
         copy.wait()
 
@@ -378,7 +379,7 @@
     de_rows, spread = call(
         embed_grad_body,
         (block, blocks),
-        (tensor_all(du), hold(unit), hold(enorm)),
+        (tensor_all(du), unit, enorm),
         hbm=(0, 1),
         after=(keep,),
     )
@@ -391,7 +392,7 @@
         (rank, de, hold(w_out), hold(slope)),
         smem=(0,),
         hbm=(1, 2, 3, 4),
-        after=(n_x,),
+        beside=(n_x,),
         flops=2 * 180_000_000,
         size=4 << 20,
     )
@@ -401,9 +402,9 @@
     dn, rest, *sent = call(
         dn_body,
         (blocks, sds((ROWS, D), F32), block, block, block),
-        (dpre, w_in, hold(keep), *got),
+        (dpre, w_in, keep, *got),
         hbm=(0, 1, 2, 3, 4),
-        after=(n_core, n_xc),
+        beside=(n_core, n_xc),
         flops=2 * 80_000_000,
         size=2 << 20,
     )
@@ -415,10 +416,11 @@
     payload = call(
         weights_body,
         sds((8, 40, D), BF),
-        (hold(n_mine), hold(n_own), n_core, n_x, n_xc)
+        (n_mine, n_own, n_core, n_x, n_xc)
         + (hold(e_mine), hold(e_own), e_core, e_x, e_xc),
         hbm=(0,),
-        after=(rows, *got),
+        after=(rows,),
+        beside=got,
         flops=2 * 160_000_000,
         size=3 << 20,
     )

time: 137 us -> 136 us (level)
  no operation moved by 1% of the time
where the time goes in v3:
time: 136 us; the launch traced here: 134 us
  starting transfers between devices  77 us (57%)
  waiting for transfers between devices  29.6 us (22%)
  Pallas kernels  25.4 us (19%)
  between operations  2.27 us (2%)
    ppermute x31, starting transfers between devices, swap(): return lax.ppermute(x, axis, [(i, i ^ mask) for i in range(n)])  45.2 us
    all_to_all x5, starting transfers between devices, tensor_all(): return lax.all_to_all(x, 'tensor', 0, 0, tiled=True)  28.1 us
    pallas_call x11, Pallas kernels, call(): pl.pallas_call(kernel, out_shape=tuple((pltpu.HBM(o.shape, o.dtype) if i...  21.4 us
    ppermute x31, waiting for transfers between devices, swap(): return lax.ppermute(x, axis, [(i, i ^ mask) for i in range(n)])  13.6 us
    all_to_all x5, waiting for transfers between devices, tensor_all(): return lax.all_to_all(x, 'tensor', 0, 0, tiled=True)  10.5 us
    all_to_all x1, waiting for transfers between devices, local(): lax.all_to_all(payload, 'dp', 0, 0, tiled=True, axis_index_groups=groups)  5.52 us
    pallas_call x1, Pallas kernels, forward(): pl.pallas_call(forward_body, out_shape=tuple((pltpu.HBM(*shape) for shape...  4.05 us
    all_to_all x1, starting transfers between devices, local(): lax.all_to_all(payload, 'dp', 0, 0, tiled=True, axis_index_groups=groups)  3.69 us
  transfers between devices with their start and end apart: 37, of which 13 were waited for; matrix products, arithmetic and copies ran while one was open for 0% of the time, Pallas kernels for 11%

profile of v3, /device:TPU:1, one launch (start us, length us, event | category | flops | bytes accessed | tf_op | source)
XLA Modules:
  0.0 134.4 jit_solution(8250255237669194582)
XLA Ops:
  0.6 4.0 %shard_map.111 = (bf16[128,1152]{1,0:T(8,128)(2,1)}, bf16[128,538]{1,0:T(8,128)(2,1)}, f32[128,538]{1,0:T(8,128)}, bf16[8,16,1152]{2,1,0:T(8,128)(2,1)}) custom-call(bf16[128,1152]{1,0:T(8,128)(2,1)} %refs_2_.4, f32[1152]{0:T(1024)} %refs_3_.3, bf16[538,1152]{1,0:T(8,128)(2,1)} %bitcast.5, f32[538]{0:T(1024)} %b_in.1, bf16[538,1152]{1,0:T(8,128)(2,1)} %refs_2_.3), custom_call_target="tpu_custom_call" | custom-call | flops 320000000 | bytes 4194304 | tf_op jit(solution)/shard_map/pallas_call | solution.py:140
  4.7 7.6 %all-to-all-start = ((bf16[8,16,1152]{2,1,0:T(8,128)(2,1)}), bf16[8,16,1152]{2,1,0:T(8,128)(2,1)S(1)}, u32[]{:S(2)}, u32[]{:S(2)}) async-start(bf16[8,16,1152]{2,1,0:T(8,128)(2,1)} %get-tuple-element.38.refs_3_), calls=%async_computation | async-start | bytes 589824 | tf_op jit(solution)/shard_map/all_to_all | solution.py:327
  12.3 3.1 %collective-permute-start = (bf16[16,1152]{1,0:T(8,128)(2,1)S(1)}, bf16[16,1152]{1,0:T(8,128)(2,1)S(1)}, u32[]{:S(2)}, u32[]{:S(2)}) collective-permute-start(bf16[16,1152]{1,0:T(8,128)(2,1)S(1)} %copy-done.5), channel_id=1, source_target_pairs={{0,32},{8,40},{16,48},{24,56},{32,0},{40,8},{48,16},{56,24},{64,96... | collective-permute-start | bytes 110600 | tf_op jit(solution)/shard_map/ppermute | solution.py:28
  15.4 5.1 %collective-permute-start.1 = (bf16[16,1152]{1,0:T(8,128)(2,1)S(1)}, bf16[16,1152]{1,0:T(8,128)(2,1)S(1)}, u32[]{:S(2)}, u32[]{:S(2)}) collective-permute-start(bf16[16,1152]{1,0:T(8,128)(2,1)S(1)} %copy-done.5), channel_id=1, source_target_pairs={{0,64},{8,72},{16,80},{24,88},{32,96},{40,104},{48,112},{56,120},{... | collective-permute-start | bytes 110600 | tf_op jit(solution)/shard_map/ppermute | solution.py:28
  20.6 2.5 %shard_map.112 = (bf16[320,128]{1,0:T(8,128)(2,1)}, bf16[960,128]{1,0:T(8,128)(2,1)}, bf16[1280,128]{1,0:T(8,128)(2,1)}) custom-call(s32[3]{0:T(128)S(1)} %pad_add_fusion.refs_0_, bf16[8,16,1152]{2,1,0:T(8,128)(2,1)} %bitcast.7, bf16[128,538]{1,0:T(8,128)(2,1)} %get-tuple-element.40.refs_2_, bf16[8,16,1152]{2,1,0:T(8,128)(2,1)} %get-tuple-element.38.refs_3_), custom_call_target="tpu_custom_call" | custom-call | flops 200000000 | bytes 2097152 | tf_op jit(solution)/shard_map/pallas_call | solution.py:64
  23.1 2.4 %collective-permute-done.2.refs_6_ = bf16[16,1152]{1,0:T(8,128)(2,1)S(1)} collective-permute-done((bf16[16,1152]{1,0:T(8,128)(2,1)S(1)}, bf16[16,1152]{1,0:T(8,128)(2,1)S(1)}, u32[]{:S(2)}, u32[]{:S(2)}) %collective-permute-start.2) | collective-permute-done | bytes 36896 | tf_op jit(solution)/shard_map/ppermute | solution.py:28
  29.7 6.6 %all-to-all-start.1 = ((bf16[8,16,1152]{2,1,0:T(8,128)(2,1)}), bf16[8,16,1152]{2,1,0:T(8,128)(2,1)S(1)}, u32[]{:S(2)}, u32[]{:S(2)}) async-start(bf16[8,16,1152]{2,1,0:T(8,128)(2,1)} %get-tuple-element.42), calls=%async_computation.1 | async-start | bytes 589824 | tf_op jit(solution)/shard_map/all_to_all | solution.py:327
  36.3 4.1 %collective-permute-start.6 = (bf16[4,16,1152]{2,1,0:T(8,128)(2,1)}, bf16[4,16,1152]{2,1,0:T(8,128)(2,1)S(1)}, u32[]{:S(2)}, u32[]{:S(2)}) collective-permute-start(bf16[4,16,1152]{2,1,0:T(8,128)(2,1)} %get-tuple-element.43.refs_4_), channel_id=1, source_target_pairs={{0,8},{8,0},{16,24},{24,16},{32,40},{40,32},{48,56},{56,48},{64,72... | collective-permute-start | bytes 442376 | tf_op jit(solution)/shard_map/ppermute | solution.py:28
  44.1 2.6 %shard_map.114 = (bf16[8,16,1152]{2,1,0:T(8,128)(2,1)}, bf16[128,256]{1,0:T(8,128)(2,1)}, bf16[128,256]{1,0:T(8,128)(2,1)}, bf16[8,16,1152]{2,1,0:T(8,128)(2,1)}) custom-call(s32[3]{0:T(128)S(1)} %pad_add_fusion.refs_0_, f32[1]{0:T(128)S(6)} %copy.12.refs_1_.refs_0_, f32[1]{0:T(128)S(6)} %copy.13.refs_2_, ...), custom_call_target="tpu_custom_call" | custom-call | flops 300000000 | bytes 2097152 | tf_op jit(solution)/shard_map/pallas_call | solution.py:64
  46.7 5.7 %collective-permute-start.11 = (bf16[8,16,1152]{2,1,0:T(8,128)(2,1)}, bf16[8,16,1152]{2,1,0:T(8,128)(2,1)S(1)}, u32[]{:S(2)}, u32[]{:S(2)}) collective-permute-start(bf16[8,16,1152]{2,1,0:T(8,128)(2,1)} %get-tuple-element.49), channel_id=1, source_target_pairs={{0,8},{8,0},{16,24},{24,16},{32,40},{40,32},{48,56},{56,48},{64,72... | collective-permute-start | bytes 884744 | tf_op jit(solution)/shard_map/ppermute | solution.py:28
  52.4 3.6 %all-to-all-start.2 = ((bf16[8,16,1152]{2,1,0:T(8,128)(2,1)}), bf16[8,16,1152]{2,1,0:T(8,128)(2,1)S(1)}, u32[]{:S(2)}, u32[]{:S(2)}) async-start(bf16[8,16,1152]{2,1,0:T(8,128)(2,1)} %get-tuple-element.44), calls=%async_computation.2 | async-start | bytes 589824 | tf_op jit(solution)/shard_map/all_to_all | solution.py:327
  59.7 5.1 %all-to-all-done.2.refs_0_ = bf16[8,16,1152]{2,1,0:T(8,128)(2,1)S(1)} async-done(((bf16[8,16,1152]{2,1,0:T(8,128)(2,1)}), bf16[8,16,1152]{2,1,0:T(8,128)(2,1)S(1)}, u32[]{:S(2)}, u32[]{:S(2)}) %all-to-all-start.2) | async-done | bytes 294944 | tf_op jit(solution)/shard_map/all_to_all | solution.py:327
  65.7 3.4 %all-to-all-start.3 = ((bf16[8,16,1152]{2,1,0:T(8,128)(2,1)}), bf16[8,16,1152]{2,1,0:T(8,128)(2,1)S(1)}, u32[]{:S(2)}, u32[]{:S(2)}) async-start(bf16[8,16,1152]{2,1,0:T(8,128)(2,1)} %get-tuple-element.51), calls=%async_computation.3 | async-start | bytes 589824 | tf_op jit(solution)/shard_map/all_to_all | solution.py:327
  73.0 3.9 %all-to-all-done.3.refs_1_ = bf16[8,16,1152]{2,1,0:T(8,128)(2,1)S(1)} async-done(((bf16[8,16,1152]{2,1,0:T(8,128)(2,1)}), bf16[8,16,1152]{2,1,0:T(8,128)(2,1)S(1)}, u32[]{:S(2)}, u32[]{:S(2)}) %all-to-all-start.3) | async-done | bytes 294944 | tf_op jit(solution)/shard_map/all_to_all | solution.py:327
  76.9 3.2 %shard_map.117 = (bf16[128,538]{1,0:T(8,128)(2,1)S(1)}, bf16[320,128]{1,0:T(8,128)(2,1)}, bf16[960,128]{1,0:T(8,128)(2,1)}, bf16[960,128]{1,0:T(8,128)(2,1)}, bf16[960,128]{1,0:T(8,128)(2,1)}) custom-call(s32[3]{0:T(128)S(1)} %pad_add_fusion.refs_0_, bf16[8,16,1152]{2,1,0:T(8,128)(2,1)S(1)} %all-to-all-done.3.refs_1_, bf16[538,1152]{1,0:T(8,128)(2,1)} %refs_2_.3, ...), custom_call_target="tpu_custom_call" | custom-call | flops 360000000 | bytes 4194304 | tf_op jit(solution)/shard_map/pallas_call | solution.py:64
  82.4 6.9 %all-to-all-start.4 = ((bf16[8,16,1152]{2,1,0:T(8,128)(2,1)}), bf16[8,16,1152]{2,1,0:T(8,128)(2,1)S(1)}, u32[]{:S(2)}, u32[]{:S(2)}) async-start(bf16[8,16,1152]{2,1,0:T(8,128)(2,1)} %get-tuple-element.58), calls=%async_computation.4 | async-start | bytes 589824 | tf_op jit(solution)/shard_map/all_to_all | solution.py:327
  102.3 2.4 %collective-permute-done.27.refs_9_ = bf16[960,128]{1,0:T(8,128)(2,1)S(1)} collective-permute-done((bf16[960,128]{1,0:T(8,128)(2,1)}, bf16[960,128]{1,0:T(8,128)(2,1)S(1)}, u32[]{:S(2)}, u32[]{:S(2)}) %collective-permute-start.27) | collective-permute-done | bytes 245792 | tf_op jit(solution)/shard_map/ppermute | solution.py:28
  104.7 2.7 %shard_map.121 = bf16[8,40,1152]{2,1,0:T(8,128)(2,1)} custom-call(bf16[320,128]{1,0:T(8,128)(2,1)S(1)} %copy-done.6, bf16[960,128]{1,0:T(8,128)(2,1)S(1)} %copy-done.3, bf16[960,128]{1,0:T(8,128)(2,1)S(1)} %collective-permute-done.16.refs_6_.refs_2_, bf16[1280,128]{1,0:T(8,128)(2,1)S(1)} %collective-permute-done.12.refs_4_.refs_3_, ...), custom_call_target="tpu_custom_call" | custom-call | flops 320000000 | bytes 3145728 | tf_op jit(solution)/shard_map/pallas_call | solution.py:64
  107.4 3.7 %all-to-all-start.5 = ((bf16[8,40,1152]{2,1,0:T(8,128)(2,1)}), bf16[8,40,1152]{2,1,0:T(8,128)(2,1)S(1)}, u32[]{:S(2)}, u32[]{:S(2)}) async-start(bf16[8,40,1152]{2,1,0:T(8,128)(2,1)} %shard_map.121), calls=%async_computation.5 | async-start | bytes 1474560 | tf_op jit(solution)/shard_map/all_to_all | solution.py:427
  111.1 3.8 %collective-permute-start.18 = (bf16[16,1152]{1,0:T(8,128)(2,1)S(1)}, bf16[16,1152]{1,0:T(8,128)(2,1)S(1)}, u32[]{:S(2)}, u32[]{:S(2)}) collective-permute-start(bf16[16,1152]{1,0:T(8,128)(2,1)S(1)} %copy-done.4), channel_id=1, source_target_pairs={{0,1},{1,0},{2,3},{3,2},{4,5},{5,4},{6,7},{7,6},{8,9},{9,8},{10,11... | collective-permute-start | bytes 110600 | tf_op jit(solution)/shard_map/ppermute | solution.py:28
  116.1 2.4 %collective-permute-start.20 = (bf16[16,1152]{1,0:T(8,128)(2,1)S(1)}, bf16[16,1152]{1,0:T(8,128)(2,1)S(1)}, u32[]{:S(2)}, u32[]{:S(2)}) collective-permute-start(bf16[16,1152]{1,0:T(8,128)(2,1)S(1)} %copy-done.4), channel_id=1, source_target_pairs={{0,4},{1,5},{2,6},{3,7},{4,0},{5,1},{6,2},{7,3},{8,12},{9,13},{10,... | collective-permute-start | bytes 110600 | tf_op jit(solution)/shard_map/ppermute | solution.py:28
  118.7 3.6 %collective-permute-start.23 = (bf16[16,1152]{1,0:T(8,128)(2,1)S(1)}, bf16[16,1152]{1,0:T(8,128)(2,1)S(1)}, u32[]{:S(2)}, u32[]{:S(2)}) collective-permute-start(bf16[16,1152]{1,0:T(8,128)(2,1)S(1)} %collective-permute-done.18.refs_2_), channel_id=1, source_target_pairs={{0,4},{1,5},{2,6},{3,7},{4,0},{5,1},{6,2},{7,3},{8,12},{9,13},{10,... | collective-permute-start | bytes 110600 | tf_op jit(solution)/shard_map/ppermute | solution.py:28
  124.3 2.3 %collective-permute-done.24.refs_8_ = bf16[16,1152]{1,0:T(8,128)(2,1)S(1)} collective-permute-done((bf16[16,1152]{1,0:T(8,128)(2,1)S(1)}, bf16[16,1152]{1,0:T(8,128)(2,1)S(1)}, u32[]{:S(2)}, u32[]{:S(2)}) %collective-permute-start.24) | collective-permute-done | bytes 36896 | tf_op jit(solution)/shard_map/ppermute | solution.py:28
  128.0 5.5 %all-to-all-done.5.refs_0_ = bf16[8,40,1152]{2,1,0:T(8,128)(2,1)S(1)} async-done(((bf16[8,40,1152]{2,1,0:T(8,128)(2,1)}), bf16[8,40,1152]{2,1,0:T(8,128)(2,1)S(1)}, u32[]{:S(2)}, u32[]{:S(2)}) %all-to-all-start.5) | async-done | bytes 737312 | tf_op jit(solution)/shard_map/all_to_all | solution.py:427
  (89 shorter events, 36.2 us)
Async XLA Ops:
  4.7 20.7 %all-to-all-start = ((bf16[8,16,1152]{2,1,0:T(8,128)(2,1)}), bf16[8,16,1152]{2,1,0:T(8,128)(2,1)S(1)}, u32[]{:S(2)}, u32[]{:S(2)}) async-start(bf16[8,16,1152]{2,1,0:T(8,128)(2,1)} %get-tuple-element.38.refs_3_), calls=%async_computation | async-start | bytes 589824 | tf_op jit(solution)/shard_map/all_to_all | solution.py:327
  12.3 10.7 %collective-permute-start = (bf16[16,1152]{1,0:T(8,128)(2,1)S(1)}, bf16[16,1152]{1,0:T(8,128)(2,1)S(1)}, u32[]{:S(2)}, u32[]{:S(2)}) collective-permute-start(bf16[16,1152]{1,0:T(8,128)(2,1)S(1)} %copy-done.5), channel_id=1, source_target_pairs={{0,32},{8,40},{16,48},{24,56},{32,0},{40,8},{48,16},{56,24},{64,96... | collective-permute-start | bytes 110600 | tf_op jit(solution)/shard_map/ppermute | solution.py:28
  15.4 7.7 %collective-permute-start.1 = (bf16[16,1152]{1,0:T(8,128)(2,1)S(1)}, bf16[16,1152]{1,0:T(8,128)(2,1)S(1)}, u32[]{:S(2)}, u32[]{:S(2)}) collective-permute-start(bf16[16,1152]{1,0:T(8,128)(2,1)S(1)} %copy-done.5), channel_id=1, source_target_pairs={{0,64},{8,72},{16,80},{24,88},{32,96},{40,104},{48,112},{56,120},{... | collective-permute-start | bytes 110600 | tf_op jit(solution)/shard_map/ppermute | solution.py:28
  27.0 13.4 %collective-permute-start.3 = (bf16[4,16,1152]{2,1,0:T(8,128)(2,1)}, bf16[4,16,1152]{2,1,0:T(8,128)(2,1)S(1)}, u32[]{:S(2)}, u32[]{:S(2)}) collective-permute-start(bf16[4,16,1152]{2,1,0:T(8,128)(2,1)} %get-tuple-element.43.refs_4_), channel_id=1, source_target_pairs={{0,16},{8,24},{16,0},{24,8},{32,48},{40,56},{48,32},{56,40},{64,80... | collective-permute-start | bytes 442376 | tf_op jit(solution)/shard_map/ppermute | solution.py:28
  27.8 12.6 %collective-permute-start.4 = (bf16[4,16,1152]{2,1,0:T(8,128)(2,1)}, bf16[4,16,1152]{2,1,0:T(8,128)(2,1)S(1)}, u32[]{:S(2)}, u32[]{:S(2)}) collective-permute-start(bf16[4,16,1152]{2,1,0:T(8,128)(2,1)} %get-tuple-element.43.refs_4_), channel_id=1, source_target_pairs={{0,128},{8,136},{16,144},{24,152},{32,160},{40,168},{48,176},{56,1... | collective-permute-start | bytes 442376 | tf_op jit(solution)/shard_map/ppermute | solution.py:28
  28.1 12.7 %collective-permute-start.5 = (bf16[4,16,1152]{2,1,0:T(8,128)(2,1)}, bf16[4,16,1152]{2,1,0:T(8,128)(2,1)S(1)}, u32[]{:S(2)}, u32[]{:S(2)}) collective-permute-start(bf16[4,16,1152]{2,1,0:T(8,128)(2,1)} %get-tuple-element.43.refs_4_), channel_id=1, source_target_pairs={{0,144},{8,152},{16,128},{24,136},{32,176},{40,184},{48,160},{56,1... | collective-permute-start | bytes 442376 | tf_op jit(solution)/shard_map/ppermute | solution.py:28
  29.7 14.4 %all-to-all-start.1 = ((bf16[8,16,1152]{2,1,0:T(8,128)(2,1)}), bf16[8,16,1152]{2,1,0:T(8,128)(2,1)S(1)}, u32[]{:S(2)}, u32[]{:S(2)}) async-start(bf16[8,16,1152]{2,1,0:T(8,128)(2,1)} %get-tuple-element.42), calls=%async_computation.1 | async-start | bytes 589824 | tf_op jit(solution)/shard_map/all_to_all | solution.py:327
  41.0 15.1 %collective-permute-start.12 = (bf16[1280,128]{1,0:T(8,128)(2,1)S(1)}, bf16[1280,128]{1,0:T(8,128)(2,1)S(1)}, u32[]{:S(2)}, u32[]{:S(2)}) collective-permute-start(bf16[1280,128]{1,0:T(8,128)(2,1)S(1)} %copy-done.12), channel_id=1, source_target_pairs={{0,128},{8,136},{16,144},{24,152},{32,160},{40,168},{48,176},{56,1... | collective-permute-start | bytes 983048 | tf_op jit(solution)/shard_map/ppermute | solution.py:28
  46.7 10.8 %collective-permute-start.11 = (bf16[8,16,1152]{2,1,0:T(8,128)(2,1)}, bf16[8,16,1152]{2,1,0:T(8,128)(2,1)S(1)}, u32[]{:S(2)}, u32[]{:S(2)}) collective-permute-start(bf16[8,16,1152]{2,1,0:T(8,128)(2,1)} %get-tuple-element.49), channel_id=1, source_target_pairs={{0,8},{8,0},{16,24},{24,16},{32,40},{40,32},{48,56},{56,48},{64,72... | collective-permute-start | bytes 884744 | tf_op jit(solution)/shard_map/ppermute | solution.py:28
  52.4 12.5 %all-to-all-start.2 = ((bf16[8,16,1152]{2,1,0:T(8,128)(2,1)}), bf16[8,16,1152]{2,1,0:T(8,128)(2,1)S(1)}, u32[]{:S(2)}, u32[]{:S(2)}) async-start(bf16[8,16,1152]{2,1,0:T(8,128)(2,1)} %get-tuple-element.44), calls=%async_computation.2 | async-start | bytes 589824 | tf_op jit(solution)/shard_map/all_to_all | solution.py:327
  56.0 24.1 %collective-permute-start.17 = (bf16[1280,128]{1,0:T(8,128)(2,1)S(1)}, bf16[1280,128]{1,0:T(8,128)(2,1)S(1)}, u32[]{:S(2)}, u32[]{:S(2)}) collective-permute-start(bf16[1280,128]{1,0:T(8,128)(2,1)S(1)} %collective-permute-done.12.refs_4_.refs_3_), channel_id=1, source_target_pairs={{0,8},{8,0},{16,24},{24,16},{32,40},{40,32},{48,56},{56,48},{64,72... | collective-permute-start | bytes 983048 | tf_op jit(solution)/shard_map/ppermute | solution.py:28
  65.7 11.2 %all-to-all-start.3 = ((bf16[8,16,1152]{2,1,0:T(8,128)(2,1)}), bf16[8,16,1152]{2,1,0:T(8,128)(2,1)S(1)}, u32[]{:S(2)}, u32[]{:S(2)}) async-start(bf16[8,16,1152]{2,1,0:T(8,128)(2,1)} %get-tuple-element.51), calls=%async_computation.3 | async-start | bytes 589824 | tf_op jit(solution)/shard_map/all_to_all | solution.py:327
  69.2 10.9 %collective-permute-start.16 = (bf16[960,128]{1,0:T(8,128)(2,1)S(1)}, bf16[960,128]{1,0:T(8,128)(2,1)S(1)}, u32[]{:S(2)}, u32[]{:S(2)}) collective-permute-start(bf16[960,128]{1,0:T(8,128)(2,1)S(1)} %copy-done.3), channel_id=1, source_target_pairs={{0,8},{8,0},{16,24},{24,16},{32,40},{40,32},{48,56},{56,48},{64,72... | collective-permute-start | bytes 737288 | tf_op jit(solution)/shard_map/ppermute | solution.py:28
  70.4 9.8 %collective-permute-start.13 = (bf16[64,1152]{1,0:T(8,128)(2,1)}, bf16[64,1152]{1,0:T(8,128)(2,1)S(1)}, u32[]{:S(2)}, u32[]{:S(2)}) collective-permute-start(bf16[64,1152]{1,0:T(8,128)(2,1)} %get-tuple-element.55), channel_id=1, source_target_pairs={{0,16},{8,24},{16,0},{24,8},{32,48},{40,56},{48,32},{56,40},{64,80... | collective-permute-start | bytes 442376 | tf_op jit(solution)/shard_map/ppermute | solution.py:28
  71.2 9.0 %collective-permute-start.14 = (bf16[64,1152]{1,0:T(8,128)(2,1)}, bf16[64,1152]{1,0:T(8,128)(2,1)}, u32[]{:S(2)}, u32[]{:S(2)}) collective-permute-start(bf16[64,1152]{1,0:T(8,128)(2,1)} %get-tuple-element.56), channel_id=1, source_target_pairs={{0,128},{8,136},{16,144},{24,152},{32,160},{40,168},{48,176},{56,1... | collective-permute-start | bytes 442376 | tf_op jit(solution)/shard_map/ppermute | solution.py:28
  71.9 8.3 %collective-permute-start.15 = (bf16[64,1152]{1,0:T(8,128)(2,1)}, bf16[64,1152]{1,0:T(8,128)(2,1)}, u32[]{:S(2)}, u32[]{:S(2)}) collective-permute-start(bf16[64,1152]{1,0:T(8,128)(2,1)} %get-tuple-element.57), channel_id=1, source_target_pairs={{0,144},{8,152},{16,128},{24,136},{32,176},{40,184},{48,160},{56,1... | collective-permute-start | bytes 442376 | tf_op jit(solution)/shard_map/ppermute | solution.py:28
  82.4 16.1 %all-to-all-start.4 = ((bf16[8,16,1152]{2,1,0:T(8,128)(2,1)}), bf16[8,16,1152]{2,1,0:T(8,128)(2,1)S(1)}, u32[]{:S(2)}, u32[]{:S(2)}) async-start(bf16[8,16,1152]{2,1,0:T(8,128)(2,1)} %get-tuple-element.58), calls=%async_computation.4 | async-start | bytes 589824 | tf_op jit(solution)/shard_map/all_to_all | solution.py:327
  89.4 13.0 %collective-permute-start.25 = (bf16[960,128]{1,0:T(8,128)(2,1)}, bf16[960,128]{1,0:T(8,128)(2,1)S(1)}, u32[]{:S(2)}, u32[]{:S(2)}) collective-permute-start(bf16[960,128]{1,0:T(8,128)(2,1)} %get-tuple-element.62.refs_6_), channel_id=1, source_target_pairs={{0,8},{8,0},{16,24},{24,16},{32,40},{40,32},{48,56},{56,48},{64,72... | collective-permute-start | bytes 737288 | tf_op jit(solution)/shard_map/ppermute | solution.py:28
  91.2 11.1 %collective-permute-start.26 = (bf16[960,128]{1,0:T(8,128)(2,1)}, bf16[960,128]{1,0:T(8,128)(2,1)S(1)}, u32[]{:S(2)}, u32[]{:S(2)}) collective-permute-start(bf16[960,128]{1,0:T(8,128)(2,1)} %get-tuple-element.63), channel_id=1, source_target_pairs={{0,128},{8,136},{16,144},{24,152},{32,160},{40,168},{48,176},{56,1... | collective-permute-start | bytes 737288 | tf_op jit(solution)/shard_map/ppermute | solution.py:28
  91.2 13.5 %collective-permute-start.27 = (bf16[960,128]{1,0:T(8,128)(2,1)}, bf16[960,128]{1,0:T(8,128)(2,1)S(1)}, u32[]{:S(2)}, u32[]{:S(2)}) collective-permute-start(bf16[960,128]{1,0:T(8,128)(2,1)} %get-tuple-element.64), channel_id=1, source_target_pairs={{0,136},{8,128},{16,152},{24,144},{32,168},{40,160},{48,184},{56,1... | collective-permute-start | bytes 737288 | tf_op jit(solution)/shard_map/ppermute | solution.py:28
  94.1 7.0 %collective-permute-start.29 = (bf16[16,1152]{1,0:T(8,128)(2,1)}, bf16[16,1152]{1,0:T(8,128)(2,1)S(1)}, u32[]{:S(2)}, u32[]{:S(2)}) collective-permute-start(bf16[16,1152]{1,0:T(8,128)(2,1)} %get-tuple-element.66), channel_id=1, source_target_pairs={{0,64},{8,72},{16,80},{24,88},{32,96},{40,104},{48,112},{56,120},{... | collective-permute-start | bytes 110600 | tf_op jit(solution)/shard_map/ppermute | solution.py:28
  107.4 26.1 %all-to-all-start.5 = ((bf16[8,40,1152]{2,1,0:T(8,128)(2,1)}), bf16[8,40,1152]{2,1,0:T(8,128)(2,1)S(1)}, u32[]{:S(2)}, u32[]{:S(2)}) async-start(bf16[8,40,1152]{2,1,0:T(8,128)(2,1)} %shard_map.121), calls=%async_computation.5 | async-start | bytes 1474560 | tf_op jit(solution)/shard_map/all_to_all | solution.py:427
  111.1 7.6 %collective-permute-start.18 = (bf16[16,1152]{1,0:T(8,128)(2,1)S(1)}, bf16[16,1152]{1,0:T(8,128)(2,1)S(1)}, u32[]{:S(2)}, u32[]{:S(2)}) collective-permute-start(bf16[16,1152]{1,0:T(8,128)(2,1)S(1)} %copy-done.4), channel_id=1, source_target_pairs={{0,1},{1,0},{2,3},{3,2},{4,5},{5,4},{6,7},{7,6},{8,9},{9,8},{10,11... | collective-permute-start | bytes 110600 | tf_op jit(solution)/shard_map/ppermute | solution.py:28
  114.9 7.4 %collective-permute-start.19 = (bf16[16,1152]{1,0:T(8,128)(2,1)S(1)}, bf16[16,1152]{1,0:T(8,128)(2,1)S(1)}, u32[]{:S(2)}, u32[]{:S(2)}) collective-permute-start(bf16[16,1152]{1,0:T(8,128)(2,1)S(1)} %copy-done.4), channel_id=1, source_target_pairs={{0,2},{1,3},{2,0},{3,1},{4,6},{5,7},{6,4},{7,5},{8,10},{9,11},{10,... | collective-permute-start | bytes 110600 | tf_op jit(solution)/shard_map/ppermute | solution.py:28
  (26 other events, 280.3 us)

commit v4 on v3

--- a/solution.py
+++ b/solution.py
@@ -411,7 +411,7 @@
     dn = tensor_all(dn)
     got = [dp(x, mask) for x, mask in zip(sent, (4, 8, 12))]
     rows = call(
-        image_body, block, (rank, dn, images, gain, de_rows), smem=(0,), hbm=(0,)
+        image_body, block, (rank, dn, images, gain, de_rows), smem=(0,), hbm=(0,), beside=(e_core,)
     )
     payload = call(
         weights_body,

time: 136 us -> 136 us (level)
  starting transfers between devices: 77 us -> 78.6 us
    ppermute x31, starting transfers between devices: 45.2 us -> 48.8 us  [swap(): return lax.ppermute(x, axis, [(i, i ^ mask) for i in range(n)])]
    all_to_all x5, starting transfers between devices: 28.1 us -> 25.8 us  [tensor_all(): return lax.all_to_all(x, 'tensor', 0, 0, tiled=True)]
  transfers between devices with their start and end apart: 37 -> 37, of which waited for: 13 -> 12; matrix products, arithmetic and copies ran while one was open for 0% -> 0% of each run, Pallas kernels for 11% -> 12%
where the time goes in v4:
time: 136 us; the launch traced here: 135 us
  starting transfers between devices  78.6 us (58%)
  waiting for transfers between devices  28.4 us (21%)
  Pallas kernels  25.4 us (19%)
  between operations  2.25 us (2%)
    ppermute x31, starting transfers between devices, swap(): return lax.ppermute(x, axis, [(i, i ^ mask) for i in range(n)])  48.8 us
    all_to_all x5, starting transfers between devices, tensor_all(): return lax.all_to_all(x, 'tensor', 0, 0, tiled=True)  25.8 us
    pallas_call x11, Pallas kernels, call(): pl.pallas_call(kernel, out_shape=tuple((pltpu.HBM(o.shape, o.dtype) if i...  21.3 us
    ppermute x31, waiting for transfers between devices, swap(): return lax.ppermute(x, axis, [(i, i ^ mask) for i in range(n)])  12.4 us
    all_to_all x5, waiting for transfers between devices, tensor_all(): return lax.all_to_all(x, 'tensor', 0, 0, tiled=True)  10.5 us
    all_to_all x1, waiting for transfers between devices, local(): lax.all_to_all(payload, 'dp', 0, 0, tiled=True, axis_index_groups=groups)  5.54 us
    pallas_call x1, Pallas kernels, forward(): pl.pallas_call(forward_body, out_shape=tuple((pltpu.HBM(*shape) for shape...  4.05 us
    all_to_all x1, starting transfers between devices, local(): lax.all_to_all(payload, 'dp', 0, 0, tiled=True, axis_index_groups=groups)  3.96 us
  transfers between devices with their start and end apart: 37, of which 12 were waited for; matrix products, arithmetic and copies ran while one was open for 0% of the time, Pallas kernels for 12%

profile of v4, /device:TPU:1, one launch (start us, length us, event | category | flops | bytes accessed | tf_op | source)
XLA Modules:
  0.0 134.8 jit_solution(1074019619798801888)
XLA Ops:
  0.6 4.0 %shard_map.111 = (bf16[128,1152]{1,0:T(8,128)(2,1)}, bf16[128,538]{1,0:T(8,128)(2,1)}, f32[128,538]{1,0:T(8,128)}, bf16[8,16,1152]{2,1,0:T(8,128)(2,1)}) custom-call(bf16[128,1152]{1,0:T(8,128)(2,1)} %refs_2_.4, f32[1152]{0:T(1024)} %refs_3_.3, bf16[538,1152]{1,0:T(8,128)(2,1)} %bitcast.5, f32[538]{0:T(1024)} %b_in.1, bf16[538,1152]{1,0:T(8,128)(2,1)} %refs_2_.3), custom_call_target="tpu_custom_call" | custom-call | flops 320000000 | bytes 4194304 | tf_op jit(solution)/shard_map/pallas_call | solution.py:140
  4.7 7.6 %all-to-all-start = ((bf16[8,16,1152]{2,1,0:T(8,128)(2,1)}), bf16[8,16,1152]{2,1,0:T(8,128)(2,1)S(1)}, u32[]{:S(2)}, u32[]{:S(2)}) async-start(bf16[8,16,1152]{2,1,0:T(8,128)(2,1)} %get-tuple-element.38.refs_3_), calls=%async_computation | async-start | bytes 589824 | tf_op jit(solution)/shard_map/all_to_all | solution.py:327
  12.3 3.1 %collective-permute-start = (bf16[16,1152]{1,0:T(8,128)(2,1)S(1)}, bf16[16,1152]{1,0:T(8,128)(2,1)S(1)}, u32[]{:S(2)}, u32[]{:S(2)}) collective-permute-start(bf16[16,1152]{1,0:T(8,128)(2,1)S(1)} %copy-done.5), channel_id=1, source_target_pairs={{0,32},{8,40},{16,48},{24,56},{32,0},{40,8},{48,16},{56,24},{64,96... | collective-permute-start | bytes 110600 | tf_op jit(solution)/shard_map/ppermute | solution.py:28
  15.4 5.1 %collective-permute-start.1 = (bf16[16,1152]{1,0:T(8,128)(2,1)S(1)}, bf16[16,1152]{1,0:T(8,128)(2,1)S(1)}, u32[]{:S(2)}, u32[]{:S(2)}) collective-permute-start(bf16[16,1152]{1,0:T(8,128)(2,1)S(1)} %copy-done.5), channel_id=1, source_target_pairs={{0,64},{8,72},{16,80},{24,88},{32,96},{40,104},{48,112},{56,120},{... | collective-permute-start | bytes 110600 | tf_op jit(solution)/shard_map/ppermute | solution.py:28
  20.6 2.4 %shard_map.112 = (bf16[320,128]{1,0:T(8,128)(2,1)}, bf16[960,128]{1,0:T(8,128)(2,1)}, bf16[1280,128]{1,0:T(8,128)(2,1)}) custom-call(s32[3]{0:T(128)S(1)} %pad_add_fusion.refs_0_, bf16[8,16,1152]{2,1,0:T(8,128)(2,1)} %bitcast.7, bf16[128,538]{1,0:T(8,128)(2,1)} %get-tuple-element.40.refs_2_, bf16[8,16,1152]{2,1,0:T(8,128)(2,1)} %get-tuple-element.38.refs_3_), custom_call_target="tpu_custom_call" | custom-call | flops 200000000 | bytes 2097152 | tf_op jit(solution)/shard_map/pallas_call | solution.py:64
  29.7 6.6 %all-to-all-start.1 = ((bf16[8,16,1152]{2,1,0:T(8,128)(2,1)}), bf16[8,16,1152]{2,1,0:T(8,128)(2,1)S(1)}, u32[]{:S(2)}, u32[]{:S(2)}) async-start(bf16[8,16,1152]{2,1,0:T(8,128)(2,1)} %get-tuple-element.42), calls=%async_computation.1 | async-start | bytes 589824 | tf_op jit(solution)/shard_map/all_to_all | solution.py:327
  36.3 4.1 %collective-permute-start.6 = (bf16[4,16,1152]{2,1,0:T(8,128)(2,1)}, bf16[4,16,1152]{2,1,0:T(8,128)(2,1)S(1)}, u32[]{:S(2)}, u32[]{:S(2)}) collective-permute-start(bf16[4,16,1152]{2,1,0:T(8,128)(2,1)} %get-tuple-element.43.refs_4_), channel_id=1, source_target_pairs={{0,8},{8,0},{16,24},{24,16},{32,40},{40,32},{48,56},{56,48},{64,72... | collective-permute-start | bytes 442376 | tf_op jit(solution)/shard_map/ppermute | solution.py:28
  44.1 2.5 %shard_map.114 = (bf16[8,16,1152]{2,1,0:T(8,128)(2,1)}, bf16[128,256]{1,0:T(8,128)(2,1)}, bf16[128,256]{1,0:T(8,128)(2,1)}, bf16[8,16,1152]{2,1,0:T(8,128)(2,1)}) custom-call(s32[3]{0:T(128)S(1)} %pad_add_fusion.refs_0_, f32[1]{0:T(128)S(6)} %copy.12.refs_1_.refs_0_, f32[1]{0:T(128)S(6)} %copy.13.refs_2_, ...), custom_call_target="tpu_custom_call" | custom-call | flops 300000000 | bytes 2097152 | tf_op jit(solution)/shard_map/pallas_call | solution.py:64
  46.6 5.7 %collective-permute-start.11 = (bf16[8,16,1152]{2,1,0:T(8,128)(2,1)}, bf16[8,16,1152]{2,1,0:T(8,128)(2,1)S(1)}, u32[]{:S(2)}, u32[]{:S(2)}) collective-permute-start(bf16[8,16,1152]{2,1,0:T(8,128)(2,1)} %get-tuple-element.49), channel_id=1, source_target_pairs={{0,8},{8,0},{16,24},{24,16},{32,40},{40,32},{48,56},{56,48},{64,72... | collective-permute-start | bytes 884744 | tf_op jit(solution)/shard_map/ppermute | solution.py:28
  52.4 3.6 %all-to-all-start.2 = ((bf16[8,16,1152]{2,1,0:T(8,128)(2,1)}), bf16[8,16,1152]{2,1,0:T(8,128)(2,1)S(1)}, u32[]{:S(2)}, u32[]{:S(2)}) async-start(bf16[8,16,1152]{2,1,0:T(8,128)(2,1)} %get-tuple-element.44), calls=%async_computation.2 | async-start | bytes 589824 | tf_op jit(solution)/shard_map/all_to_all | solution.py:327
  59.7 5.1 %all-to-all-done.2.refs_0_ = bf16[8,16,1152]{2,1,0:T(8,128)(2,1)S(1)} async-done(((bf16[8,16,1152]{2,1,0:T(8,128)(2,1)}), bf16[8,16,1152]{2,1,0:T(8,128)(2,1)S(1)}, u32[]{:S(2)}, u32[]{:S(2)}) %all-to-all-start.2) | async-done | bytes 294944 | tf_op jit(solution)/shard_map/all_to_all | solution.py:327
  65.7 3.4 %all-to-all-start.3 = ((bf16[8,16,1152]{2,1,0:T(8,128)(2,1)}), bf16[8,16,1152]{2,1,0:T(8,128)(2,1)S(1)}, u32[]{:S(2)}, u32[]{:S(2)}) async-start(bf16[8,16,1152]{2,1,0:T(8,128)(2,1)} %get-tuple-element.51), calls=%async_computation.3 | async-start | bytes 589824 | tf_op jit(solution)/shard_map/all_to_all | solution.py:327
  73.0 3.9 %all-to-all-done.3.refs_1_ = bf16[8,16,1152]{2,1,0:T(8,128)(2,1)S(1)} async-done(((bf16[8,16,1152]{2,1,0:T(8,128)(2,1)}), bf16[8,16,1152]{2,1,0:T(8,128)(2,1)S(1)}, u32[]{:S(2)}, u32[]{:S(2)}) %all-to-all-start.3) | async-done | bytes 294944 | tf_op jit(solution)/shard_map/all_to_all | solution.py:327
  76.9 3.2 %shard_map.117 = (bf16[128,538]{1,0:T(8,128)(2,1)S(1)}, bf16[320,128]{1,0:T(8,128)(2,1)}, bf16[960,128]{1,0:T(8,128)(2,1)}, bf16[960,128]{1,0:T(8,128)(2,1)}, bf16[960,128]{1,0:T(8,128)(2,1)}) custom-call(s32[3]{0:T(128)S(1)} %pad_add_fusion.refs_0_, bf16[8,16,1152]{2,1,0:T(8,128)(2,1)S(1)} %all-to-all-done.3.refs_1_, bf16[538,1152]{1,0:T(8,128)(2,1)} %refs_2_.3, ...), custom_call_target="tpu_custom_call" | custom-call | flops 360000000 | bytes 4194304 | tf_op jit(solution)/shard_map/pallas_call | solution.py:64
  84.7 4.6 %all-to-all-start.4 = ((bf16[8,16,1152]{2,1,0:T(8,128)(2,1)}), bf16[8,16,1152]{2,1,0:T(8,128)(2,1)S(1)}, u32[]{:S(2)}, u32[]{:S(2)}) async-start(bf16[8,16,1152]{2,1,0:T(8,128)(2,1)} %get-tuple-element.58), calls=%async_computation.4 | async-start | bytes 589824 | tf_op jit(solution)/shard_map/all_to_all | solution.py:327
  90.0 2.8 %collective-permute-start.27 = (bf16[960,128]{1,0:T(8,128)(2,1)}, bf16[960,128]{1,0:T(8,128)(2,1)S(1)}, u32[]{:S(2)}, u32[]{:S(2)}) collective-permute-start(bf16[960,128]{1,0:T(8,128)(2,1)} %get-tuple-element.64), channel_id=1, source_target_pairs={{0,136},{8,128},{16,152},{24,144},{32,168},{40,160},{48,184},{56,1... | collective-permute-start | bytes 737288 | tf_op jit(solution)/shard_map/ppermute | solution.py:28
  95.5 3.0 %collective-permute-start.30 = (bf16[16,1152]{1,0:T(8,128)(2,1)}, bf16[16,1152]{1,0:T(8,128)(2,1)S(1)}, u32[]{:S(2)}, u32[]{:S(2)}) collective-permute-start(bf16[16,1152]{1,0:T(8,128)(2,1)} %get-tuple-element.67), channel_id=1, source_target_pairs={{0,96},{8,104},{16,112},{24,120},{32,64},{40,72},{48,80},{56,88},{... | collective-permute-start | bytes 110600 | tf_op jit(solution)/shard_map/ppermute | solution.py:28
  101.8 2.9 %collective-permute-done.27.refs_9_ = bf16[960,128]{1,0:T(8,128)(2,1)S(1)} collective-permute-done((bf16[960,128]{1,0:T(8,128)(2,1)}, bf16[960,128]{1,0:T(8,128)(2,1)S(1)}, u32[]{:S(2)}, u32[]{:S(2)}) %collective-permute-start.27) | collective-permute-done | bytes 245792 | tf_op jit(solution)/shard_map/ppermute | solution.py:28
  104.7 2.7 %shard_map.121 = bf16[8,40,1152]{2,1,0:T(8,128)(2,1)} custom-call(bf16[320,128]{1,0:T(8,128)(2,1)S(1)} %copy-done.6, bf16[960,128]{1,0:T(8,128)(2,1)S(1)} %copy-done.3, bf16[960,128]{1,0:T(8,128)(2,1)S(1)} %collective-permute-done.16.refs_6_.refs_2_, bf16[1280,128]{1,0:T(8,128)(2,1)S(1)} %collective-permute-done.12.refs_4_.refs_3_, ...), custom_call_target="tpu_custom_call" | custom-call | flops 320000000 | bytes 3145728 | tf_op jit(solution)/shard_map/pallas_call | solution.py:64
  107.4 4.0 %all-to-all-start.5 = ((bf16[8,40,1152]{2,1,0:T(8,128)(2,1)}), bf16[8,40,1152]{2,1,0:T(8,128)(2,1)S(1)}, u32[]{:S(2)}, u32[]{:S(2)}) async-start(bf16[8,40,1152]{2,1,0:T(8,128)(2,1)} %shard_map.121), calls=%async_computation.5 | async-start | bytes 1474560 | tf_op jit(solution)/shard_map/all_to_all | solution.py:427
  111.4 3.6 %collective-permute-start.19 = (bf16[16,1152]{1,0:T(8,128)(2,1)S(1)}, bf16[16,1152]{1,0:T(8,128)(2,1)S(1)}, u32[]{:S(2)}, u32[]{:S(2)}) collective-permute-start(bf16[16,1152]{1,0:T(8,128)(2,1)S(1)} %copy-done.4), channel_id=1, source_target_pairs={{0,1},{1,0},{2,3},{3,2},{4,5},{5,4},{6,7},{7,6},{8,9},{9,8},{10,11... | collective-permute-start | bytes 110600 | tf_op jit(solution)/shard_map/ppermute | solution.py:28
  118.8 3.6 %collective-permute-start.24 = (bf16[16,1152]{1,0:T(8,128)(2,1)S(1)}, bf16[16,1152]{1,0:T(8,128)(2,1)S(1)}, u32[]{:S(2)}, u32[]{:S(2)}) collective-permute-start(bf16[16,1152]{1,0:T(8,128)(2,1)S(1)} %collective-permute-done.19.refs_2_), channel_id=1, source_target_pairs={{0,4},{1,5},{2,6},{3,7},{4,0},{5,1},{6,2},{7,3},{8,12},{9,13},{10,... | collective-permute-start | bytes 110600 | tf_op jit(solution)/shard_map/ppermute | solution.py:28
  124.3 2.6 %collective-permute-done.25.refs_8_ = bf16[16,1152]{1,0:T(8,128)(2,1)S(1)} collective-permute-done((bf16[16,1152]{1,0:T(8,128)(2,1)S(1)}, bf16[16,1152]{1,0:T(8,128)(2,1)S(1)}, u32[]{:S(2)}, u32[]{:S(2)}) %collective-permute-start.25) | collective-permute-done | bytes 36896 | tf_op jit(solution)/shard_map/ppermute | solution.py:28
  128.3 5.5 %all-to-all-done.5.refs_0_ = bf16[8,40,1152]{2,1,0:T(8,128)(2,1)S(1)} async-done(((bf16[8,40,1152]{2,1,0:T(8,128)(2,1)}), bf16[8,40,1152]{2,1,0:T(8,128)(2,1)S(1)}, u32[]{:S(2)}, u32[]{:S(2)}) %all-to-all-start.5) | async-done | bytes 737312 | tf_op jit(solution)/shard_map/all_to_all | solution.py:427
  (89 shorter events, 36.9 us)
Async XLA Ops:
  4.7 20.7 %all-to-all-start = ((bf16[8,16,1152]{2,1,0:T(8,128)(2,1)}), bf16[8,16,1152]{2,1,0:T(8,128)(2,1)S(1)}, u32[]{:S(2)}, u32[]{:S(2)}) async-start(bf16[8,16,1152]{2,1,0:T(8,128)(2,1)} %get-tuple-element.38.refs_3_), calls=%async_computation | async-start | bytes 589824 | tf_op jit(solution)/shard_map/all_to_all | solution.py:327
  12.3 10.7 %collective-permute-start = (bf16[16,1152]{1,0:T(8,128)(2,1)S(1)}, bf16[16,1152]{1,0:T(8,128)(2,1)S(1)}, u32[]{:S(2)}, u32[]{:S(2)}) collective-permute-start(bf16[16,1152]{1,0:T(8,128)(2,1)S(1)} %copy-done.5), channel_id=1, source_target_pairs={{0,32},{8,40},{16,48},{24,56},{32,0},{40,8},{48,16},{56,24},{64,96... | collective-permute-start | bytes 110600 | tf_op jit(solution)/shard_map/ppermute | solution.py:28
  15.4 7.7 %collective-permute-start.1 = (bf16[16,1152]{1,0:T(8,128)(2,1)S(1)}, bf16[16,1152]{1,0:T(8,128)(2,1)S(1)}, u32[]{:S(2)}, u32[]{:S(2)}) collective-permute-start(bf16[16,1152]{1,0:T(8,128)(2,1)S(1)} %copy-done.5), channel_id=1, source_target_pairs={{0,64},{8,72},{16,80},{24,88},{32,96},{40,104},{48,112},{56,120},{... | collective-permute-start | bytes 110600 | tf_op jit(solution)/shard_map/ppermute | solution.py:28
  27.0 13.4 %collective-permute-start.3 = (bf16[4,16,1152]{2,1,0:T(8,128)(2,1)}, bf16[4,16,1152]{2,1,0:T(8,128)(2,1)S(1)}, u32[]{:S(2)}, u32[]{:S(2)}) collective-permute-start(bf16[4,16,1152]{2,1,0:T(8,128)(2,1)} %get-tuple-element.43.refs_4_), channel_id=1, source_target_pairs={{0,16},{8,24},{16,0},{24,8},{32,48},{40,56},{48,32},{56,40},{64,80... | collective-permute-start | bytes 442376 | tf_op jit(solution)/shard_map/ppermute | solution.py:28
  27.8 12.6 %collective-permute-start.4 = (bf16[4,16,1152]{2,1,0:T(8,128)(2,1)}, bf16[4,16,1152]{2,1,0:T(8,128)(2,1)S(1)}, u32[]{:S(2)}, u32[]{:S(2)}) collective-permute-start(bf16[4,16,1152]{2,1,0:T(8,128)(2,1)} %get-tuple-element.43.refs_4_), channel_id=1, source_target_pairs={{0,128},{8,136},{16,144},{24,152},{32,160},{40,168},{48,176},{56,1... | collective-permute-start | bytes 442376 | tf_op jit(solution)/shard_map/ppermute | solution.py:28
  28.1 12.7 %collective-permute-start.5 = (bf16[4,16,1152]{2,1,0:T(8,128)(2,1)}, bf16[4,16,1152]{2,1,0:T(8,128)(2,1)S(1)}, u32[]{:S(2)}, u32[]{:S(2)}) collective-permute-start(bf16[4,16,1152]{2,1,0:T(8,128)(2,1)} %get-tuple-element.43.refs_4_), channel_id=1, source_target_pairs={{0,144},{8,152},{16,128},{24,136},{32,176},{40,184},{48,160},{56,1... | collective-permute-start | bytes 442376 | tf_op jit(solution)/shard_map/ppermute | solution.py:28
  29.7 14.4 %all-to-all-start.1 = ((bf16[8,16,1152]{2,1,0:T(8,128)(2,1)}), bf16[8,16,1152]{2,1,0:T(8,128)(2,1)S(1)}, u32[]{:S(2)}, u32[]{:S(2)}) async-start(bf16[8,16,1152]{2,1,0:T(8,128)(2,1)} %get-tuple-element.42), calls=%async_computation.1 | async-start | bytes 589824 | tf_op jit(solution)/shard_map/all_to_all | solution.py:327
  41.0 15.1 %collective-permute-start.12 = (bf16[1280,128]{1,0:T(8,128)(2,1)S(1)}, bf16[1280,128]{1,0:T(8,128)(2,1)S(1)}, u32[]{:S(2)}, u32[]{:S(2)}) collective-permute-start(bf16[1280,128]{1,0:T(8,128)(2,1)S(1)} %copy-done.12), channel_id=1, source_target_pairs={{0,128},{8,136},{16,144},{24,152},{32,160},{40,168},{48,176},{56,1... | collective-permute-start | bytes 983048 | tf_op jit(solution)/shard_map/ppermute | solution.py:28
  46.6 10.8 %collective-permute-start.11 = (bf16[8,16,1152]{2,1,0:T(8,128)(2,1)}, bf16[8,16,1152]{2,1,0:T(8,128)(2,1)S(1)}, u32[]{:S(2)}, u32[]{:S(2)}) collective-permute-start(bf16[8,16,1152]{2,1,0:T(8,128)(2,1)} %get-tuple-element.49), channel_id=1, source_target_pairs={{0,8},{8,0},{16,24},{24,16},{32,40},{40,32},{48,56},{56,48},{64,72... | collective-permute-start | bytes 884744 | tf_op jit(solution)/shard_map/ppermute | solution.py:28
  52.4 12.5 %all-to-all-start.2 = ((bf16[8,16,1152]{2,1,0:T(8,128)(2,1)}), bf16[8,16,1152]{2,1,0:T(8,128)(2,1)S(1)}, u32[]{:S(2)}, u32[]{:S(2)}) async-start(bf16[8,16,1152]{2,1,0:T(8,128)(2,1)} %get-tuple-element.44), calls=%async_computation.2 | async-start | bytes 589824 | tf_op jit(solution)/shard_map/all_to_all | solution.py:327
  56.0 26.5 %collective-permute-start.17 = (bf16[1280,128]{1,0:T(8,128)(2,1)S(1)}, bf16[1280,128]{1,0:T(8,128)(2,1)S(1)}, u32[]{:S(2)}, u32[]{:S(2)}) collective-permute-start(bf16[1280,128]{1,0:T(8,128)(2,1)S(1)} %collective-permute-done.12.refs_4_.refs_3_), channel_id=1, source_target_pairs={{0,8},{8,0},{16,24},{24,16},{32,40},{40,32},{48,56},{56,48},{64,72... | collective-permute-start | bytes 983048 | tf_op jit(solution)/shard_map/ppermute | solution.py:28
  65.7 11.2 %all-to-all-start.3 = ((bf16[8,16,1152]{2,1,0:T(8,128)(2,1)}), bf16[8,16,1152]{2,1,0:T(8,128)(2,1)S(1)}, u32[]{:S(2)}, u32[]{:S(2)}) async-start(bf16[8,16,1152]{2,1,0:T(8,128)(2,1)} %get-tuple-element.51), calls=%async_computation.3 | async-start | bytes 589824 | tf_op jit(solution)/shard_map/all_to_all | solution.py:327
  69.2 11.0 %collective-permute-start.16 = (bf16[960,128]{1,0:T(8,128)(2,1)S(1)}, bf16[960,128]{1,0:T(8,128)(2,1)S(1)}, u32[]{:S(2)}, u32[]{:S(2)}) collective-permute-start(bf16[960,128]{1,0:T(8,128)(2,1)S(1)} %copy-done.3), channel_id=1, source_target_pairs={{0,8},{8,0},{16,24},{24,16},{32,40},{40,32},{48,56},{56,48},{64,72... | collective-permute-start | bytes 737288 | tf_op jit(solution)/shard_map/ppermute | solution.py:28
  70.4 12.1 %collective-permute-start.13 = (bf16[64,1152]{1,0:T(8,128)(2,1)}, bf16[64,1152]{1,0:T(8,128)(2,1)S(1)}, u32[]{:S(2)}, u32[]{:S(2)}) collective-permute-start(bf16[64,1152]{1,0:T(8,128)(2,1)} %get-tuple-element.55), channel_id=1, source_target_pairs={{0,16},{8,24},{16,0},{24,8},{32,48},{40,56},{48,32},{56,40},{64,80... | collective-permute-start | bytes 442376 | tf_op jit(solution)/shard_map/ppermute | solution.py:28
  71.2 11.4 %collective-permute-start.14 = (bf16[64,1152]{1,0:T(8,128)(2,1)}, bf16[64,1152]{1,0:T(8,128)(2,1)}, u32[]{:S(2)}, u32[]{:S(2)}) collective-permute-start(bf16[64,1152]{1,0:T(8,128)(2,1)} %get-tuple-element.56), channel_id=1, source_target_pairs={{0,128},{8,136},{16,144},{24,152},{32,160},{40,168},{48,176},{56,1... | collective-permute-start | bytes 442376 | tf_op jit(solution)/shard_map/ppermute | solution.py:28
  71.9 10.6 %collective-permute-start.15 = (bf16[64,1152]{1,0:T(8,128)(2,1)}, bf16[64,1152]{1,0:T(8,128)(2,1)}, u32[]{:S(2)}, u32[]{:S(2)}) collective-permute-start(bf16[64,1152]{1,0:T(8,128)(2,1)} %get-tuple-element.57), channel_id=1, source_target_pairs={{0,144},{8,152},{16,128},{24,136},{32,176},{40,184},{48,160},{56,1... | collective-permute-start | bytes 442376 | tf_op jit(solution)/shard_map/ppermute | solution.py:28
  80.2 15.3 %collective-permute-start.18 = (bf16[960,128]{1,0:T(8,128)(2,1)}, bf16[960,128]{1,0:T(8,128)(2,1)S(1)}, u32[]{:S(2)}, u32[]{:S(2)}) collective-permute-start(bf16[960,128]{1,0:T(8,128)(2,1)} %get-tuple-element.60.refs_6_), channel_id=1, source_target_pairs={{0,8},{8,0},{16,24},{24,16},{32,40},{40,32},{48,56},{56,48},{64,72... | collective-permute-start | bytes 737288 | tf_op jit(solution)/shard_map/ppermute | solution.py:28
  84.7 13.7 %all-to-all-start.4 = ((bf16[8,16,1152]{2,1,0:T(8,128)(2,1)}), bf16[8,16,1152]{2,1,0:T(8,128)(2,1)S(1)}, u32[]{:S(2)}, u32[]{:S(2)}) async-start(bf16[8,16,1152]{2,1,0:T(8,128)(2,1)} %get-tuple-element.58), calls=%async_computation.4 | async-start | bytes 589824 | tf_op jit(solution)/shard_map/all_to_all | solution.py:327
  89.3 12.4 %collective-permute-start.26 = (bf16[960,128]{1,0:T(8,128)(2,1)}, bf16[960,128]{1,0:T(8,128)(2,1)S(1)}, u32[]{:S(2)}, u32[]{:S(2)}) collective-permute-start(bf16[960,128]{1,0:T(8,128)(2,1)} %get-tuple-element.63), channel_id=1, source_target_pairs={{0,128},{8,136},{16,144},{24,152},{32,160},{40,168},{48,176},{56,1... | collective-permute-start | bytes 737288 | tf_op jit(solution)/shard_map/ppermute | solution.py:28
  90.0 14.7 %collective-permute-start.27 = (bf16[960,128]{1,0:T(8,128)(2,1)}, bf16[960,128]{1,0:T(8,128)(2,1)S(1)}, u32[]{:S(2)}, u32[]{:S(2)}) collective-permute-start(bf16[960,128]{1,0:T(8,128)(2,1)} %get-tuple-element.64), channel_id=1, source_target_pairs={{0,136},{8,128},{16,152},{24,144},{32,168},{40,160},{48,184},{56,1... | collective-permute-start | bytes 737288 | tf_op jit(solution)/shard_map/ppermute | solution.py:28
  94.0 7.2 %collective-permute-start.29 = (bf16[16,1152]{1,0:T(8,128)(2,1)}, bf16[16,1152]{1,0:T(8,128)(2,1)S(1)}, u32[]{:S(2)}, u32[]{:S(2)}) collective-permute-start(bf16[16,1152]{1,0:T(8,128)(2,1)} %get-tuple-element.66), channel_id=1, source_target_pairs={{0,64},{8,72},{16,80},{24,88},{32,96},{40,104},{48,112},{56,120},{... | collective-permute-start | bytes 110600 | tf_op jit(solution)/shard_map/ppermute | solution.py:28
  107.4 26.5 %all-to-all-start.5 = ((bf16[8,40,1152]{2,1,0:T(8,128)(2,1)}), bf16[8,40,1152]{2,1,0:T(8,128)(2,1)S(1)}, u32[]{:S(2)}, u32[]{:S(2)}) async-start(bf16[8,40,1152]{2,1,0:T(8,128)(2,1)} %shard_map.121), calls=%async_computation.5 | async-start | bytes 1474560 | tf_op jit(solution)/shard_map/all_to_all | solution.py:427
  111.4 7.4 %collective-permute-start.19 = (bf16[16,1152]{1,0:T(8,128)(2,1)S(1)}, bf16[16,1152]{1,0:T(8,128)(2,1)S(1)}, u32[]{:S(2)}, u32[]{:S(2)}) collective-permute-start(bf16[16,1152]{1,0:T(8,128)(2,1)S(1)} %copy-done.4), channel_id=1, source_target_pairs={{0,1},{1,0},{2,3},{3,2},{4,5},{5,4},{6,7},{7,6},{8,9},{9,8},{10,11... | collective-permute-start | bytes 110600 | tf_op jit(solution)/shard_map/ppermute | solution.py:28
  114.9 7.5 %collective-permute-start.20 = (bf16[16,1152]{1,0:T(8,128)(2,1)S(1)}, bf16[16,1152]{1,0:T(8,128)(2,1)S(1)}, u32[]{:S(2)}, u32[]{:S(2)}) collective-permute-start(bf16[16,1152]{1,0:T(8,128)(2,1)S(1)} %copy-done.4), channel_id=1, source_target_pairs={{0,2},{1,3},{2,0},{3,1},{4,6},{5,7},{6,4},{7,5},{8,10},{9,11},{10,... | collective-permute-start | bytes 110600 | tf_op jit(solution)/shard_map/ppermute | solution.py:28
  (26 other events, 282.5 us)

commit v5 on v4

--- a/solution.py
+++ b/solution.py
@@ -343,12 +343,12 @@
     unit, enorm, spread, four = call(
         embed_body,
         (sds((ROWS, D), F32), sds((ROWS, 128), F32), blocks, sds((4, ROWS, D), BF)),
-        (rank, images, tensor_all(part), texts, dp(texts, 4), dp(texts, 8), dp(texts, 12)),
+        (rank, images, tensor_all(part), texts, dp(texts, 8), dp(texts, 4), dp(texts, 12)),
         smem=(0,),
         hbm=(0, 1, 2, 3),
         after=(n_own,),
     )
-    t_own = [four, dp(four, 2), dp(four, 16), dp(four, 18)]
+    t_own = [four, dp(four, 18), dp(four, 16), dp(four, 2)]
     t_oth = [dp(x, 1) for x in t_own]
     unit_b = tensor_all(spread)
     du, c_own, c_oth, again = call(
@@ -372,7 +372,7 @@
         flops=2 * 75_000_000,
         size=2 << 20,
     )
-    got = [dp(x, mask) for x, mask in zip(sent, (2, 16, 18))]
+    got = [dp(x, mask) for x, mask in zip(sent, (18, 16, 2))]
     n_core = dp(n_own, 1)
     n_x = dp(n_tox, 16)
     n_xc = dp(n_x, 1)
@@ -409,7 +409,7 @@
         size=2 << 20,
     )
     dn = tensor_all(dn)
-    got = [dp(x, mask) for x, mask in zip(sent, (4, 8, 12))]
+    got = [dp(x, mask) for x, mask in zip(sent, (8, 4, 12))]
     rows = call(
         image_body, block, (rank, dn, images, gain, de_rows), smem=(0,), hbm=(0,), beside=(e_core,)
     )

time: 136 us -> 138 us (1.015)
  waiting for transfers between devices: 28.4 us -> 31.2 us
    ppermute x31, waiting for transfers between devices: 12.4 us -> 15 us  [swap(): return lax.ppermute(x, axis, [(i, i ^ mask) for i in range(n)])]
  transfers between devices with their start and end apart: 37 -> 37, of which waited for: 12 -> 14; matrix products, arithmetic and copies ran while one was open for 0% -> 0% of each run, Pallas kernels for 12% -> 12%
where the time goes in v5:
time: 138 us; the launch traced here: 137 us
  starting transfers between devices  78.3 us (57%)
  waiting for transfers between devices  31.2 us (23%)
  Pallas kernels  25.4 us (18%)
  between operations  2.24 us (2%)
    ppermute x31, starting transfers between devices, swap(): return lax.ppermute(x, axis, [(i, i ^ mask) for i in range(n)])  48.2 us
    all_to_all x5, starting transfers between devices, tensor_all(): return lax.all_to_all(x, 'tensor', 0, 0, tiled=True)  26.4 us
    pallas_call x11, Pallas kernels, call(): pl.pallas_call(kernel, out_shape=tuple((pltpu.HBM(o.shape, o.dtype) if i...  21.4 us
    ppermute x31, waiting for transfers between devices, swap(): return lax.ppermute(x, axis, [(i, i ^ mask) for i in range(n)])  15 us
    all_to_all x5, waiting for transfers between devices, tensor_all(): return lax.all_to_all(x, 'tensor', 0, 0, tiled=True)  10.5 us
    all_to_all x1, waiting for transfers between devices, local(): lax.all_to_all(payload, 'dp', 0, 0, tiled=True, axis_index_groups=groups)  5.71 us
    pallas_call x1, Pallas kernels, forward(): pl.pallas_call(forward_body, out_shape=tuple((pltpu.HBM(*shape) for shape...  4.05 us
    all_to_all x1, starting transfers between devices, local(): lax.all_to_all(payload, 'dp', 0, 0, tiled=True, axis_index_groups=groups)  3.69 us
  transfers between devices with their start and end apart: 37, of which 14 were waited for; matrix products, arithmetic and copies ran while one was open for 0% of the time, Pallas kernels for 12%

profile of v5, /device:TPU:1, one launch (start us, length us, event | category | flops | bytes accessed | tf_op | source)
XLA Modules:
  0.0 137.3 jit_solution(10871441948061651682)
XLA Ops:
  0.6 4.0 %shard_map.111 = (bf16[128,1152]{1,0:T(8,128)(2,1)}, bf16[128,538]{1,0:T(8,128)(2,1)}, f32[128,538]{1,0:T(8,128)}, bf16[8,16,1152]{2,1,0:T(8,128)(2,1)}) custom-call(bf16[128,1152]{1,0:T(8,128)(2,1)} %refs_2_.4, f32[1152]{0:T(1024)} %refs_3_.3, bf16[538,1152]{1,0:T(8,128)(2,1)} %bitcast.5, f32[538]{0:T(1024)} %b_in.1, bf16[538,1152]{1,0:T(8,128)(2,1)} %refs_2_.3), custom_call_target="tpu_custom_call" | custom-call | flops 320000000 | bytes 4194304 | tf_op jit(solution)/shard_map/pallas_call | solution.py:140
  4.7 7.6 %all-to-all-start = ((bf16[8,16,1152]{2,1,0:T(8,128)(2,1)}), bf16[8,16,1152]{2,1,0:T(8,128)(2,1)S(1)}, u32[]{:S(2)}, u32[]{:S(2)}) async-start(bf16[8,16,1152]{2,1,0:T(8,128)(2,1)} %get-tuple-element.38.refs_3_), calls=%async_computation | async-start | bytes 589824 | tf_op jit(solution)/shard_map/all_to_all | solution.py:327
  12.3 7.0 %collective-permute-start = (bf16[16,1152]{1,0:T(8,128)(2,1)S(1)}, bf16[16,1152]{1,0:T(8,128)(2,1)S(1)}, u32[]{:S(2)}, u32[]{:S(2)}) collective-permute-start(bf16[16,1152]{1,0:T(8,128)(2,1)S(1)} %copy-done.5), channel_id=1, source_target_pairs={{0,64},{8,72},{16,80},{24,88},{32,96},{40,104},{48,112},{56,120},{... | collective-permute-start | bytes 110600 | tf_op jit(solution)/shard_map/ppermute | solution.py:28
  20.6 2.4 %shard_map.112 = (bf16[320,128]{1,0:T(8,128)(2,1)}, bf16[960,128]{1,0:T(8,128)(2,1)}, bf16[1280,128]{1,0:T(8,128)(2,1)}) custom-call(s32[3]{0:T(128)S(1)} %pad_add_fusion.refs_0_, bf16[8,16,1152]{2,1,0:T(8,128)(2,1)} %bitcast.7, bf16[128,538]{1,0:T(8,128)(2,1)} %get-tuple-element.40.refs_2_, bf16[8,16,1152]{2,1,0:T(8,128)(2,1)} %get-tuple-element.38.refs_3_), custom_call_target="tpu_custom_call" | custom-call | flops 200000000 | bytes 2097152 | tf_op jit(solution)/shard_map/pallas_call | solution.py:64
  29.7 6.6 %all-to-all-start.1 = ((bf16[8,16,1152]{2,1,0:T(8,128)(2,1)}), bf16[8,16,1152]{2,1,0:T(8,128)(2,1)S(1)}, u32[]{:S(2)}, u32[]{:S(2)}) async-start(bf16[8,16,1152]{2,1,0:T(8,128)(2,1)} %get-tuple-element.42), calls=%async_computation.1 | async-start | bytes 589824 | tf_op jit(solution)/shard_map/all_to_all | solution.py:327
  36.3 4.1 %collective-permute-start.6 = (bf16[4,16,1152]{2,1,0:T(8,128)(2,1)}, bf16[4,16,1152]{2,1,0:T(8,128)(2,1)S(1)}, u32[]{:S(2)}, u32[]{:S(2)}) collective-permute-start(bf16[4,16,1152]{2,1,0:T(8,128)(2,1)} %get-tuple-element.43.refs_4_), channel_id=1, source_target_pairs={{0,8},{8,0},{16,24},{24,16},{32,40},{40,32},{48,56},{56,48},{64,72... | collective-permute-start | bytes 442376 | tf_op jit(solution)/shard_map/ppermute | solution.py:28
  44.1 2.6 %shard_map.114 = (bf16[8,16,1152]{2,1,0:T(8,128)(2,1)}, bf16[128,256]{1,0:T(8,128)(2,1)}, bf16[128,256]{1,0:T(8,128)(2,1)}, bf16[8,16,1152]{2,1,0:T(8,128)(2,1)}) custom-call(s32[3]{0:T(128)S(1)} %pad_add_fusion.refs_0_, f32[1]{0:T(128)S(6)} %copy.12.refs_1_.refs_0_, f32[1]{0:T(128)S(6)} %copy.13.refs_2_, ...), custom_call_target="tpu_custom_call" | custom-call | flops 300000000 | bytes 2097152 | tf_op jit(solution)/shard_map/pallas_call | solution.py:64
  46.7 5.7 %collective-permute-start.11 = (bf16[8,16,1152]{2,1,0:T(8,128)(2,1)}, bf16[8,16,1152]{2,1,0:T(8,128)(2,1)S(1)}, u32[]{:S(2)}, u32[]{:S(2)}) collective-permute-start(bf16[8,16,1152]{2,1,0:T(8,128)(2,1)} %get-tuple-element.49), channel_id=1, source_target_pairs={{0,8},{8,0},{16,24},{24,16},{32,40},{40,32},{48,56},{56,48},{64,72... | collective-permute-start | bytes 884744 | tf_op jit(solution)/shard_map/ppermute | solution.py:28
  52.4 3.6 %all-to-all-start.2 = ((bf16[8,16,1152]{2,1,0:T(8,128)(2,1)}), bf16[8,16,1152]{2,1,0:T(8,128)(2,1)S(1)}, u32[]{:S(2)}, u32[]{:S(2)}) async-start(bf16[8,16,1152]{2,1,0:T(8,128)(2,1)} %get-tuple-element.44), calls=%async_computation.2 | async-start | bytes 589824 | tf_op jit(solution)/shard_map/all_to_all | solution.py:327
  59.7 5.1 %all-to-all-done.2.refs_0_ = bf16[8,16,1152]{2,1,0:T(8,128)(2,1)S(1)} async-done(((bf16[8,16,1152]{2,1,0:T(8,128)(2,1)}), bf16[8,16,1152]{2,1,0:T(8,128)(2,1)S(1)}, u32[]{:S(2)}, u32[]{:S(2)}) %all-to-all-start.2) | async-done | bytes 294944 | tf_op jit(solution)/shard_map/all_to_all | solution.py:327
  65.7 3.4 %all-to-all-start.3 = ((bf16[8,16,1152]{2,1,0:T(8,128)(2,1)}), bf16[8,16,1152]{2,1,0:T(8,128)(2,1)S(1)}, u32[]{:S(2)}, u32[]{:S(2)}) async-start(bf16[8,16,1152]{2,1,0:T(8,128)(2,1)} %get-tuple-element.51), calls=%async_computation.3 | async-start | bytes 589824 | tf_op jit(solution)/shard_map/all_to_all | solution.py:327
  73.0 3.9 %all-to-all-done.3.refs_1_ = bf16[8,16,1152]{2,1,0:T(8,128)(2,1)S(1)} async-done(((bf16[8,16,1152]{2,1,0:T(8,128)(2,1)}), bf16[8,16,1152]{2,1,0:T(8,128)(2,1)S(1)}, u32[]{:S(2)}, u32[]{:S(2)}) %all-to-all-start.3) | async-done | bytes 294944 | tf_op jit(solution)/shard_map/all_to_all | solution.py:327
  76.9 3.2 %shard_map.117 = (bf16[128,538]{1,0:T(8,128)(2,1)S(1)}, bf16[320,128]{1,0:T(8,128)(2,1)}, bf16[960,128]{1,0:T(8,128)(2,1)}, bf16[960,128]{1,0:T(8,128)(2,1)}, bf16[960,128]{1,0:T(8,128)(2,1)}) custom-call(s32[3]{0:T(128)S(1)} %pad_add_fusion.refs_0_, bf16[8,16,1152]{2,1,0:T(8,128)(2,1)S(1)} %all-to-all-done.3.refs_1_, bf16[538,1152]{1,0:T(8,128)(2,1)} %refs_2_.3, ...), custom_call_target="tpu_custom_call" | custom-call | flops 360000000 | bytes 4194304 | tf_op jit(solution)/shard_map/pallas_call | solution.py:64
  80.2 2.4 %collective-permute-start.18 = (bf16[960,128]{1,0:T(8,128)(2,1)}, bf16[960,128]{1,0:T(8,128)(2,1)S(1)}, u32[]{:S(2)}, u32[]{:S(2)}) collective-permute-start(bf16[960,128]{1,0:T(8,128)(2,1)} %get-tuple-element.60.refs_6_), channel_id=1, source_target_pairs={{0,8},{8,0},{16,24},{24,16},{32,40},{40,32},{48,56},{56,48},{64,72... | collective-permute-start | bytes 737288 | tf_op jit(solution)/shard_map/ppermute | solution.py:28
  84.7 5.2 %all-to-all-start.4 = ((bf16[8,16,1152]{2,1,0:T(8,128)(2,1)}), bf16[8,16,1152]{2,1,0:T(8,128)(2,1)S(1)}, u32[]{:S(2)}, u32[]{:S(2)}) async-start(bf16[8,16,1152]{2,1,0:T(8,128)(2,1)} %get-tuple-element.58), calls=%async_computation.4 | async-start | bytes 589824 | tf_op jit(solution)/shard_map/all_to_all | solution.py:327
  90.0 2.9 %collective-permute-start.26 = (bf16[960,128]{1,0:T(8,128)(2,1)}, bf16[960,128]{1,0:T(8,128)(2,1)S(1)}, u32[]{:S(2)}, u32[]{:S(2)}) collective-permute-start(bf16[960,128]{1,0:T(8,128)(2,1)} %get-tuple-element.63), channel_id=1, source_target_pairs={{0,128},{8,136},{16,144},{24,152},{32,160},{40,168},{48,176},{56,1... | collective-permute-start | bytes 737288 | tf_op jit(solution)/shard_map/ppermute | solution.py:28
  95.3 3.3 %collective-permute-start.30 = (bf16[16,1152]{1,0:T(8,128)(2,1)}, bf16[16,1152]{1,0:T(8,128)(2,1)S(1)}, u32[]{:S(2)}, u32[]{:S(2)}) collective-permute-start(bf16[16,1152]{1,0:T(8,128)(2,1)} %get-tuple-element.67), channel_id=1, source_target_pairs={{0,96},{8,104},{16,112},{24,120},{32,64},{40,72},{48,80},{56,88},{... | collective-permute-start | bytes 110600 | tf_op jit(solution)/shard_map/ppermute | solution.py:28
  102.4 5.3 %collective-permute-done.27.refs_9_ = bf16[960,128]{1,0:T(8,128)(2,1)S(1)} collective-permute-done((bf16[960,128]{1,0:T(8,128)(2,1)}, bf16[960,128]{1,0:T(8,128)(2,1)S(1)}, u32[]{:S(2)}, u32[]{:S(2)}) %collective-permute-start.27) | collective-permute-done | bytes 245792 | tf_op jit(solution)/shard_map/ppermute | solution.py:28
  107.6 2.7 %shard_map.121 = bf16[8,40,1152]{2,1,0:T(8,128)(2,1)} custom-call(bf16[320,128]{1,0:T(8,128)(2,1)S(1)} %copy-done.6, bf16[960,128]{1,0:T(8,128)(2,1)S(1)} %copy-done.3, bf16[960,128]{1,0:T(8,128)(2,1)S(1)} %collective-permute-done.16.refs_6_.refs_2_, bf16[1280,128]{1,0:T(8,128)(2,1)S(1)} %collective-permute-done.12.refs_4_.refs_3_, ...), custom_call_target="tpu_custom_call" | custom-call | flops 320000000 | bytes 3145728 | tf_op jit(solution)/shard_map/pallas_call | solution.py:64
  110.3 3.7 %all-to-all-start.5 = ((bf16[8,40,1152]{2,1,0:T(8,128)(2,1)}), bf16[8,40,1152]{2,1,0:T(8,128)(2,1)S(1)}, u32[]{:S(2)}, u32[]{:S(2)}) async-start(bf16[8,40,1152]{2,1,0:T(8,128)(2,1)} %shard_map.121), calls=%async_computation.5 | async-start | bytes 1474560 | tf_op jit(solution)/shard_map/all_to_all | solution.py:427
  114.0 3.5 %collective-permute-start.19 = (bf16[16,1152]{1,0:T(8,128)(2,1)S(1)}, bf16[16,1152]{1,0:T(8,128)(2,1)S(1)}, u32[]{:S(2)}, u32[]{:S(2)}) collective-permute-start(bf16[16,1152]{1,0:T(8,128)(2,1)S(1)} %copy-done.4), channel_id=1, source_target_pairs={{0,1},{1,0},{2,3},{3,2},{4,5},{5,4},{6,7},{7,6},{8,9},{9,8},{10,11... | collective-permute-start | bytes 110600 | tf_op jit(solution)/shard_map/ppermute | solution.py:28
  118.7 2.4 %collective-permute-start.21 = (bf16[16,1152]{1,0:T(8,128)(2,1)S(1)}, bf16[16,1152]{1,0:T(8,128)(2,1)S(1)}, u32[]{:S(2)}, u32[]{:S(2)}) collective-permute-start(bf16[16,1152]{1,0:T(8,128)(2,1)S(1)} %copy-done.4), channel_id=1, source_target_pairs={{0,4},{1,5},{2,6},{3,7},{4,0},{5,1},{6,2},{7,3},{8,12},{9,13},{10,... | collective-permute-start | bytes 110600 | tf_op jit(solution)/shard_map/ppermute | solution.py:28
  121.4 3.6 %collective-permute-start.24 = (bf16[16,1152]{1,0:T(8,128)(2,1)S(1)}, bf16[16,1152]{1,0:T(8,128)(2,1)S(1)}, u32[]{:S(2)}, u32[]{:S(2)}) collective-permute-start(bf16[16,1152]{1,0:T(8,128)(2,1)S(1)} %collective-permute-done.19.refs_2_), channel_id=1, source_target_pairs={{0,4},{1,5},{2,6},{3,7},{4,0},{5,1},{6,2},{7,3},{8,12},{9,13},{10,... | collective-permute-start | bytes 110600 | tf_op jit(solution)/shard_map/ppermute | solution.py:28
  130.7 5.7 %all-to-all-done.5.refs_0_ = bf16[8,40,1152]{2,1,0:T(8,128)(2,1)S(1)} async-done(((bf16[8,40,1152]{2,1,0:T(8,128)(2,1)}), bf16[8,40,1152]{2,1,0:T(8,128)(2,1)S(1)}, u32[]{:S(2)}, u32[]{:S(2)}) %all-to-all-start.5) | async-done | bytes 737312 | tf_op jit(solution)/shard_map/all_to_all | solution.py:427
  (89 shorter events, 35.3 us)
Async XLA Ops:
  4.7 20.7 %all-to-all-start = ((bf16[8,16,1152]{2,1,0:T(8,128)(2,1)}), bf16[8,16,1152]{2,1,0:T(8,128)(2,1)S(1)}, u32[]{:S(2)}, u32[]{:S(2)}) async-start(bf16[8,16,1152]{2,1,0:T(8,128)(2,1)} %get-tuple-element.38.refs_3_), calls=%async_computation | async-start | bytes 589824 | tf_op jit(solution)/shard_map/all_to_all | solution.py:327
  12.3 10.7 %collective-permute-start = (bf16[16,1152]{1,0:T(8,128)(2,1)S(1)}, bf16[16,1152]{1,0:T(8,128)(2,1)S(1)}, u32[]{:S(2)}, u32[]{:S(2)}) collective-permute-start(bf16[16,1152]{1,0:T(8,128)(2,1)S(1)} %copy-done.5), channel_id=1, source_target_pairs={{0,64},{8,72},{16,80},{24,88},{32,96},{40,104},{48,112},{56,120},{... | collective-permute-start | bytes 110600 | tf_op jit(solution)/shard_map/ppermute | solution.py:28
  27.0 13.4 %collective-permute-start.3 = (bf16[4,16,1152]{2,1,0:T(8,128)(2,1)}, bf16[4,16,1152]{2,1,0:T(8,128)(2,1)S(1)}, u32[]{:S(2)}, u32[]{:S(2)}) collective-permute-start(bf16[4,16,1152]{2,1,0:T(8,128)(2,1)} %get-tuple-element.43.refs_4_), channel_id=1, source_target_pairs={{0,144},{8,152},{16,128},{24,136},{32,176},{40,184},{48,160},{56,1... | collective-permute-start | bytes 442376 | tf_op jit(solution)/shard_map/ppermute | solution.py:28
  27.8 12.6 %collective-permute-start.4 = (bf16[4,16,1152]{2,1,0:T(8,128)(2,1)}, bf16[4,16,1152]{2,1,0:T(8,128)(2,1)S(1)}, u32[]{:S(2)}, u32[]{:S(2)}) collective-permute-start(bf16[4,16,1152]{2,1,0:T(8,128)(2,1)} %get-tuple-element.43.refs_4_), channel_id=1, source_target_pairs={{0,128},{8,136},{16,144},{24,152},{32,160},{40,168},{48,176},{56,1... | collective-permute-start | bytes 442376 | tf_op jit(solution)/shard_map/ppermute | solution.py:28
  29.0 11.9 %collective-permute-start.5 = (bf16[4,16,1152]{2,1,0:T(8,128)(2,1)}, bf16[4,16,1152]{2,1,0:T(8,128)(2,1)S(1)}, u32[]{:S(2)}, u32[]{:S(2)}) collective-permute-start(bf16[4,16,1152]{2,1,0:T(8,128)(2,1)} %get-tuple-element.43.refs_4_), channel_id=1, source_target_pairs={{0,16},{8,24},{16,0},{24,8},{32,48},{40,56},{48,32},{56,40},{64,80... | collective-permute-start | bytes 442376 | tf_op jit(solution)/shard_map/ppermute | solution.py:28
  29.7 14.4 %all-to-all-start.1 = ((bf16[8,16,1152]{2,1,0:T(8,128)(2,1)}), bf16[8,16,1152]{2,1,0:T(8,128)(2,1)S(1)}, u32[]{:S(2)}, u32[]{:S(2)}) async-start(bf16[8,16,1152]{2,1,0:T(8,128)(2,1)} %get-tuple-element.42), calls=%async_computation.1 | async-start | bytes 589824 | tf_op jit(solution)/shard_map/all_to_all | solution.py:327
  41.0 15.1 %collective-permute-start.12 = (bf16[1280,128]{1,0:T(8,128)(2,1)S(1)}, bf16[1280,128]{1,0:T(8,128)(2,1)S(1)}, u32[]{:S(2)}, u32[]{:S(2)}) collective-permute-start(bf16[1280,128]{1,0:T(8,128)(2,1)S(1)} %copy-done.12), channel_id=1, source_target_pairs={{0,128},{8,136},{16,144},{24,152},{32,160},{40,168},{48,176},{56,1... | collective-permute-start | bytes 983048 | tf_op jit(solution)/shard_map/ppermute | solution.py:28
  46.7 10.8 %collective-permute-start.11 = (bf16[8,16,1152]{2,1,0:T(8,128)(2,1)}, bf16[8,16,1152]{2,1,0:T(8,128)(2,1)S(1)}, u32[]{:S(2)}, u32[]{:S(2)}) collective-permute-start(bf16[8,16,1152]{2,1,0:T(8,128)(2,1)} %get-tuple-element.49), channel_id=1, source_target_pairs={{0,8},{8,0},{16,24},{24,16},{32,40},{40,32},{48,56},{56,48},{64,72... | collective-permute-start | bytes 884744 | tf_op jit(solution)/shard_map/ppermute | solution.py:28
  52.4 12.5 %all-to-all-start.2 = ((bf16[8,16,1152]{2,1,0:T(8,128)(2,1)}), bf16[8,16,1152]{2,1,0:T(8,128)(2,1)S(1)}, u32[]{:S(2)}, u32[]{:S(2)}) async-start(bf16[8,16,1152]{2,1,0:T(8,128)(2,1)} %get-tuple-element.44), calls=%async_computation.2 | async-start | bytes 589824 | tf_op jit(solution)/shard_map/all_to_all | solution.py:327
  56.0 26.5 %collective-permute-start.17 = (bf16[1280,128]{1,0:T(8,128)(2,1)S(1)}, bf16[1280,128]{1,0:T(8,128)(2,1)S(1)}, u32[]{:S(2)}, u32[]{:S(2)}) collective-permute-start(bf16[1280,128]{1,0:T(8,128)(2,1)S(1)} %collective-permute-done.12.refs_4_.refs_3_), channel_id=1, source_target_pairs={{0,8},{8,0},{16,24},{24,16},{32,40},{40,32},{48,56},{56,48},{64,72... | collective-permute-start | bytes 983048 | tf_op jit(solution)/shard_map/ppermute | solution.py:28
  65.7 11.2 %all-to-all-start.3 = ((bf16[8,16,1152]{2,1,0:T(8,128)(2,1)}), bf16[8,16,1152]{2,1,0:T(8,128)(2,1)S(1)}, u32[]{:S(2)}, u32[]{:S(2)}) async-start(bf16[8,16,1152]{2,1,0:T(8,128)(2,1)} %get-tuple-element.51), calls=%async_computation.3 | async-start | bytes 589824 | tf_op jit(solution)/shard_map/all_to_all | solution.py:327
  69.2 11.0 %collective-permute-start.16 = (bf16[960,128]{1,0:T(8,128)(2,1)S(1)}, bf16[960,128]{1,0:T(8,128)(2,1)S(1)}, u32[]{:S(2)}, u32[]{:S(2)}) collective-permute-start(bf16[960,128]{1,0:T(8,128)(2,1)S(1)} %copy-done.3), channel_id=1, source_target_pairs={{0,8},{8,0},{16,24},{24,16},{32,40},{40,32},{48,56},{56,48},{64,72... | collective-permute-start | bytes 737288 | tf_op jit(solution)/shard_map/ppermute | solution.py:28
  70.4 12.1 %collective-permute-start.13 = (bf16[64,1152]{1,0:T(8,128)(2,1)}, bf16[64,1152]{1,0:T(8,128)(2,1)S(1)}, u32[]{:S(2)}, u32[]{:S(2)}) collective-permute-start(bf16[64,1152]{1,0:T(8,128)(2,1)} %get-tuple-element.55), channel_id=1, source_target_pairs={{0,144},{8,152},{16,128},{24,136},{32,176},{40,184},{48,160},{56,1... | collective-permute-start | bytes 442376 | tf_op jit(solution)/shard_map/ppermute | solution.py:28
  71.6 10.9 %collective-permute-start.14 = (bf16[64,1152]{1,0:T(8,128)(2,1)}, bf16[64,1152]{1,0:T(8,128)(2,1)}, u32[]{:S(2)}, u32[]{:S(2)}) collective-permute-start(bf16[64,1152]{1,0:T(8,128)(2,1)} %get-tuple-element.56), channel_id=1, source_target_pairs={{0,128},{8,136},{16,144},{24,152},{32,160},{40,168},{48,176},{56,1... | collective-permute-start | bytes 442376 | tf_op jit(solution)/shard_map/ppermute | solution.py:28
  72.3 10.2 %collective-permute-start.15 = (bf16[64,1152]{1,0:T(8,128)(2,1)}, bf16[64,1152]{1,0:T(8,128)(2,1)}, u32[]{:S(2)}, u32[]{:S(2)}) collective-permute-start(bf16[64,1152]{1,0:T(8,128)(2,1)} %get-tuple-element.57), channel_id=1, source_target_pairs={{0,16},{8,24},{16,0},{24,8},{32,48},{40,56},{48,32},{56,40},{64,80... | collective-permute-start | bytes 442376 | tf_op jit(solution)/shard_map/ppermute | solution.py:28
  80.2 15.1 %collective-permute-start.18 = (bf16[960,128]{1,0:T(8,128)(2,1)}, bf16[960,128]{1,0:T(8,128)(2,1)S(1)}, u32[]{:S(2)}, u32[]{:S(2)}) collective-permute-start(bf16[960,128]{1,0:T(8,128)(2,1)} %get-tuple-element.60.refs_6_), channel_id=1, source_target_pairs={{0,8},{8,0},{16,24},{24,16},{32,40},{40,32},{48,56},{56,48},{64,72... | collective-permute-start | bytes 737288 | tf_op jit(solution)/shard_map/ppermute | solution.py:28
  84.7 13.8 %all-to-all-start.4 = ((bf16[8,16,1152]{2,1,0:T(8,128)(2,1)}), bf16[8,16,1152]{2,1,0:T(8,128)(2,1)S(1)}, u32[]{:S(2)}, u32[]{:S(2)}) async-start(bf16[8,16,1152]{2,1,0:T(8,128)(2,1)} %get-tuple-element.58), calls=%async_computation.4 | async-start | bytes 589824 | tf_op jit(solution)/shard_map/all_to_all | solution.py:327
  90.0 12.4 %collective-permute-start.26 = (bf16[960,128]{1,0:T(8,128)(2,1)}, bf16[960,128]{1,0:T(8,128)(2,1)S(1)}, u32[]{:S(2)}, u32[]{:S(2)}) collective-permute-start(bf16[960,128]{1,0:T(8,128)(2,1)} %get-tuple-element.63), channel_id=1, source_target_pairs={{0,128},{8,136},{16,144},{24,152},{32,160},{40,168},{48,176},{56,1... | collective-permute-start | bytes 737288 | tf_op jit(solution)/shard_map/ppermute | solution.py:28
  92.8 14.8 %collective-permute-start.27 = (bf16[960,128]{1,0:T(8,128)(2,1)}, bf16[960,128]{1,0:T(8,128)(2,1)S(1)}, u32[]{:S(2)}, u32[]{:S(2)}) collective-permute-start(bf16[960,128]{1,0:T(8,128)(2,1)} %get-tuple-element.64), channel_id=1, source_target_pairs={{0,136},{8,128},{16,152},{24,144},{32,168},{40,160},{48,184},{56,1... | collective-permute-start | bytes 737288 | tf_op jit(solution)/shard_map/ppermute | solution.py:28
  92.9 7.4 %collective-permute-start.28 = (bf16[16,1152]{1,0:T(8,128)(2,1)}, bf16[16,1152]{1,0:T(8,128)(2,1)S(1)}, u32[]{:S(2)}, u32[]{:S(2)}) collective-permute-start(bf16[16,1152]{1,0:T(8,128)(2,1)} %get-tuple-element.65), channel_id=1, source_target_pairs={{0,64},{8,72},{16,80},{24,88},{32,96},{40,104},{48,112},{56,120},{... | collective-permute-start | bytes 110600 | tf_op jit(solution)/shard_map/ppermute | solution.py:28
  110.3 26.1 %all-to-all-start.5 = ((bf16[8,40,1152]{2,1,0:T(8,128)(2,1)}), bf16[8,40,1152]{2,1,0:T(8,128)(2,1)S(1)}, u32[]{:S(2)}, u32[]{:S(2)}) async-start(bf16[8,40,1152]{2,1,0:T(8,128)(2,1)} %shard_map.121), calls=%async_computation.5 | async-start | bytes 1474560 | tf_op jit(solution)/shard_map/all_to_all | solution.py:427
  114.0 7.4 %collective-permute-start.19 = (bf16[16,1152]{1,0:T(8,128)(2,1)S(1)}, bf16[16,1152]{1,0:T(8,128)(2,1)S(1)}, u32[]{:S(2)}, u32[]{:S(2)}) collective-permute-start(bf16[16,1152]{1,0:T(8,128)(2,1)S(1)} %copy-done.4), channel_id=1, source_target_pairs={{0,1},{1,0},{2,3},{3,2},{4,5},{5,4},{6,7},{7,6},{8,9},{9,8},{10,11... | collective-permute-start | bytes 110600 | tf_op jit(solution)/shard_map/ppermute | solution.py:28
  117.5 7.5 %collective-permute-start.20 = (bf16[16,1152]{1,0:T(8,128)(2,1)S(1)}, bf16[16,1152]{1,0:T(8,128)(2,1)S(1)}, u32[]{:S(2)}, u32[]{:S(2)}) collective-permute-start(bf16[16,1152]{1,0:T(8,128)(2,1)S(1)} %copy-done.4), channel_id=1, source_target_pairs={{0,2},{1,3},{2,0},{3,1},{4,6},{5,7},{6,4},{7,5},{8,10},{9,11},{10,... | collective-permute-start | bytes 110600 | tf_op jit(solution)/shard_map/ppermute | solution.py:28
  118.7 6.5 %collective-permute-start.21 = (bf16[16,1152]{1,0:T(8,128)(2,1)S(1)}, bf16[16,1152]{1,0:T(8,128)(2,1)S(1)}, u32[]{:S(2)}, u32[]{:S(2)}) collective-permute-start(bf16[16,1152]{1,0:T(8,128)(2,1)S(1)} %copy-done.4), channel_id=1, source_target_pairs={{0,4},{1,5},{2,6},{3,7},{4,0},{5,1},{6,2},{7,3},{8,12},{9,13},{10,... | collective-permute-start | bytes 110600 | tf_op jit(solution)/shard_map/ppermute | solution.py:28
  (26 other events, 280.8 us)

commit v6 on v5

--- a/solution.py
+++ b/solution.py
@@ -348,7 +348,7 @@
         hbm=(0, 1, 2, 3),
         after=(n_own,),
     )
-    t_own = [four, dp(four, 18), dp(four, 16), dp(four, 2)]
+    t_own = [four, dp(four, 2), dp(four, 16), dp(four, 18)]
     t_oth = [dp(x, 1) for x in t_own]
     unit_b = tensor_all(spread)
     du, c_own, c_oth, again = call(
@@ -372,7 +372,7 @@
         flops=2 * 75_000_000,
         size=2 << 20,
     )
-    got = [dp(x, mask) for x, mask in zip(sent, (18, 16, 2))]
+    got = [dp(x, mask) for x, mask in zip(sent, (2, 16, 18))]
     n_core = dp(n_own, 1)
     n_x = dp(n_tox, 16)
     n_xc = dp(n_x, 1)

time: 138 us -> 135 us (0.978)
  waiting for transfers between devices: 31.2 us -> 28.4 us
    ppermute x31, waiting for transfers between devices: 15 us -> 12.2 us  [swap(): return lax.ppermute(x, axis, [(i, i ^ mask) for i in range(n)])]
  transfers between devices with their start and end apart: 37 -> 37, of which waited for: 14 -> 13; matrix products, arithmetic and copies ran while one was open for 0% -> 0% of each run, Pallas kernels for 12% -> 12%
where the time goes in v6:
time: 135 us; the launch traced here: 134 us
  starting transfers between devices  78.3 us (58%)
  waiting for transfers between devices  28.4 us (21%)
  Pallas kernels  25.4 us (19%)
  between operations  2.24 us (2%)
    ppermute x31, starting transfers between devices, swap(): return lax.ppermute(x, axis, [(i, i ^ mask) for i in range(n)])  48.9 us
    all_to_all x5, starting transfers between devices, tensor_all(): return lax.all_to_all(x, 'tensor', 0, 0, tiled=True)  25.8 us
    pallas_call x11, Pallas kernels, call(): pl.pallas_call(kernel, out_shape=tuple((pltpu.HBM(o.shape, o.dtype) if i...  21.3 us
    ppermute x31, waiting for transfers between devices, swap(): return lax.ppermute(x, axis, [(i, i ^ mask) for i in range(n)])  12.2 us
    all_to_all x5, waiting for transfers between devices, tensor_all(): return lax.all_to_all(x, 'tensor', 0, 0, tiled=True)  10.5 us
    all_to_all x1, waiting for transfers between devices, local(): lax.all_to_all(payload, 'dp', 0, 0, tiled=True, axis_index_groups=groups)  5.7 us
    pallas_call x1, Pallas kernels, forward(): pl.pallas_call(forward_body, out_shape=tuple((pltpu.HBM(*shape) for shape...  4.05 us
    all_to_all x1, starting transfers between devices, local(): lax.all_to_all(payload, 'dp', 0, 0, tiled=True, axis_index_groups=groups)  3.69 us
  transfers between devices with their start and end apart: 37, of which 13 were waited for; matrix products, arithmetic and copies ran while one was open for 0% of the time, Pallas kernels for 12%

profile of v6, /device:TPU:1, one launch (start us, length us, event | category | flops | bytes accessed | tf_op | source)
XLA Modules:
  0.0 134.5 jit_solution(11011313326630874277)
XLA Ops:
  0.6 4.0 %shard_map.111 = (bf16[128,1152]{1,0:T(8,128)(2,1)}, bf16[128,538]{1,0:T(8,128)(2,1)}, f32[128,538]{1,0:T(8,128)}, bf16[8,16,1152]{2,1,0:T(8,128)(2,1)}) custom-call(bf16[128,1152]{1,0:T(8,128)(2,1)} %refs_2_.4, f32[1152]{0:T(1024)} %refs_3_.3, bf16[538,1152]{1,0:T(8,128)(2,1)} %bitcast.5, f32[538]{0:T(1024)} %b_in.1, bf16[538,1152]{1,0:T(8,128)(2,1)} %refs_2_.3), custom_call_target="tpu_custom_call" | custom-call | flops 320000000 | bytes 4194304 | tf_op jit(solution)/shard_map/pallas_call | solution.py:140
  4.7 7.6 %all-to-all-start = ((bf16[8,16,1152]{2,1,0:T(8,128)(2,1)}), bf16[8,16,1152]{2,1,0:T(8,128)(2,1)S(1)}, u32[]{:S(2)}, u32[]{:S(2)}) async-start(bf16[8,16,1152]{2,1,0:T(8,128)(2,1)} %get-tuple-element.38.refs_3_), calls=%async_computation | async-start | bytes 589824 | tf_op jit(solution)/shard_map/all_to_all | solution.py:327
  12.3 7.0 %collective-permute-start = (bf16[16,1152]{1,0:T(8,128)(2,1)S(1)}, bf16[16,1152]{1,0:T(8,128)(2,1)S(1)}, u32[]{:S(2)}, u32[]{:S(2)}) collective-permute-start(bf16[16,1152]{1,0:T(8,128)(2,1)S(1)} %copy-done.5), channel_id=1, source_target_pairs={{0,64},{8,72},{16,80},{24,88},{32,96},{40,104},{48,112},{56,120},{... | collective-permute-start | bytes 110600 | tf_op jit(solution)/shard_map/ppermute | solution.py:28
  20.6 2.4 %shard_map.112 = (bf16[320,128]{1,0:T(8,128)(2,1)}, bf16[960,128]{1,0:T(8,128)(2,1)}, bf16[1280,128]{1,0:T(8,128)(2,1)}) custom-call(s32[3]{0:T(128)S(1)} %pad_add_fusion.refs_0_, bf16[8,16,1152]{2,1,0:T(8,128)(2,1)} %bitcast.7, bf16[128,538]{1,0:T(8,128)(2,1)} %get-tuple-element.40.refs_2_, bf16[8,16,1152]{2,1,0:T(8,128)(2,1)} %get-tuple-element.38.refs_3_), custom_call_target="tpu_custom_call" | custom-call | flops 200000000 | bytes 2097152 | tf_op jit(solution)/shard_map/pallas_call | solution.py:64
  29.7 6.6 %all-to-all-start.1 = ((bf16[8,16,1152]{2,1,0:T(8,128)(2,1)}), bf16[8,16,1152]{2,1,0:T(8,128)(2,1)S(1)}, u32[]{:S(2)}, u32[]{:S(2)}) async-start(bf16[8,16,1152]{2,1,0:T(8,128)(2,1)} %get-tuple-element.42), calls=%async_computation.1 | async-start | bytes 589824 | tf_op jit(solution)/shard_map/all_to_all | solution.py:327
  36.3 4.1 %collective-permute-start.6 = (bf16[4,16,1152]{2,1,0:T(8,128)(2,1)}, bf16[4,16,1152]{2,1,0:T(8,128)(2,1)S(1)}, u32[]{:S(2)}, u32[]{:S(2)}) collective-permute-start(bf16[4,16,1152]{2,1,0:T(8,128)(2,1)} %get-tuple-element.43.refs_4_), channel_id=1, source_target_pairs={{0,8},{8,0},{16,24},{24,16},{32,40},{40,32},{48,56},{56,48},{64,72... | collective-permute-start | bytes 442376 | tf_op jit(solution)/shard_map/ppermute | solution.py:28
  44.1 2.5 %shard_map.114 = (bf16[8,16,1152]{2,1,0:T(8,128)(2,1)}, bf16[128,256]{1,0:T(8,128)(2,1)}, bf16[128,256]{1,0:T(8,128)(2,1)}, bf16[8,16,1152]{2,1,0:T(8,128)(2,1)}) custom-call(s32[3]{0:T(128)S(1)} %pad_add_fusion.refs_0_, f32[1]{0:T(128)S(6)} %copy.12.refs_1_.refs_0_, f32[1]{0:T(128)S(6)} %copy.13.refs_2_, ...), custom_call_target="tpu_custom_call" | custom-call | flops 300000000 | bytes 2097152 | tf_op jit(solution)/shard_map/pallas_call | solution.py:64
  46.6 5.7 %collective-permute-start.11 = (bf16[8,16,1152]{2,1,0:T(8,128)(2,1)}, bf16[8,16,1152]{2,1,0:T(8,128)(2,1)S(1)}, u32[]{:S(2)}, u32[]{:S(2)}) collective-permute-start(bf16[8,16,1152]{2,1,0:T(8,128)(2,1)} %get-tuple-element.49), channel_id=1, source_target_pairs={{0,8},{8,0},{16,24},{24,16},{32,40},{40,32},{48,56},{56,48},{64,72... | collective-permute-start | bytes 884744 | tf_op jit(solution)/shard_map/ppermute | solution.py:28
  52.4 3.6 %all-to-all-start.2 = ((bf16[8,16,1152]{2,1,0:T(8,128)(2,1)}), bf16[8,16,1152]{2,1,0:T(8,128)(2,1)S(1)}, u32[]{:S(2)}, u32[]{:S(2)}) async-start(bf16[8,16,1152]{2,1,0:T(8,128)(2,1)} %get-tuple-element.44), calls=%async_computation.2 | async-start | bytes 589824 | tf_op jit(solution)/shard_map/all_to_all | solution.py:327
  59.7 5.1 %all-to-all-done.2.refs_0_ = bf16[8,16,1152]{2,1,0:T(8,128)(2,1)S(1)} async-done(((bf16[8,16,1152]{2,1,0:T(8,128)(2,1)}), bf16[8,16,1152]{2,1,0:T(8,128)(2,1)S(1)}, u32[]{:S(2)}, u32[]{:S(2)}) %all-to-all-start.2) | async-done | bytes 294944 | tf_op jit(solution)/shard_map/all_to_all | solution.py:327
  65.7 3.4 %all-to-all-start.3 = ((bf16[8,16,1152]{2,1,0:T(8,128)(2,1)}), bf16[8,16,1152]{2,1,0:T(8,128)(2,1)S(1)}, u32[]{:S(2)}, u32[]{:S(2)}) async-start(bf16[8,16,1152]{2,1,0:T(8,128)(2,1)} %get-tuple-element.51), calls=%async_computation.3 | async-start | bytes 589824 | tf_op jit(solution)/shard_map/all_to_all | solution.py:327
  73.0 3.9 %all-to-all-done.3.refs_1_ = bf16[8,16,1152]{2,1,0:T(8,128)(2,1)S(1)} async-done(((bf16[8,16,1152]{2,1,0:T(8,128)(2,1)}), bf16[8,16,1152]{2,1,0:T(8,128)(2,1)S(1)}, u32[]{:S(2)}, u32[]{:S(2)}) %all-to-all-start.3) | async-done | bytes 294944 | tf_op jit(solution)/shard_map/all_to_all | solution.py:327
  76.9 3.2 %shard_map.117 = (bf16[128,538]{1,0:T(8,128)(2,1)S(1)}, bf16[320,128]{1,0:T(8,128)(2,1)}, bf16[960,128]{1,0:T(8,128)(2,1)}, bf16[960,128]{1,0:T(8,128)(2,1)}, bf16[960,128]{1,0:T(8,128)(2,1)}) custom-call(s32[3]{0:T(128)S(1)} %pad_add_fusion.refs_0_, bf16[8,16,1152]{2,1,0:T(8,128)(2,1)S(1)} %all-to-all-done.3.refs_1_, bf16[538,1152]{1,0:T(8,128)(2,1)} %refs_2_.3, ...), custom_call_target="tpu_custom_call" | custom-call | flops 360000000 | bytes 4194304 | tf_op jit(solution)/shard_map/pallas_call | solution.py:64
  80.2 2.4 %collective-permute-start.18 = (bf16[960,128]{1,0:T(8,128)(2,1)}, bf16[960,128]{1,0:T(8,128)(2,1)S(1)}, u32[]{:S(2)}, u32[]{:S(2)}) collective-permute-start(bf16[960,128]{1,0:T(8,128)(2,1)} %get-tuple-element.60.refs_6_), channel_id=1, source_target_pairs={{0,8},{8,0},{16,24},{24,16},{32,40},{40,32},{48,56},{56,48},{64,72... | collective-permute-start | bytes 737288 | tf_op jit(solution)/shard_map/ppermute | solution.py:28
  84.7 4.6 %all-to-all-start.4 = ((bf16[8,16,1152]{2,1,0:T(8,128)(2,1)}), bf16[8,16,1152]{2,1,0:T(8,128)(2,1)S(1)}, u32[]{:S(2)}, u32[]{:S(2)}) async-start(bf16[8,16,1152]{2,1,0:T(8,128)(2,1)} %get-tuple-element.58), calls=%async_computation.4 | async-start | bytes 589824 | tf_op jit(solution)/shard_map/all_to_all | solution.py:327
  90.0 2.8 %collective-permute-start.27 = (bf16[960,128]{1,0:T(8,128)(2,1)}, bf16[960,128]{1,0:T(8,128)(2,1)S(1)}, u32[]{:S(2)}, u32[]{:S(2)}) collective-permute-start(bf16[960,128]{1,0:T(8,128)(2,1)} %get-tuple-element.64), channel_id=1, source_target_pairs={{0,136},{8,128},{16,152},{24,144},{32,168},{40,160},{48,184},{56,1... | collective-permute-start | bytes 737288 | tf_op jit(solution)/shard_map/ppermute | solution.py:28
  95.3 3.2 %collective-permute-start.30 = (bf16[16,1152]{1,0:T(8,128)(2,1)}, bf16[16,1152]{1,0:T(8,128)(2,1)S(1)}, u32[]{:S(2)}, u32[]{:S(2)}) collective-permute-start(bf16[16,1152]{1,0:T(8,128)(2,1)} %get-tuple-element.67), channel_id=1, source_target_pairs={{0,96},{8,104},{16,112},{24,120},{32,64},{40,72},{48,80},{56,88},{... | collective-permute-start | bytes 110600 | tf_op jit(solution)/shard_map/ppermute | solution.py:28
  101.0 3.8 %collective-permute-done.27.refs_9_ = bf16[960,128]{1,0:T(8,128)(2,1)S(1)} collective-permute-done((bf16[960,128]{1,0:T(8,128)(2,1)}, bf16[960,128]{1,0:T(8,128)(2,1)S(1)}, u32[]{:S(2)}, u32[]{:S(2)}) %collective-permute-start.27) | collective-permute-done | bytes 245792 | tf_op jit(solution)/shard_map/ppermute | solution.py:28
  104.7 2.7 %shard_map.121 = bf16[8,40,1152]{2,1,0:T(8,128)(2,1)} custom-call(bf16[320,128]{1,0:T(8,128)(2,1)S(1)} %copy-done.6, bf16[960,128]{1,0:T(8,128)(2,1)S(1)} %copy-done.3, bf16[960,128]{1,0:T(8,128)(2,1)S(1)} %collective-permute-done.16.refs_6_.refs_2_, bf16[1280,128]{1,0:T(8,128)(2,1)S(1)} %collective-permute-done.12.refs_4_.refs_3_, ...), custom_call_target="tpu_custom_call" | custom-call | flops 320000000 | bytes 3145728 | tf_op jit(solution)/shard_map/pallas_call | solution.py:64
  107.4 3.7 %all-to-all-start.5 = ((bf16[8,40,1152]{2,1,0:T(8,128)(2,1)}), bf16[8,40,1152]{2,1,0:T(8,128)(2,1)S(1)}, u32[]{:S(2)}, u32[]{:S(2)}) async-start(bf16[8,40,1152]{2,1,0:T(8,128)(2,1)} %shard_map.121), calls=%async_computation.5 | async-start | bytes 1474560 | tf_op jit(solution)/shard_map/all_to_all | solution.py:427
  111.1 3.6 %collective-permute-start.19 = (bf16[16,1152]{1,0:T(8,128)(2,1)S(1)}, bf16[16,1152]{1,0:T(8,128)(2,1)S(1)}, u32[]{:S(2)}, u32[]{:S(2)}) collective-permute-start(bf16[16,1152]{1,0:T(8,128)(2,1)S(1)} %copy-done.4), channel_id=1, source_target_pairs={{0,1},{1,0},{2,3},{3,2},{4,5},{5,4},{6,7},{7,6},{8,9},{9,8},{10,11... | collective-permute-start | bytes 110600 | tf_op jit(solution)/shard_map/ppermute | solution.py:28
  115.9 2.4 %collective-permute-start.21 = (bf16[16,1152]{1,0:T(8,128)(2,1)S(1)}, bf16[16,1152]{1,0:T(8,128)(2,1)S(1)}, u32[]{:S(2)}, u32[]{:S(2)}) collective-permute-start(bf16[16,1152]{1,0:T(8,128)(2,1)S(1)} %copy-done.4), channel_id=1, source_target_pairs={{0,4},{1,5},{2,6},{3,7},{4,0},{5,1},{6,2},{7,3},{8,12},{9,13},{10,... | collective-permute-start | bytes 110600 | tf_op jit(solution)/shard_map/ppermute | solution.py:28
  118.6 3.6 %collective-permute-start.24 = (bf16[16,1152]{1,0:T(8,128)(2,1)S(1)}, bf16[16,1152]{1,0:T(8,128)(2,1)S(1)}, u32[]{:S(2)}, u32[]{:S(2)}) collective-permute-start(bf16[16,1152]{1,0:T(8,128)(2,1)S(1)} %collective-permute-done.19.refs_2_), channel_id=1, source_target_pairs={{0,4},{1,5},{2,6},{3,7},{4,0},{5,1},{6,2},{7,3},{8,12},{9,13},{10,... | collective-permute-start | bytes 110600 | tf_op jit(solution)/shard_map/ppermute | solution.py:28
  127.9 5.7 %all-to-all-done.5.refs_0_ = bf16[8,40,1152]{2,1,0:T(8,128)(2,1)S(1)} async-done(((bf16[8,40,1152]{2,1,0:T(8,128)(2,1)}), bf16[8,40,1152]{2,1,0:T(8,128)(2,1)S(1)}, u32[]{:S(2)}, u32[]{:S(2)}) %all-to-all-start.5) | async-done | bytes 737312 | tf_op jit(solution)/shard_map/all_to_all | solution.py:427
  (89 shorter events, 34.7 us)
Async XLA Ops:
  4.7 20.7 %all-to-all-start = ((bf16[8,16,1152]{2,1,0:T(8,128)(2,1)}), bf16[8,16,1152]{2,1,0:T(8,128)(2,1)S(1)}, u32[]{:S(2)}, u32[]{:S(2)}) async-start(bf16[8,16,1152]{2,1,0:T(8,128)(2,1)} %get-tuple-element.38.refs_3_), calls=%async_computation | async-start | bytes 589824 | tf_op jit(solution)/shard_map/all_to_all | solution.py:327
  12.3 10.7 %collective-permute-start = (bf16[16,1152]{1,0:T(8,128)(2,1)S(1)}, bf16[16,1152]{1,0:T(8,128)(2,1)S(1)}, u32[]{:S(2)}, u32[]{:S(2)}) collective-permute-start(bf16[16,1152]{1,0:T(8,128)(2,1)S(1)} %copy-done.5), channel_id=1, source_target_pairs={{0,64},{8,72},{16,80},{24,88},{32,96},{40,104},{48,112},{56,120},{... | collective-permute-start | bytes 110600 | tf_op jit(solution)/shard_map/ppermute | solution.py:28
  27.0 13.4 %collective-permute-start.3 = (bf16[4,16,1152]{2,1,0:T(8,128)(2,1)}, bf16[4,16,1152]{2,1,0:T(8,128)(2,1)S(1)}, u32[]{:S(2)}, u32[]{:S(2)}) collective-permute-start(bf16[4,16,1152]{2,1,0:T(8,128)(2,1)} %get-tuple-element.43.refs_4_), channel_id=1, source_target_pairs={{0,16},{8,24},{16,0},{24,8},{32,48},{40,56},{48,32},{56,40},{64,80... | collective-permute-start | bytes 442376 | tf_op jit(solution)/shard_map/ppermute | solution.py:28
  27.8 12.6 %collective-permute-start.4 = (bf16[4,16,1152]{2,1,0:T(8,128)(2,1)}, bf16[4,16,1152]{2,1,0:T(8,128)(2,1)S(1)}, u32[]{:S(2)}, u32[]{:S(2)}) collective-permute-start(bf16[4,16,1152]{2,1,0:T(8,128)(2,1)} %get-tuple-element.43.refs_4_), channel_id=1, source_target_pairs={{0,128},{8,136},{16,144},{24,152},{32,160},{40,168},{48,176},{56,1... | collective-permute-start | bytes 442376 | tf_op jit(solution)/shard_map/ppermute | solution.py:28
  28.1 12.7 %collective-permute-start.5 = (bf16[4,16,1152]{2,1,0:T(8,128)(2,1)}, bf16[4,16,1152]{2,1,0:T(8,128)(2,1)S(1)}, u32[]{:S(2)}, u32[]{:S(2)}) collective-permute-start(bf16[4,16,1152]{2,1,0:T(8,128)(2,1)} %get-tuple-element.43.refs_4_), channel_id=1, source_target_pairs={{0,144},{8,152},{16,128},{24,136},{32,176},{40,184},{48,160},{56,1... | collective-permute-start | bytes 442376 | tf_op jit(solution)/shard_map/ppermute | solution.py:28
  29.7 14.4 %all-to-all-start.1 = ((bf16[8,16,1152]{2,1,0:T(8,128)(2,1)}), bf16[8,16,1152]{2,1,0:T(8,128)(2,1)S(1)}, u32[]{:S(2)}, u32[]{:S(2)}) async-start(bf16[8,16,1152]{2,1,0:T(8,128)(2,1)} %get-tuple-element.42), calls=%async_computation.1 | async-start | bytes 589824 | tf_op jit(solution)/shard_map/all_to_all | solution.py:327
  41.0 15.1 %collective-permute-start.12 = (bf16[1280,128]{1,0:T(8,128)(2,1)S(1)}, bf16[1280,128]{1,0:T(8,128)(2,1)S(1)}, u32[]{:S(2)}, u32[]{:S(2)}) collective-permute-start(bf16[1280,128]{1,0:T(8,128)(2,1)S(1)} %copy-done.12), channel_id=1, source_target_pairs={{0,128},{8,136},{16,144},{24,152},{32,160},{40,168},{48,176},{56,1... | collective-permute-start | bytes 983048 | tf_op jit(solution)/shard_map/ppermute | solution.py:28
  46.6 10.8 %collective-permute-start.11 = (bf16[8,16,1152]{2,1,0:T(8,128)(2,1)}, bf16[8,16,1152]{2,1,0:T(8,128)(2,1)S(1)}, u32[]{:S(2)}, u32[]{:S(2)}) collective-permute-start(bf16[8,16,1152]{2,1,0:T(8,128)(2,1)} %get-tuple-element.49), channel_id=1, source_target_pairs={{0,8},{8,0},{16,24},{24,16},{32,40},{40,32},{48,56},{56,48},{64,72... | collective-permute-start | bytes 884744 | tf_op jit(solution)/shard_map/ppermute | solution.py:28
  52.4 12.5 %all-to-all-start.2 = ((bf16[8,16,1152]{2,1,0:T(8,128)(2,1)}), bf16[8,16,1152]{2,1,0:T(8,128)(2,1)S(1)}, u32[]{:S(2)}, u32[]{:S(2)}) async-start(bf16[8,16,1152]{2,1,0:T(8,128)(2,1)} %get-tuple-element.44), calls=%async_computation.2 | async-start | bytes 589824 | tf_op jit(solution)/shard_map/all_to_all | solution.py:327
  56.0 26.5 %collective-permute-start.17 = (bf16[1280,128]{1,0:T(8,128)(2,1)S(1)}, bf16[1280,128]{1,0:T(8,128)(2,1)S(1)}, u32[]{:S(2)}, u32[]{:S(2)}) collective-permute-start(bf16[1280,128]{1,0:T(8,128)(2,1)S(1)} %collective-permute-done.12.refs_4_.refs_3_), channel_id=1, source_target_pairs={{0,8},{8,0},{16,24},{24,16},{32,40},{40,32},{48,56},{56,48},{64,72... | collective-permute-start | bytes 983048 | tf_op jit(solution)/shard_map/ppermute | solution.py:28
  65.7 11.2 %all-to-all-start.3 = ((bf16[8,16,1152]{2,1,0:T(8,128)(2,1)}), bf16[8,16,1152]{2,1,0:T(8,128)(2,1)S(1)}, u32[]{:S(2)}, u32[]{:S(2)}) async-start(bf16[8,16,1152]{2,1,0:T(8,128)(2,1)} %get-tuple-element.51), calls=%async_computation.3 | async-start | bytes 589824 | tf_op jit(solution)/shard_map/all_to_all | solution.py:327
  69.2 11.0 %collective-permute-start.16 = (bf16[960,128]{1,0:T(8,128)(2,1)S(1)}, bf16[960,128]{1,0:T(8,128)(2,1)S(1)}, u32[]{:S(2)}, u32[]{:S(2)}) collective-permute-start(bf16[960,128]{1,0:T(8,128)(2,1)S(1)} %copy-done.3), channel_id=1, source_target_pairs={{0,8},{8,0},{16,24},{24,16},{32,40},{40,32},{48,56},{56,48},{64,72... | collective-permute-start | bytes 737288 | tf_op jit(solution)/shard_map/ppermute | solution.py:28
  70.4 12.1 %collective-permute-start.13 = (bf16[64,1152]{1,0:T(8,128)(2,1)}, bf16[64,1152]{1,0:T(8,128)(2,1)S(1)}, u32[]{:S(2)}, u32[]{:S(2)}) collective-permute-start(bf16[64,1152]{1,0:T(8,128)(2,1)} %get-tuple-element.55), channel_id=1, source_target_pairs={{0,16},{8,24},{16,0},{24,8},{32,48},{40,56},{48,32},{56,40},{64,80... | collective-permute-start | bytes 442376 | tf_op jit(solution)/shard_map/ppermute | solution.py:28
  71.2 11.4 %collective-permute-start.14 = (bf16[64,1152]{1,0:T(8,128)(2,1)}, bf16[64,1152]{1,0:T(8,128)(2,1)}, u32[]{:S(2)}, u32[]{:S(2)}) collective-permute-start(bf16[64,1152]{1,0:T(8,128)(2,1)} %get-tuple-element.56), channel_id=1, source_target_pairs={{0,128},{8,136},{16,144},{24,152},{32,160},{40,168},{48,176},{56,1... | collective-permute-start | bytes 442376 | tf_op jit(solution)/shard_map/ppermute | solution.py:28
  71.9 10.6 %collective-permute-start.15 = (bf16[64,1152]{1,0:T(8,128)(2,1)}, bf16[64,1152]{1,0:T(8,128)(2,1)}, u32[]{:S(2)}, u32[]{:S(2)}) collective-permute-start(bf16[64,1152]{1,0:T(8,128)(2,1)} %get-tuple-element.57), channel_id=1, source_target_pairs={{0,144},{8,152},{16,128},{24,136},{32,176},{40,184},{48,160},{56,1... | collective-permute-start | bytes 442376 | tf_op jit(solution)/shard_map/ppermute | solution.py:28
  80.2 15.1 %collective-permute-start.18 = (bf16[960,128]{1,0:T(8,128)(2,1)}, bf16[960,128]{1,0:T(8,128)(2,1)S(1)}, u32[]{:S(2)}, u32[]{:S(2)}) collective-permute-start(bf16[960,128]{1,0:T(8,128)(2,1)} %get-tuple-element.60.refs_6_), channel_id=1, source_target_pairs={{0,8},{8,0},{16,24},{24,16},{32,40},{40,32},{48,56},{56,48},{64,72... | collective-permute-start | bytes 737288 | tf_op jit(solution)/shard_map/ppermute | solution.py:28
  84.7 13.7 %all-to-all-start.4 = ((bf16[8,16,1152]{2,1,0:T(8,128)(2,1)}), bf16[8,16,1152]{2,1,0:T(8,128)(2,1)S(1)}, u32[]{:S(2)}, u32[]{:S(2)}) async-start(bf16[8,16,1152]{2,1,0:T(8,128)(2,1)} %get-tuple-element.58), calls=%async_computation.4 | async-start | bytes 589824 | tf_op jit(solution)/shard_map/all_to_all | solution.py:327
  89.3 11.6 %collective-permute-start.26 = (bf16[960,128]{1,0:T(8,128)(2,1)}, bf16[960,128]{1,0:T(8,128)(2,1)S(1)}, u32[]{:S(2)}, u32[]{:S(2)}) collective-permute-start(bf16[960,128]{1,0:T(8,128)(2,1)} %get-tuple-element.63), channel_id=1, source_target_pairs={{0,128},{8,136},{16,144},{24,152},{32,160},{40,168},{48,176},{56,1... | collective-permute-start | bytes 737288 | tf_op jit(solution)/shard_map/ppermute | solution.py:28
  90.0 14.7 %collective-permute-start.27 = (bf16[960,128]{1,0:T(8,128)(2,1)}, bf16[960,128]{1,0:T(8,128)(2,1)S(1)}, u32[]{:S(2)}, u32[]{:S(2)}) collective-permute-start(bf16[960,128]{1,0:T(8,128)(2,1)} %get-tuple-element.64), channel_id=1, source_target_pairs={{0,136},{8,128},{16,152},{24,144},{32,168},{40,160},{48,184},{56,1... | collective-permute-start | bytes 737288 | tf_op jit(solution)/shard_map/ppermute | solution.py:28
  92.8 7.8 %collective-permute-start.28 = (bf16[16,1152]{1,0:T(8,128)(2,1)}, bf16[16,1152]{1,0:T(8,128)(2,1)S(1)}, u32[]{:S(2)}, u32[]{:S(2)}) collective-permute-start(bf16[16,1152]{1,0:T(8,128)(2,1)} %get-tuple-element.65), channel_id=1, source_target_pairs={{0,64},{8,72},{16,80},{24,88},{32,96},{40,104},{48,112},{56,120},{... | collective-permute-start | bytes 110600 | tf_op jit(solution)/shard_map/ppermute | solution.py:28
  107.4 26.2 %all-to-all-start.5 = ((bf16[8,40,1152]{2,1,0:T(8,128)(2,1)}), bf16[8,40,1152]{2,1,0:T(8,128)(2,1)S(1)}, u32[]{:S(2)}, u32[]{:S(2)}) async-start(bf16[8,40,1152]{2,1,0:T(8,128)(2,1)} %shard_map.121), calls=%async_computation.5 | async-start | bytes 1474560 | tf_op jit(solution)/shard_map/all_to_all | solution.py:427
  111.1 7.5 %collective-permute-start.19 = (bf16[16,1152]{1,0:T(8,128)(2,1)S(1)}, bf16[16,1152]{1,0:T(8,128)(2,1)S(1)}, u32[]{:S(2)}, u32[]{:S(2)}) collective-permute-start(bf16[16,1152]{1,0:T(8,128)(2,1)S(1)} %copy-done.4), channel_id=1, source_target_pairs={{0,1},{1,0},{2,3},{3,2},{4,5},{5,4},{6,7},{7,6},{8,9},{9,8},{10,11... | collective-permute-start | bytes 110600 | tf_op jit(solution)/shard_map/ppermute | solution.py:28
  114.7 7.5 %collective-permute-start.20 = (bf16[16,1152]{1,0:T(8,128)(2,1)S(1)}, bf16[16,1152]{1,0:T(8,128)(2,1)S(1)}, u32[]{:S(2)}, u32[]{:S(2)}) collective-permute-start(bf16[16,1152]{1,0:T(8,128)(2,1)S(1)} %copy-done.4), channel_id=1, source_target_pairs={{0,2},{1,3},{2,0},{3,1},{4,6},{5,7},{6,4},{7,5},{8,10},{9,11},{10,... | collective-permute-start | bytes 110600 | tf_op jit(solution)/shard_map/ppermute | solution.py:28
  115.9 6.5 %collective-permute-start.21 = (bf16[16,1152]{1,0:T(8,128)(2,1)S(1)}, bf16[16,1152]{1,0:T(8,128)(2,1)S(1)}, u32[]{:S(2)}, u32[]{:S(2)}) collective-permute-start(bf16[16,1152]{1,0:T(8,128)(2,1)S(1)} %copy-done.4), channel_id=1, source_target_pairs={{0,4},{1,5},{2,6},{3,7},{4,0},{5,1},{6,2},{7,3},{8,12},{9,13},{10,... | collective-permute-start | bytes 110600 | tf_op jit(solution)/shard_map/ppermute | solution.py:28
  (26 other events, 278.6 us)
